TPU v7x, 32 devices: a whole 2x2x4 slice. The times are simulated.
32 devices in a mesh: tm: 8 (over z, y), space: 4 (over x, core).
Axes of the slice: x: 2, y: 2, z: 4, core: 2. Of those that a mesh axis runs over, the one named last changes fastest.
Arguments:
- start_state: float32 [16384], P('space'), may hold values from -6 to 6
- forcing: float32 [64, 16384], P('tm', 'space'), may hold values from -6 to 6
- iterate: float32 [64, 16384], P('tm', 'space'), may hold values from -6 to 6
- blocks: float32 [256, 64, 448], P('space'), may hold values from -1 to 1, as said below
- columns: int32 [256, 7], P('space'), may hold values from 0 to 255, as said below
- kdiag: float32 [16384], P('space'), may hold values from 1.05 to 1.5
Outputs:
- updated: float32 [64, 16384], P('tm', 'space')
Inputs may be any that keep to these rules, and one draw needn't show every extreme that they name: columns[b, 0] = b; every entry lies within 4 of b. The absolute values in any row of blocks sum to at most 1.
All inputs are finite; a program needn't handle non-finite values.
Results may differ from a plain program's by a relative error of at most 0.0003.
Values sent between devices are 32-bit elements; how exact they have to be, the bound alone decides.
No kernel may reach another device: no remote copies, remote signals or barrier semaphores. Data moves between devices by JAX's collectives and lax.ppermute only.
A program may use at most 64 MiB of HBM per device.

v0:
```python
import math

import jax
import jax.numpy as jnp
from jax import lax
from jax.sharding import PartitionSpec as P

GHOST = 4
SWEEPS = 2


CORNER_WEIGHT = 0.05


def with_halo(value, sides, width):
    for axis, dim in sides:
        peers, length = (lax.axis_size(axis), value.shape[dim])
        up = [(i, (i + 1) % peers) for i in range(peers - 1)]
        down = [(j, i) for i, j in up]
        last = lax.slice_in_dim(value, length - width, length, axis=dim)
        first = lax.slice_in_dim(value, 0, width, axis=dim)
        before = lax.ppermute(last, axis, up)
        after = lax.ppermute(first, axis, down)
        value = jnp.concatenate([before, value, after], axis=dim)
    return value


def passed_along(value, axis, by):
    peers = lax.axis_size(axis)
    pairs = [(i, i + by) for i in range(peers) if 0 <= i + by < peers]
    return lax.ppermute(value, axis, pairs)


def block_product(blocks, local_cols, padded):
    block_rows = blocks.shape[0]
    block_size = blocks.shape[1]
    channels = padded.shape[0]
    tiles = padded.reshape(channels, -1, block_size)
    picked = jnp.take(tiles, local_cols, axis=1).reshape(channels, block_rows, -1)
    result = jnp.einsum("bim,cbm->cbi", blocks, picked, precision=lax.Precision.HIGHEST)
    return result.reshape(channels, block_rows * block_size)


def bit_reverse(numbers, bit_count):
    result = jnp.zeros_like(numbers)
    for bit_index in range(bit_count):
        result = result + ((numbers >> bit_index & 1) << bit_count - 1 - bit_index)
    return result


def matmul_high(matrix, field):
    return jnp.einsum("sj,jr->sr", matrix, field, precision=lax.Precision.HIGHEST)


def local(start_state, forcing, iterate, blocks, columns, kdiag):
    steps_dev = iterate.shape[0]
    block_rows = blocks.shape[0]
    block_size = blocks.shape[1]
    ghost_rows = GHOST * block_size
    devices_tm = lax.axis_size("tm")
    total_steps = steps_dev * devices_tm
    bit_count = devices_tm.bit_length() - 1
    tm_index = lax.axis_index("tm")
    space_index = lax.axis_index("space")
    local_cols = columns - (space_index * block_rows - GHOST)
    padded_iter = with_halo(iterate, (("space", 1),), ghost_rows)
    coupled = block_product(blocks, local_cols, padded_iter)
    before = passed_along(iterate[steps_dev - 1], "tm", 1)
    before = jnp.where(tm_index == 0, start_state, before)
    previous = jnp.concatenate([before[None], iterate[: steps_dev - 1]], axis=0)
    residual = forcing + previous - iterate - kdiag[None] * iterate - coupled
    global_steps = (tm_index * steps_dev + lax.iota(jnp.int32, steps_dev)).astype(jnp.float32)
    scale_up = jnp.power(jnp.float32(CORNER_WEIGHT), global_steps / total_steps)
    scaled = residual * scale_up[:, None]
    owned = bit_reverse(tm_index, bit_count)
    freqs = owned + devices_tm * lax.iota(jnp.int32, steps_dev)
    two_pi = 2.0 * math.pi
    all_steps = lax.all_to_all(scaled, "tm", split_axis=1, concat_axis=0, tiled=True)
    slots = lax.iota(jnp.int32, total_steps)
    slot_freqs = bit_reverse(slots // steps_dev, bit_count) + devices_tm * (slots % steps_dev)
    phase = slot_freqs[:, None] * slots[None, :] % total_steps
    theta = -two_pi * phase.astype(jnp.float32) / total_steps
    forward_re = matmul_high(jnp.cos(theta), all_steps)
    forward_im = matmul_high(jnp.sin(theta), all_steps)
    spectrum = lax.all_to_all(
        jnp.stack([forward_re, forward_im], axis=1), "tm", split_axis=0, concat_axis=2, tiled=True
    )
    spec_re = spectrum[:, 0]
    spec_im = spectrum[:, 1]
    root = CORNER_WEIGHT ** (1.0 / total_steps)
    freq_angle = two_pi * freqs.astype(jnp.float32) / total_steps
    lam_re = 1.0 - root * jnp.cos(freq_angle)
    lam_im = root * jnp.sin(freq_angle)
    diag_re = lam_re[:, None] + kdiag[None]
    diag_im = jnp.broadcast_to(lam_im[:, None], diag_re.shape)
    denom = diag_re * diag_re + diag_im * diag_im

    def divide(num_re, num_im):
        return (
            (num_re * diag_re + num_im * diag_im) / denom,
            (num_im * diag_re - num_re * diag_im) / denom,
        )

    sol_re, sol_im = divide(spec_re, spec_im)
    for sweep_index in range(SWEEPS):
        stacked = jnp.concatenate([sol_re, sol_im], axis=0)
        padded = with_halo(stacked, (("space", 1),), ghost_rows)
        coupled_both = block_product(blocks, local_cols, padded)
        sol_re, sol_im = divide(
            spec_re - coupled_both[:steps_dev], spec_im - coupled_both[steps_dev:]
        )
    gathered = lax.all_to_all(
        jnp.stack([sol_re, sol_im], axis=1), "tm", split_axis=2, concat_axis=0, tiled=True
    )
    slots = lax.iota(jnp.int32, total_steps)
    slot_freqs = bit_reverse(slots // steps_dev, bit_count) + devices_tm * (slots % steps_dev)
    phase = slots[:, None] * slot_freqs[None, :] % total_steps
    theta = two_pi * phase.astype(jnp.float32) / total_steps
    real_steps = (
        matmul_high(jnp.cos(theta), gathered[:, 0]) - matmul_high(jnp.sin(theta), gathered[:, 1])
    ) / total_steps
    back = lax.all_to_all(real_steps, "tm", split_axis=0, concat_axis=1, tiled=True)
    scale_down = jnp.power(jnp.float32(CORNER_WEIGHT), -global_steps / total_steps)
    return iterate + scale_down[:, None] * back


def solution(mesh):
    placed = (
        P("space"),
        P("tm", "space"),
        P("tm", "space"),
        P("space", None, None),
        P("space", None),
        P("space"),
    )
    return jax.shard_map(
        local, mesh=mesh, in_specs=placed, out_specs=P("tm", "space"), check_vma=False
    )
```

profile of v0, /device:TPU:0, one launch (start us, length us, event | category | flops | bytes accessed | tf_op | source)
XLA Modules:
  0.0 168.3 jit_solution(16154826268964823630)
XLA Ops:
  5.3 4.3 %collective-permute-start = (f32[4096]{0:T(1024)S(1)}, f32[4096]{0:T(1024)S(1)}, u32[]{:S(2)}, u32[]{:S(2)}) collective-permute-start(f32[4096]{0:T(1024)S(1)} %bitcast.95), channel_id=1, source_target_pairs={{0,4},{4,8},{8,12},{12,16},{16,20},{20,24},{24,28},{1,5},{5,9},{9,... | collective-permute-start | bytes 49160 | tf_op jit(solution)/shard_map/ppermute | solution.py:31
  17.7 9.3 %convolution_bitcast_fusion.2 = f32[8,64,64]{2,0,1:T(8,128)S(1)} fusion(f32[64,64,448]{2,1,0:T(8,128)} %param.11, f32[8,64,448]{2,1,0:T(8,128)S(1)} %broadcast_select_fusion), kind=kOutput, calls=%fused_computation.7 | convolution fusion | flops 176160768 | bytes 8388608 | tf_op jit(solution)/shard_map/bim,cbm->cbi/dot_general | solution.py:40
  28.0 4.9 %all-to-all-start = ((f32[8,8,512]{2,0,1:T(8,128)}), f32[8,8,512]{2,0,1:T(8,128)S(1)}, u32[]{:S(2)}, u32[]{:S(2)}) async-start(f32[8,8,512]{2,0,1:T(8,128)} %bitcast.5), calls=%async_computation | async-start | bytes 262144 | tf_op jit(solution)/shard_map/all_to_all | solution.py:78
  32.9 7.3 %all-to-all-done = f32[8,8,512]{2,0,1:T(8,128)S(1)} async-done(((f32[8,8,512]{2,0,1:T(8,128)}), f32[8,8,512]{2,0,1:T(8,128)S(1)}, u32[]{:S(2)}, u32[]{:S(2)}) %all-to-all-start) | async-done | bytes 131104 | tf_op jit(solution)/shard_map/all_to_all | solution.py:78
  42.1 3.4 %all-to-all-start.1 = ((f32[64,2,512]{2,1,0:T(2,128)}), f32[64,2,512]{2,1,0:T(2,128)S(1)}, u32[]{:S(2)}, u32[]{:S(2)}) async-start(f32[64,2,512]{2,1,0:T(2,128)} %copy.85), calls=%async_computation.1 | async-start | bytes 524288 | tf_op jit(solution)/shard_map/all_to_all | solution.py:85
  45.6 10.0 %all-to-all-done.1 = f32[64,2,512]{2,1,0:T(2,128)S(1)} async-done(((f32[64,2,512]{2,1,0:T(2,128)}), f32[64,2,512]{2,1,0:T(2,128)S(1)}, u32[]{:S(2)}, u32[]{:S(2)}) %all-to-all-start.1) | async-done | bytes 262176 | tf_op jit(solution)/shard_map/all_to_all | solution.py:85
  59.1 3.4 %collective-permute-done.4 = f32[16,256]{1,0:T(8,128)S(1)} collective-permute-done((f32[16,256]{1,0:T(8,128)S(1)}, f32[16,256]{1,0:T(8,128)S(1)}, u32[]{:S(2)}, u32[]{:S(2)}) %collective-permute-start.4) | collective-permute-done | bytes 16416 | tf_op jit(solution)/shard_map/ppermute | solution.py:23
  62.8 2.9 %gather_fusion.1 = f32[448,16,64]{2,1,0:T(8,128)} fusion(f32[16,72,64]{2,0,1:T(8,128)S(1)} %copy.90, s32[1024]{0:T(1024)S(1)} %pad_clamp_fusion), kind=kCustom, calls=%fused_computation.clone | custom fusion | bytes 3671808 | tf_op jit(solution)/shard_map/jit(_take)/gather | solution.py:39
  65.7 2.4 %select_bitcast_fusion.1 = f32[16,64,7,64]{3,0,2,1:T(8,128)S(1)} fusion(f32[64,7,16,64]{3,2,1,0:T(8,128)} %bitcast.82, pred[64,7]{1,0:T(8,128)(4,1)S(1)} %copy.79), kind=kLoop, calls=%fused_computation.4 | loop fusion | flops 458752 | bytes 3670464 | tf_op jit(solution)/shard_map/jit(_take)/select_n | solution.py:39
  68.1 3.7 %copy.104 = f32[16,64,7,64]{3,2,0,1:T(8,128)} copy(f32[16,64,7,64]{3,0,2,1:T(8,128)S(1)} %select_bitcast_fusion.1) | data formatting | bytes 3670016 | tf_op jit(solution)/shard_map/reshape | solution.py:39
  71.8 3.3 %reshape.293 = f32[16,64,448]{2,0,1:T(8,128)S(1)} reshape(f32[16,64,7,64]{3,2,0,1:T(8,128)} %copy.104) | data formatting | bytes 3670016 | tf_op jit(solution)/shard_map/reshape | solution.py:39
  75.1 9.0 %convolution_bitcast_fusion.1 = f32[16,64,64]{2,0,1:T(8,128)S(1)} fusion(f32[16,64,448]{2,0,1:T(8,128)S(1)} %reshape.293, f32[64,64,448]{2,1,0:T(8,128)} %param.11), kind=kOutput, calls=%fused_computation.6 | convolution fusion | flops 352321536 | bytes 9437184 | tf_op jit(solution)/shard_map/bim,cbm->cbi/dot_general | solution.py:40
  84.7 4.4 %collective-permute-start.5 = (f32[16,256]{1,0:T(8,128)S(1)}, f32[16,256]{1,0:T(8,128)S(1)}, u32[]{:S(2)}, u32[]{:S(2)}) collective-permute-start(f32[16,256]{1,0:T(8,128)S(1)} %get-tuple-element.18), channel_id=1, source_target_pairs={{0,1},{1,2},{2,3},{4,5},{5,6},{6,7},{8,9},{9,10},{10,11},{12,13},{... | collective-permute-start | bytes 49160 | tf_op jit(solution)/shard_map/ppermute | solution.py:22
  92.4 2.9 %gather_fusion.2 = f32[448,16,64]{2,1,0:T(8,128)} fusion(f32[16,72,64]{2,0,1:T(8,128)S(1)} %copy.96, s32[1024]{0:T(1024)S(1)} %pad_clamp_fusion), kind=kCustom, calls=%fused_computation.1.clone | custom fusion | bytes 3671808 | tf_op jit(solution)/shard_map/jit(_take)/gather | solution.py:39
  97.7 3.7 %copy.105 = f32[16,64,7,64]{3,2,0,1:T(8,128)} copy(f32[16,64,7,64]{3,0,2,1:T(8,128)S(1)} %select_bitcast_fusion) | data formatting | bytes 3670016 | tf_op jit(solution)/shard_map/reshape | solution.py:39
  101.5 3.3 %reshape.294 = f32[16,64,448]{2,0,1:T(8,128)S(1)} reshape(f32[16,64,7,64]{3,2,0,1:T(8,128)} %copy.105) | data formatting | bytes 3670016 | tf_op jit(solution)/shard_map/reshape | solution.py:39
  104.8 9.0 %convolution_bitcast_fusion = f32[16,64,64]{2,0,1:T(8,128)S(1)} fusion(f32[16,64,448]{2,0,1:T(8,128)S(1)} %reshape.294, f32[64,64,448]{2,1,0:T(8,128)} %param.11), kind=kOutput, calls=%fused_computation.5 | convolution fusion | flops 352321536 | bytes 9437184 | tf_op jit(solution)/shard_map/bim,cbm->cbi/dot_general | solution.py:40
  114.4 4.4 %copy.101 = f32[8,2,4096]{0,1,2:T(2,128)} copy(f32[8,2,4096]{2,0,1:T(8,128)S(1)} %pad_maximum_fusion.3) | data formatting | bytes 524288 | tf_op jit(solution)/shard_map/stack | solution.py:113
  118.7 8.3 %reshape.295 = f32[8,1,8192]{2,1,0:T(1,128)S(1)} reshape(f32[4096,2,8]{2,1,0:T(2,128)} %bitcast.83) | data formatting | bytes 524288
  127.0 12.0 %all_to_all.74 = f32[8,1,8192]{2,1,0:T(1,128)S(1)} all-to-all(f32[8,1,8192]{2,1,0:T(1,128)S(1)} %reshape.295), channel_id=1, replica_groups=mesh['tm'=8,'space'=4] {'tm'}, dimensions={0} | all-to-all | bytes 524288 | tf_op jit(solution)/shard_map/all_to_all | solution.py:112
  140.7 8.3 %reshape.296 = f32[4096,2,8]{2,1,0:T(2,128)} reshape(f32[8,8192]{1,0:T(8,128)S(1)} %reduce) | data formatting | bytes 524288
  149.1 5.1 %copy.107 = f32[8,2,8,512]{3,0,2,1:T(8,128)S(1)} copy(f32[8,2,8,512]{0,1,3,2:T(2,128)} %bitcast.84) | data formatting | bytes 524288 | tf_op jit(solution)/shard_map/all_to_all | solution.py:112
  155.6 4.5 %all-to-all-start.3 = ((f32[8,8,512]{2,1,0:T(8,128)}), f32[8,8,512]{2,1,0:T(8,128)S(1)}, u32[]{:S(2)}, u32[]{:S(2)}) async-start(f32[8,8,512]{2,1,0:T(8,128)} %fusion.1), calls=%async_computation.3 | async-start | bytes 262144 | tf_op jit(solution)/shard_map/all_to_all | solution.py:122
  160.2 7.3 %all-to-all-done.3 = f32[8,8,512]{2,1,0:T(8,128)S(1)} async-done(((f32[8,8,512]{2,1,0:T(8,128)}), f32[8,8,512]{2,1,0:T(8,128)S(1)}, u32[]{:S(2)}, u32[]{:S(2)}) %all-to-all-start.3) | async-done | bytes 131104 | tf_op jit(solution)/shard_map/all_to_all | solution.py:122
  (77 shorter events, 30.7 us)
Async XLA Ops:
  0.7 10.2 %collective-permute-start.1 = (f32[8,256]{1,0:T(8,128)S(1)}, f32[8,256]{1,0:T(8,128)S(1)}, u32[]{:S(2)}, u32[]{:S(2)}) collective-permute-start(f32[8,256]{1,0:T(8,128)S(1)} %get-tuple-element.22), channel_id=1, source_target_pairs={{0,1},{1,2},{2,3},{4,5},{5,6},{6,7},{8,9},{9,10},{10,11},{12,13},{... | collective-permute-start | bytes 24584 | tf_op jit(solution)/shard_map/ppermute | solution.py:22
  3.1 7.9 %collective-permute-start.2 = (f32[8,256]{1,0:T(8,128)S(1)}, f32[8,256]{1,0:T(8,128)S(1)}, u32[]{:S(2)}, u32[]{:S(2)}) collective-permute-start(f32[8,256]{1,0:T(8,128)S(1)} %get-tuple-element.23), channel_id=1, source_target_pairs={{1,0},{2,1},{3,2},{5,4},{6,5},{7,6},{9,8},{10,9},{11,10},{13,12},{... | collective-permute-start | bytes 24584 | tf_op jit(solution)/shard_map/ppermute | solution.py:23
  5.3 21.9 %collective-permute-start = (f32[4096]{0:T(1024)S(1)}, f32[4096]{0:T(1024)S(1)}, u32[]{:S(2)}, u32[]{:S(2)}) collective-permute-start(f32[4096]{0:T(1024)S(1)} %bitcast.95), channel_id=1, source_target_pairs={{0,4},{4,8},{8,12},{12,16},{16,20},{20,24},{24,28},{1,5},{5,9},{9,... | collective-permute-start | bytes 49160 | tf_op jit(solution)/shard_map/ppermute | solution.py:31
  17.6 9.6 %copy-start.3 = (f32[4096]{0:T(1024)S(1)}, f32[4096]{0:T(1024)}, u32[]{:S(2)}) copy-start(f32[4096]{0:T(1024)} %param.8) | copy-start | bytes 49156
  17.7 9.6 %copy-start = (f32[8,4096]{1,0:T(8,128)S(1)}, f32[8,4096]{1,0:T(8,128)}, u32[]{:S(2)}) copy-start(f32[8,4096]{1,0:T(8,128)} %param.10) | copy-start | bytes 393220
  17.7 9.6 %copy-start.1 = (f32[4096]{0:T(1024)S(1)}, f32[4096]{0:T(1024)}, u32[]{:S(2)}) copy-start(f32[4096]{0:T(1024)} %param.13) | copy-start | bytes 49156
  17.7 9.6 %copy-start.2 = (f32[8,4096]{1,0:T(8,128)S(1)}, f32[8,4096]{1,0:T(8,128)}, u32[]{:S(2)}) copy-start(f32[8,4096]{1,0:T(8,128)} %param.9) | copy-start | bytes 393220
  28.0 12.2 %all-to-all-start = ((f32[8,8,512]{2,0,1:T(8,128)}), f32[8,8,512]{2,0,1:T(8,128)S(1)}, u32[]{:S(2)}, u32[]{:S(2)}) async-start(f32[8,8,512]{2,0,1:T(8,128)} %bitcast.5), calls=%async_computation | async-start | bytes 262144 | tf_op jit(solution)/shard_map/all_to_all | solution.py:78
  42.1 13.5 %all-to-all-start.1 = ((f32[64,2,512]{2,1,0:T(2,128)}), f32[64,2,512]{2,1,0:T(2,128)S(1)}, u32[]{:S(2)}, u32[]{:S(2)}) async-start(f32[64,2,512]{2,1,0:T(2,128)} %copy.85), calls=%async_computation.1 | async-start | bytes 524288 | tf_op jit(solution)/shard_map/all_to_all | solution.py:85
  55.8 3.3 %collective-permute-start.3 = (f32[16,256]{1,0:T(8,128)S(1)}, f32[16,256]{1,0:T(8,128)S(1)}, u32[]{:S(2)}, u32[]{:S(2)}) collective-permute-start(f32[16,256]{1,0:T(8,128)S(1)} %get-tuple-element.20), channel_id=1, source_target_pairs={{0,1},{1,2},{2,3},{4,5},{5,6},{6,7},{8,9},{9,10},{10,11},{12,13},{... | collective-permute-start | bytes 49160 | tf_op jit(solution)/shard_map/ppermute | solution.py:22
  57.6 4.8 %collective-permute-start.4 = (f32[16,256]{1,0:T(8,128)S(1)}, f32[16,256]{1,0:T(8,128)S(1)}, u32[]{:S(2)}, u32[]{:S(2)}) collective-permute-start(f32[16,256]{1,0:T(8,128)S(1)} %get-tuple-element.21), channel_id=1, source_target_pairs={{1,0},{2,1},{3,2},{5,4},{6,5},{7,6},{9,8},{10,9},{11,10},{13,12},{... | collective-permute-start | bytes 49160 | tf_op jit(solution)/shard_map/ppermute | solution.py:23
  84.7 5.9 %collective-permute-start.5 = (f32[16,256]{1,0:T(8,128)S(1)}, f32[16,256]{1,0:T(8,128)S(1)}, u32[]{:S(2)}, u32[]{:S(2)}) collective-permute-start(f32[16,256]{1,0:T(8,128)S(1)} %get-tuple-element.18), channel_id=1, source_target_pairs={{0,1},{1,2},{2,3},{4,5},{5,6},{6,7},{8,9},{9,10},{10,11},{12,13},{... | collective-permute-start | bytes 49160 | tf_op jit(solution)/shard_map/ppermute | solution.py:22
  89.1 3.1 %collective-permute-start.6 = (f32[16,256]{1,0:T(8,128)S(1)}, f32[16,256]{1,0:T(8,128)S(1)}, u32[]{:S(2)}, u32[]{:S(2)}) collective-permute-start(f32[16,256]{1,0:T(8,128)S(1)} %get-tuple-element.19), channel_id=1, source_target_pairs={{1,0},{2,1},{3,2},{5,4},{6,5},{7,6},{9,8},{10,9},{11,10},{13,12},{... | collective-permute-start | bytes 49160 | tf_op jit(solution)/shard_map/ppermute | solution.py:23
  155.6 11.9 %all-to-all-start.3 = ((f32[8,8,512]{2,1,0:T(8,128)}), f32[8,8,512]{2,1,0:T(8,128)S(1)}, u32[]{:S(2)}, u32[]{:S(2)}) async-start(f32[8,8,512]{2,1,0:T(8,128)} %fusion.1), calls=%async_computation.3 | async-start | bytes 262144 | tf_op jit(solution)/shard_map/all_to_all | solution.py:122
where the time goes:
time: 169 us; the launch traced here: 168 us
  local copies, waits for them, and re-layouts  56.9 us (34%)
  starting transfers between devices  29.9 us (18%)
  matrix products  29.7 us (18%)
  waiting for transfers between devices  29.6 us (18%)
  blocking collectives  12 us (7%)
  other arithmetic  9.83 us (6%)
    dot_general x3, matrix products, block_product(): jnp.einsum('bim,cbm->cbi', blocks, picked, precision=lax.Precision.HIGHEST)  27.3 us
    unnamed x10, local copies, waits for them, and re-layouts  16.6 us
    reshape x4, local copies, waits for them, and re-layouts, block_product(): jnp.take(tiles, local_cols, axis=1).reshape(channels, block_rows, -1)  14.1 us
    all_to_all x1, blocking collectives, local(): lax.all_to_all(jnp.stack([sol_re, sol_im], axis=1), 'tm', split_axis=2, c...  12 us
    gather x5, local copies, waits for them, and re-layouts, block_product(): jnp.take(tiles, local_cols, axis=1).reshape(channels, block_rows, -1)  11.3 us
    all_to_all x1, waiting for transfers between devices, local(): lax.all_to_all(jnp.stack([forward_re, forward_im], axis=1), 'tm', split_a...  9.99 us
    ppermute x3, starting transfers between devices, with_halo(): before = lax.ppermute(last, axis, up)  8.55 us
    all_to_all x1, waiting for transfers between devices, local(): lax.all_to_all(scaled, 'tm', split_axis=1, concat_axis=0, tiled=True)  7.34 us
  transfers between devices with their start and end apart: 10, of which 5 were waited for; matrix products, arithmetic and copies ran while one was open for 11% of the time, Pallas kernels for 0%

commit v1 on v0

v1 whole, which is shorter than its diff:
```python
import functools
import math

import jax
import jax.numpy as jnp
import numpy as np
from jax import lax
from jax.experimental import pallas as pl
from jax.experimental.pallas import tpu as pltpu
from jax.sharding import PartitionSpec as P

GHOST = 4
CORNER_WEIGHT = 0.05
AXES = ("tm", "space")
F32 = jnp.float32
BF16 = jnp.bfloat16


def snake(count):
    order = []
    for pair in range(0, count - 1, 2):
        order += [pair, pair + 1] if pair % 4 == 0 else [pair + 1, pair]
    return order + ([count - 1] if count % 2 else [])


def split(value):
    high = value.astype(BF16)
    return high, (value - high.astype(F32)).astype(BF16)


def np_split(value):
    high = value.astype(np.float32).astype(BF16)
    return high, (value - high.astype(np.float64)).astype(np.float32).astype(BF16)


def tables(total, times):
    half = total // 2
    freq = np.arange(half)
    t = np.asarray(times)[:, None]
    angle = 2.0 * math.pi * ((t * freq[None]) % total) / total
    nyquist = np.where(t % 2 == 0, 1.0, -1.0)
    cos, sin = np.cos(angle), np.sin(angle)
    grow = CORNER_WEIGHT ** (t / total)
    forward = np.concatenate([cos, nyquist, -sin[:, 1:]], axis=1) * grow
    twice = np.where(freq == 0, 1.0, 2.0)[None]
    back = np.concatenate([twice * cos, nyquist, -2.0 * sin[:, 1:]], axis=1) / grow / total
    high, low = np_split(forward)
    forward = np.concatenate([high, high, low, low], axis=0)
    high, low = np_split(back)
    back = np.concatenate([high, high, low, low], axis=1)
    root = CORNER_WEIGHT ** (1.0 / total)
    theta = 2.0 * math.pi * freq / total
    lam_re = np.concatenate([1.0 - root * np.cos(theta), [1.0 + root], 1.0 - root * np.cos(theta[1:])])
    lam_im = np.concatenate([root * np.sin(theta), [0.0], -root * np.sin(theta[1:])])
    return forward, back, np.stack([lam_re, lam_im]).astype(np.float32)


def blocks_kernel(sel_ref, own_ref, halo_ref, out_ref):
    take = sel_ref[1, pl.program_id(0)]
    value = jnp.where(take == 1, halo_ref[...], own_ref[...])
    high, low = split(value)
    size = value.shape[1]
    out_ref[:, :size] = high
    out_ref[:, size:] = low


def product(a_ref, row, cols_ref, base, v_ref, size, slots, channels):
    picked = []
    for n in range(slots):
        at = pl.multiple_of((cols_ref[row, n] + base) * size, size)
        picked.append(v_ref[pl.ds(at, size), :])
    picked = jnp.concatenate(picked, axis=0)
    out = jnp.dot(a_ref[row], picked, preferred_element_type=F32)
    out = out[:size] + out[size:]
    return out[:, :channels] + out[:, channels:]


def store_split(ref, at, value):
    high, low = split(value)
    rows, channels = value.shape
    ref[at : at + rows, :channels] = high
    ref[at : at + rows, channels:] = low


def residual_kernel(
    dims, cols_ref, before_ref, a_ref, x_ref, f_ref, left_ref, right_ref, start_ref, kd_ref, out_ref, v_ref, c_ref
):
    size, slots, chunk, total, steps = dims
    rows = chunk * size
    edge = GHOST * size
    store_split(v_ref, 0, left_ref[...].T)
    store_split(v_ref, edge, x_ref[...].T)
    store_split(v_ref, edge + rows, right_ref[...].T)
    for b in range(chunk):
        c_ref[b * size : (b + 1) * size, :] = product(a_ref, b + GHOST, cols_ref, 0, v_ref, size, slots, total)
    coupled = c_ref[...].T
    keep = 1.0 + kd_ref[...]
    for at in range(0, total, steps):
        last = before_ref[at // steps]
        previous = jnp.where(last < 0, start_ref[...], x_ref[pl.ds(jnp.maximum(last, 0), 1), :])
        span = slice(at, at + steps)
        now = x_ref[span, :]
        previous = jnp.concatenate([previous, now[: steps - 1]], axis=0)
        out_ref[span, :] = f_ref[span, :] + previous - keep * now - coupled[span]


def sweeps_kernel(
    dims, cols_ref, a_ref, x_ref, r_ref, left_ref, right_ref, kd_ref, fwd_ref, back_ref, lam_ref, out_ref, s_ref, cr_ref, ci_ref, v0_ref, v1_ref, y_ref
):
    size, slots, chunk, total, _ = dims
    rows = chunk * size
    wide = 2 * GHOST * size
    half = total // 2

    def forward(value):
        high, low = split(value)
        stacked = jnp.concatenate([high, low, high, low], axis=0)
        return lax.dot_general(stacked, fwd_ref[...], (((0,), (0,)), ((), ())), preferred_element_type=F32)

    s_ref[0:wide, :] = forward(left_ref[...])
    s_ref[wide : wide + rows, :] = forward(r_ref[...])
    s_ref[wide + rows :, :] = forward(right_ref[...])
    kd = jnp.broadcast_to(kd_ref[...], (total, kd_ref.shape[1])).T
    diag = kd + lam_ref[0:1, :]
    imag = lam_ref[1:2, :]
    inverse = 1.0 / (diag * diag + imag * imag)
    cr_ref[...] = diag * inverse
    ci_ref[...] = imag * inverse

    def divide(value, at):
        swapped = jnp.concatenate([value[:, half:], value[:, :half]], axis=1)
        span = slice(at, at + value.shape[0])
        return value * cr_ref[span, :] + swapped * ci_ref[span, :]

    store_split(v0_ref, 0, divide(s_ref[...], 0))
    for b in range(chunk + 2 * GHOST):
        at = (b + GHOST) * size
        coupled = product(a_ref, b, cols_ref, GHOST, v0_ref, size, slots, total)
        store_split(v1_ref, b * size, divide(s_ref[at : at + size, :] - coupled, at))
    for b in range(chunk):
        at = (b + 2 * GHOST) * size
        coupled = product(a_ref, b + GHOST, cols_ref, 0, v1_ref, size, slots, total)
        high, low = split(divide(s_ref[at : at + size, :] - coupled, at))
        y_ref[b * size : (b + 1) * size, :] = jnp.concatenate([high, low, high, low], axis=1)
    change = lax.dot_general(back_ref[...], y_ref[...], (((1,), (1,)), ((), ())), preferred_element_type=F32)
    out_ref[...] = x_ref[...] + change


def vmem(count):
    return [pl.BlockSpec(memory_space=pltpu.VMEM)] * count


def smem(count):
    return [pl.BlockSpec(memory_space=pltpu.SMEM)] * count


PARAMS = pltpu.CompilerParams(vmem_limit_bytes=48 * 1024 * 1024)


def local(start_state, forcing, iterate, blocks, columns, kdiag):
    steps, rows_dev = iterate.shape
    block_rows, size, width = blocks.shape
    slots = width // size
    n_tm, n_space = lax.axis_size("tm"), lax.axis_size("space")
    total = steps * n_tm
    chunk = block_rows // n_tm
    rows = chunk * size
    edge = GHOST * size
    wide = 2 * edge
    dims = (size, slots, chunk, total, steps)
    order = snake(n_tm)
    place = [order.index(t) for t in range(n_tm)]

    tm_index, space_index = lax.axis_index("tm"), lax.axis_index("space")
    flipped = space_index % 2 == 1
    spot = jnp.asarray(place, jnp.int32)[tm_index]
    spot = jnp.where(flipped, n_tm - 1 - spot, spot)
    even = (space_index * n_tm + spot) % 2 == 0

    groups, ring = [], []
    for s in range(n_space):
        members = [t * n_space + s for t in (order if s % 2 == 0 else order[::-1])]
        groups.append(tuple(members))
        ring += members
    groups = tuple(groups)
    count = len(ring)

    def deal(value):
        return lax.all_to_all(value, AXES, 0, 0, axis_index_groups=groups, tiled=True)

    def ring_pairs(first):
        pairs = []
        for i in range(first, count - 1, 2):
            pairs += [(ring[i], ring[i + 1]), (ring[i + 1], ring[i])]
        return pairs

    def turned(value, crossed):
        other = value.reshape(n_tm, steps, -1)[::-1].reshape(value.shape)
        return jnp.where(crossed, other, value)

    def neighbours(value, extent):
        if extent <= rows:
            low, high = value[:, :extent], value[:, rows - extent :]
            from_a = lax.ppermute(jnp.where(even, high, low), AXES, ring_pairs(0))
            from_b = lax.ppermute(jnp.where(even, low, high), AXES, ring_pairs(1))
            left, right = jnp.where(even, from_b, from_a), jnp.where(even, from_a, from_b)
            return turned(left, spot == 0), turned(right, spot == n_tm - 1)
        left, right = [], []
        for hop in range(1, extent // rows + 1):
            up = [(ring[i], ring[i + hop]) for i in range(count - hop)]
            left.insert(0, turned(lax.ppermute(value, AXES, up), spot < hop))
            right.append(turned(lax.ppermute(value, AXES, [(j, i) for i, j in up]), spot >= n_tm - hop))
        return jnp.concatenate(left, axis=1), jnp.concatenate(right, axis=1)

    both = jnp.stack([v.reshape(steps, n_tm, rows).transpose(1, 0, 2) for v in (iterate, forcing)], axis=1)
    dealt = deal(both)
    x = dealt[:, 0].reshape(total, rows)
    f = dealt[:, 1].reshape(total, rows)
    times = [[t * steps + j for t in members for j in range(steps)] for members in (order, order[::-1])]
    made = [tables(total, at) for at in times]
    fwd = jnp.where(flipped, made[1][0], made[0][0])
    back = jnp.where(flipped, made[1][1], made[0][1])
    lam = jnp.asarray(made[0][2])
    lasts = [[at.index(at[j] - 1) if at[j] else -1 for j in range(0, total, steps)] for at in times]
    lasts = jnp.where(flipped, jnp.asarray(lasts[1], jnp.int32), jnp.asarray(lasts[0], jnp.int32))

    def packed(at_blocks, at_columns, at_kdiag):
        return jnp.concatenate(
            [at_blocks.reshape(edge, width), jnp.pad(at_columns.astype(F32).reshape(1, -1), ((0, 0), (0, width - GHOST * slots)))]
            + [jnp.pad(at_kdiag.reshape(2, edge), ((0, 0), (0, width - edge)))], axis=0
        )

    low = packed(blocks[:GHOST], columns[:GHOST], kdiag[:wide])
    high = packed(blocks[-GHOST:], columns[-GHOST:], kdiag[-wide:])
    if chunk >= 2 * GHOST and n_tm > 1:
        pairs = []
        for s in range(n_space - 1):
            i, j = ring[(s + 1) * n_tm - 1], ring[(s + 1) * n_tm]
            pairs += [(i, j), (j, i)]
        before = after = lax.ppermute(jnp.where(spot == 0, low, high), AXES, pairs)
    else:
        up = [(s, s + 1) for s in range(n_space - 1)]
        before = lax.ppermute(high, "space", up)
        after = lax.ppermute(low, "space", [(j, i) for i, j in up])

    def unpacked(value):
        return (
            value[:edge].reshape(GHOST, size, width),
            value[edge, : GHOST * slots].reshape(GHOST, slots).astype(jnp.int32),
            value[edge + 1 :, :edge].reshape(-1),
        )

    blocks_before, columns_before, kdiag_before = unpacked(before)
    blocks_after, columns_after, kdiag_after = unpacked(after)
    origin = spot * chunk
    columns_all = jnp.concatenate([columns_before, columns, columns_after], axis=0)
    cols = lax.dynamic_slice_in_dim(columns_all, origin, chunk + 2 * GHOST, 0)
    cols = jnp.clip(cols - (space_index * block_rows + origin - GHOST), -GHOST, chunk + 3 * GHOST - 1)
    kdiag_all = jnp.concatenate([kdiag_before, kdiag, kdiag_after])
    kd = lax.dynamic_slice_in_dim(kdiag_all, origin * size, rows + 2 * wide, 0)[None]
    kd_own = lax.dynamic_slice_in_dim(kdiag, origin * size, rows, 0)[None]
    start = lax.dynamic_slice_in_dim(start_state, origin * size, rows, 0)[None]

    unit = math.gcd(chunk, GHOST)
    pieces = (chunk + 2 * GHOST) // unit
    at = (origin - GHOST) // unit + jnp.arange(pieces)
    own_units, halo_units = block_rows // unit, GHOST // unit
    outside = (at < 0) | (at >= own_units)
    halo_at = jnp.where(at < 0, at + halo_units, at - own_units + halo_units)
    if before is after:
        halo = blocks_before
        halo_at = jnp.where(at < 0, halo_at, halo_at - halo_units)
        halo_last = halo_units - 1
    else:
        halo = jnp.concatenate([blocks_before, blocks_after], axis=0)
        halo_last = 2 * halo_units - 1
    sel = jnp.stack([jnp.clip(at, 0, own_units - 1), outside, jnp.clip(halo_at, 0, halo_last)]).astype(jnp.int32)
    a = pl.pallas_call(
        blocks_kernel,
        grid_spec=pltpu.PrefetchScalarGridSpec(
            num_scalar_prefetch=1,
            grid=(pieces,),
            in_specs=[
                pl.BlockSpec((unit, size, width), lambda i, sel: (sel[0, i], 0, 0)),
                pl.BlockSpec((unit, size, width), lambda i, sel: (sel[2, i], 0, 0)),
            ],
            out_specs=pl.BlockSpec((unit, 2 * size, width), lambda i, sel: (i, 0, 0)),
        ),
        out_shape=jax.ShapeDtypeStruct((chunk + 2 * GHOST, 2 * size, width), BF16),
        compiler_params=PARAMS,
        name="split_blocks",
    )(sel, blocks, halo)

    x_left, x_right = neighbours(x, edge)
    residual = pl.pallas_call(
        functools.partial(residual_kernel, dims),
        in_specs=smem(2) + vmem(7),
        out_specs=vmem(1)[0],
        out_shape=jax.ShapeDtypeStruct((total, rows), F32),
        scratch_shapes=[pltpu.VMEM((rows + 2 * edge, 2 * total), BF16), pltpu.VMEM((rows, total), F32)],
        compiler_params=PARAMS,
        name="residual",
    )(cols, lasts, a, x, f, x_left, x_right, start, kd_own)

    left, right = neighbours(residual, wide)
    span = rows + 2 * wide
    result = pl.pallas_call(
        functools.partial(sweeps_kernel, dims),
        in_specs=smem(1) + vmem(9),
        out_specs=vmem(1)[0],
        out_shape=jax.ShapeDtypeStruct((total, rows), F32),
        scratch_shapes=[pltpu.VMEM((span, total), F32)] * 3
        + [
            pltpu.VMEM((span, 2 * total), BF16),
            pltpu.VMEM((span - wide, 2 * total), BF16),
            pltpu.VMEM((rows, 4 * total), BF16),
        ],
        compiler_params=PARAMS,
        name="sweeps",
    )(cols, a, x, residual, left, right, kd, fwd, back, lam)

    returned = deal(result.reshape(n_tm, steps, rows))
    return returned.transpose(1, 0, 2).reshape(steps, rows_dev)


def solution(mesh):
    placed = (
        P("space"),
        P("tm", "space"),
        P("tm", "space"),
        P("space", None, None),
        P("space", None),
        P("space"),
    )
    return jax.shard_map(local, mesh=mesh, in_specs=placed, out_specs=P("tm", "space"), check_vma=False)
```

time: 169 us -> 54.5 us (0.32)
  local copies, waits for them, and re-layouts: 56.9 us -> 6.09 us
  matrix products: 29.7 us -> 0 us
  waiting for transfers between devices: 29.6 us -> 3.05 us
  starting transfers between devices: 29.9 us -> 14.7 us
  Pallas kernels: 0 us -> 8.26 us
  other arithmetic: 9.83 us -> 5.18 us
  blocking collectives: 12 us -> 15 us
    dot_general x7 -> x0, matrix products: 29.7 us -> none  [the longest x3 27.3 us: block_product(): jnp.einsum('bim,cbm->cbi', blocks, picked, precision=lax.Precision.HIGHEST)]
    all_to_all x3 -> x1, waiting for transfers between devices: 24.7 us -> 0.01 us  [deal(): lax.all_to_all(value, AXES, 0, 0, axis_index_groups=groups, tiled=True)]
    unnamed x10 -> x8, local copies, waits for them, and re-layouts: 16.6 us -> 1.45 us
    reshape x11 -> x2, local copies, waits for them, and re-layouts: 14.9 us -> 0.17 us  [packed(): at_columns.astype(F32).reshape(1, -1)]
    gather x5 -> x0, local copies, waits for them, and re-layouts: 11.3 us -> none  [block_product(): jnp.take(tiles, local_cols, axis=1).reshape(channels, block_rows, -1)]
    ppermute x7 -> x5, starting transfers between devices: 17.1 us -> 7.39 us  [the longest x2 5.39 us: neighbours(): from_a = lax.ppermute(jnp.where(even, high, low), AXES, ring_pairs(0))]
    pallas_call x0 -> x3, Pallas kernels: none -> 8.26 us  [the longest x1 3.52 us: local(): pl.pallas_call(functools.partial(sweeps_kernel, dims), in_specs=smem(1) +...]
    all_to_all x3 -> x0, local copies, waits for them, and re-layouts: 5.68 us -> none  [the longest x2 5.63 us: local(): lax.all_to_all(jnp.stack([sol_re, sol_im], axis=1), 'tm', split_axis=2, c...]
  transfers between devices with their start and end apart: 10 -> 6, of which waited for: 5 -> 1; matrix products, arithmetic and copies ran while one was open for 11% -> 16% of each run, Pallas kernels for 0% -> 6%
where the time goes in v1:
time: 54.5 us; the launch traced here: 53.8 us
  blocking collectives  15 us (28%)
  starting transfers between devices  14.7 us (27%)
  Pallas kernels  8.26 us (15%)
  local copies, waits for them, and re-layouts  6.09 us (11%)
  other arithmetic  5.18 us (10%)
  waiting for transfers between devices  3.05 us (6%)
  between operations  1.57 us (3%)
    all_to_all x1, blocking collectives, deal(): lax.all_to_all(value, AXES, 0, 0, axis_index_groups=groups, tiled=True)  15 us
    all_to_all x1, starting transfers between devices, deal(): lax.all_to_all(value, AXES, 0, 0, axis_index_groups=groups, tiled=True)  7.28 us
    ppermute x2, starting transfers between devices, neighbours(): from_a = lax.ppermute(jnp.where(even, high, low), AXES, ring_pairs(0))  5.39 us
    pallas_call x1, Pallas kernels, local(): pl.pallas_call(functools.partial(sweeps_kernel, dims), in_specs=smem(1) +...  3.52 us
    pallas_call x1, Pallas kernels, local(): pl.pallas_call(blocks_kernel, grid_spec=pltpu.PrefetchScalarGridSpec(num_...  3.09 us
    ppermute x2, waiting for transfers between devices, neighbours(): from_a = lax.ppermute(jnp.where(even, high, low), AXES, ring_pairs(0))  3.04 us
    another operation x1, other arithmetic, local(): jnp.stack([v.reshape(steps, n_tm, rows).transpose(1, 0, 2) for v in (iter...  1.68 us
    pallas_call x1, Pallas kernels, local(): pl.pallas_call(functools.partial(residual_kernel, dims), in_specs=smem(2)...  1.64 us
  transfers between devices with their start and end apart: 6, of which 1 were waited for; matrix products, arithmetic and copies ran while one was open for 16% of the time, Pallas kernels for 6%

profile of v1, /device:TPU:0, one launch (start us, length us, event | category | flops | bytes accessed | tf_op | source)
XLA Modules:
  0.0 53.8 jit_solution(17619687973309837167)
XLA Ops:
  0.0 1.7 %pad_maximum_fusion = f32[8,2,8,512]{3,2,1,0:T(8,128)} fusion(f32[8,1,8,512]{3,2,1,0:T(8,128)} %bitcast.50, f32[8,1,8,512]{3,2,1,0:T(8,128)} %bitcast.51), kind=kLoop, calls=%fused_computation.9 | loop fusion | flops 65536 | bytes 524288 | tf_op jit(solution)/shard_map/stack | solution.py:215
  1.7 7.3 %all-to-all-start = ((f32[8,2,8,512]{3,2,1,0:T(8,128)}), f32[8,2,8,512]{3,2,1,0:T(8,128)S(1)}, u32[]{:S(2)}, u32[]{:S(2)}) async-start(f32[8,2,8,512]{3,2,1,0:T(8,128)} %pad_maximum_fusion), calls=%async_computation | async-start | bytes 524288 | tf_op jit(solution)/shard_map/all_to_all | solution.py:189
  9.0 1.2 %dynamic_slice.15 = s32[1]{0:T(128)} dynamic-slice(s32[8]{0:T(128)} %constant.89.clone, s32[]{:T(128)S(6)} %select_n.145), dynamic_slice_sizes={1} | dynamic-slice | bytes 12 | tf_op jit(solution)/shard_map/dynamic_slice | solution.py:176
  11.5 0.8 %fusion.15 = (f32[512]{0:T(512)S(1)}, f32[512]{0:T(512)S(1)}, f32[512]{0:T(512)S(1)}) fusion(f32[4096]{0:T(1024)} %param.19, s32[]{:T(128)S(6)} %select_n.165), kind=kLoop, calls=%fused_computation.53 | loop fusion | bytes 12292 | tf_op jit(solution)/shard_map/dynamic_slice | solution.py:261
  12.4 0.8 %slice_convert_fusion.1 = (f32[4,7]{0,1:T(8,128)S(1)}, f32[4,7]{0,1:T(8,128)S(1)}) fusion(s32[64,7]{0,1:T(8,128)} %param.18), kind=kLoop, calls=%fused_computation.41 | loop fusion | flops 56 | bytes 448 | tf_op jit(solution)/shard_map/convert_element_type | solution.py:229
  13.2 0.1 copy.23
  13.4 0.1 copy.24
  13.6 1.3 %fusion.14 = (f32[4,64,448]{2,1,0:T(8,128)S(1)}, f32[4,64,448]{2,1,0:T(8,128)S(1)}) fusion(f32[64,64,448]{2,1,0:T(8,128)} %own_ref.1), kind=kLoop, calls=%fused_computation.52 | loop fusion | bytes 1835008 | tf_op jit(solution)/shard_map/slice | solution.py:234
  15.0 0.7 %collective-permute-start = (f32[259,448]{1,0:T(8,128)S(1)}, f32[259,448]{1,0:T(8,128)S(1)}, u32[]{:S(2)}, u32[]{:S(2)}) collective-permute-start(f32[259,448]{1,0:T(8,128)S(1)} %fusion), channel_id=1, source_target_pairs={{24,25},{25,24},{1,2},{2,1},{26,27},{27,26}} | collective-permute-start | bytes 1392392 | tf_op jit(solution)/shard_map/ppermute | solution.py:240
  15.7 0.7 %broadcast_select_fusion.6.before_ref = s32[8]{0:T(128)S(1)} fusion(s32[8]{0:T(128)} %constant.95.clone, s32[8]{0:T(128)} %constant.96.clone, pred[]{:T(512)S(6)} %eq.18), kind=kLoop, calls=%fused_computation.45 | loop fusion | flops 8 | bytes 97 | tf_op jit(solution)/shard_map/jit(_where)/select_n | solution.py:225
  16.4 0.8 %broadcast_select_fusion.3.back_ref = bf16[64,256]{1,0:T(8,128)(2,1)S(1)} fusion(bf16[64,256]{1,0:T(8,128)(2,1)} %constant.92.clone, bf16[64,256]{1,0:T(8,128)(2,1)} %constant.93.clone, pred[]{:T(512)S(6)} %eq.18), kind=kLoop, calls=%fused_computation.26 | loop fusion | flops 16384 | bytes 98305 | tf_op jit(solution)/shard_map/jit(_where)/select_n | solution.py:222
  17.2 0.9 %broadcast_select_fusion.fwd_ref = bf16[256,64]{1,0:T(8,128)(2,1)S(1)} fusion(bf16[256,64]{1,0:T(8,128)(2,1)} %constant.90.clone, bf16[256,64]{1,0:T(8,128)(2,1)} %constant.91.clone, pred[]{:T(512)S(6)} %eq.18), kind=kLoop, calls=%fused_computation.16 | loop fusion | flops 16384 | bytes 98305 | tf_op jit(solution)/shard_map/jit(_where)/select_n | solution.py:221
  18.1 0.8 %copy.25 = s32[64,7]{1,0:T(8,128)S(1)} copy(s32[64,7]{0,1:T(8,128)} %param.18) | data formatting | bytes 3584 | tf_op args[4]
  18.8 0.8 %dynamic_slice.17 = f32[512]{0:T(512)S(1)} dynamic-slice(f32[4096]{0:T(1024)} %param.14, s32[]{:T(128)S(6)} %select_n.165), dynamic_slice_sizes={512} | dynamic-slice | bytes 4100 | tf_op jit(solution)/shard_map/dynamic_slice | solution.py:262
  19.6 2.1 %collective-permute-start.2 = (f32[64,256]{1,0:T(8,128)S(1)}, f32[64,256]{1,0:T(8,128)S(1)}, u32[]{:S(2)}, u32[]{:S(2)}) collective-permute-start(f32[64,256]{1,0:T(8,128)S(1)} %get-tuple-element.17), channel_id=1, source_target_pairs={{0,4},{4,0},{12,8},{8,12},{16,20},{20,16},{28,24},{24,28},{25,29},... | collective-permute-start | bytes 196616 | tf_op jit(solution)/shard_map/ppermute | solution.py:204
  21.7 0.7 %collective-permute-start.1 = (f32[64,256]{1,0:T(8,128)S(1)}, f32[64,256]{1,0:T(8,128)S(1)}, u32[]{:S(2)}, u32[]{:S(2)}) collective-permute-start(f32[64,256]{1,0:T(8,128)S(1)} %get-tuple-element.18), channel_id=1, source_target_pairs={{4,12},{12,4},{8,16},{16,8},{20,28},{28,20},{24,25},{25,24},{29,21... | collective-permute-start | bytes 196616 | tf_op jit(solution)/shard_map/ppermute | solution.py:205
  22.6 3.1 %split_blocks.1.a_ref = bf16[16,128,448]{2,1,0:T(8,128)(2,1)S(1)} custom-call(s32[3,4]{1,0:T(4,128)S(1)} %pad_add_fusion.sel_ref, f32[64,64,448]{2,1,0:T(8,128)} %own_ref.1, f32[4,64,448]{2,1,0:T(8,128)S(1)} %bitcast.43), custom_call_target="tpu_custom_call" | custom-call | tf_op jit(solution)/shard_map/split_blocks/pallas_call | solution.py:278
  25.8 1.6 %residual.1.r_ref = f32[64,512]{1,0:T(8,128)S(1)} custom-call(s32[16,7]{1,0:T(8,128)S(1)} %fusion.11.cols_ref, s32[8]{0:T(128)S(1)} %broadcast_select_fusion.6.before_ref, bf16[16,128,448]{2,1,0:T(8,128)(2,1)S(1)} %split_blocks.1.a_ref, f32[64,512]{1,0:T(8,128)S(1)} %get-tuple-element.12.x_ref, f32[64,512]{1,0:T(8,128)S(1)} %get-tuple-element.11.f_ref, ...), custom_call_target="tpu_custom_call" | custom-call | tf_op jit(solution)/shard_map/residual/pallas_call | solution.py:295
  27.4 3.3 %collective-permute-start.4 = (f32[64,512]{1,0:T(8,128)S(1)}, f32[64,512]{1,0:T(8,128)S(1)}, u32[]{:S(2)}, u32[]{:S(2)}) collective-permute-start(f32[64,512]{1,0:T(8,128)S(1)} %residual.1.r_ref), channel_id=1, source_target_pairs={{0,4},{4,0},{12,8},{8,12},{16,20},{20,16},{28,24},{24,28},{25,29},... | collective-permute-start | bytes 393224 | tf_op jit(solution)/shard_map/ppermute | solution.py:204
  30.7 0.7 %collective-permute-start.3 = (f32[64,512]{1,0:T(8,128)S(1)}, f32[64,512]{1,0:T(8,128)S(1)}, u32[]{:S(2)}, u32[]{:S(2)}) collective-permute-start(f32[64,512]{1,0:T(8,128)S(1)} %residual.1.r_ref), channel_id=1, source_target_pairs={{4,12},{12,4},{8,16},{16,8},{20,28},{28,20},{24,25},{25,24},{29,21... | collective-permute-start | bytes 393224 | tf_op jit(solution)/shard_map/ppermute | solution.py:205
  31.5 3.0 %collective-permute-done.4 = f32[64,512]{1,0:T(8,128)S(1)} collective-permute-done((f32[64,512]{1,0:T(8,128)S(1)}, f32[64,512]{1,0:T(8,128)S(1)}, u32[]{:S(2)}, u32[]{:S(2)}) %collective-permute-start.4) | collective-permute-done | bytes 131104 | tf_op jit(solution)/shard_map/ppermute | solution.py:204
  34.6 3.5 %sweeps.1 = f32[64,512]{1,0:T(8,128)S(1)} custom-call(s32[16,7]{1,0:T(8,128)S(1)} %fusion.11.cols_ref, bf16[16,128,448]{2,1,0:T(8,128)(2,1)S(1)} %split_blocks.1.a_ref, f32[64,512]{1,0:T(8,128)S(1)} %get-tuple-element.12.x_ref, f32[64,512]{1,0:T(8,128)S(1)} %residual.1.r_ref, f32[64,512]{1,0:T(8,128)S(1)} %get-tuple-element.8.left_ref, ...), custom_call_target="tpu_custom_call" | custom-call | tf_op jit(solution)/shard_map/sweeps/pallas_call | solution.py:307
  38.2 15.0 %all_to_all.10 = f32[8,8,512]{2,1,0:T(8,128)S(1)} all-to-all(f32[8,8,512]{2,1,0:T(8,128)S(1)} %bitcast.44), channel_id=1, replica_groups={{0,4,12,8,16,20,28,24},{25,29,21,17,9,13,5,1},{2,6,14,10,18,22,30,26},{..., dimensions={0} | all-to-all | bytes 262144 | tf_op jit(solution)/shard_map/all_to_all | solution.py:189
  53.1 0.7 %copy.28 = f32[8,4096]{1,0:T(8,128)} copy(f32[8,4096]{1,0:T(8,128)S(1)} %bitcast.49) | data formatting | bytes 262144
  (31 shorter events, 0.7 us)
Async XLA Ops:
  1.7 17.9 %all-to-all-start = ((f32[8,2,8,512]{3,2,1,0:T(8,128)}), f32[8,2,8,512]{3,2,1,0:T(8,128)S(1)}, u32[]{:S(2)}, u32[]{:S(2)}) async-start(f32[8,2,8,512]{3,2,1,0:T(8,128)} %pad_maximum_fusion), calls=%async_computation | async-start | bytes 524288 | tf_op jit(solution)/shard_map/all_to_all | solution.py:189
  14.9 16.5 %copy-start.1 = (f32[4096]{0:T(1024)S(1)}, f32[4096]{0:T(1024)}, u32[]{:S(2)}) copy-start(f32[4096]{0:T(1024)} %param.19) | copy-start | bytes 49156
  15.0 7.4 %collective-permute-start = (f32[259,448]{1,0:T(8,128)S(1)}, f32[259,448]{1,0:T(8,128)S(1)}, u32[]{:S(2)}, u32[]{:S(2)}) collective-permute-start(f32[259,448]{1,0:T(8,128)S(1)} %fusion), channel_id=1, source_target_pairs={{24,25},{25,24},{1,2},{2,1},{26,27},{27,26}} | collective-permute-start | bytes 1392392 | tf_op jit(solution)/shard_map/ppermute | solution.py:240
  19.6 6.0 %collective-permute-start.2 = (f32[64,256]{1,0:T(8,128)S(1)}, f32[64,256]{1,0:T(8,128)S(1)}, u32[]{:S(2)}, u32[]{:S(2)}) collective-permute-start(f32[64,256]{1,0:T(8,128)S(1)} %get-tuple-element.17), channel_id=1, source_target_pairs={{0,4},{4,0},{12,8},{8,12},{16,20},{20,16},{28,24},{24,28},{25,29},... | collective-permute-start | bytes 196616 | tf_op jit(solution)/shard_map/ppermute | solution.py:204
  21.7 4.0 %collective-permute-start.1 = (f32[64,256]{1,0:T(8,128)S(1)}, f32[64,256]{1,0:T(8,128)S(1)}, u32[]{:S(2)}, u32[]{:S(2)}) collective-permute-start(f32[64,256]{1,0:T(8,128)S(1)} %get-tuple-element.18), channel_id=1, source_target_pairs={{4,12},{12,4},{8,16},{16,8},{20,28},{28,20},{24,25},{25,24},{29,21... | collective-permute-start | bytes 196616 | tf_op jit(solution)/shard_map/ppermute | solution.py:205
  22.5 12.1 %copy-start = (f32[2,64]{1,0:T(2,128)S(1)}, f32[2,64]{1,0:T(2,128)}, u32[]{:S(2)}) copy-start(f32[2,64]{1,0:T(2,128)} %constant.94.clone.lam_ref) | copy-start | bytes 1540
  27.4 7.1 %collective-permute-start.4 = (f32[64,512]{1,0:T(8,128)S(1)}, f32[64,512]{1,0:T(8,128)S(1)}, u32[]{:S(2)}, u32[]{:S(2)}) collective-permute-start(f32[64,512]{1,0:T(8,128)S(1)} %residual.1.r_ref), channel_id=1, source_target_pairs={{0,4},{4,0},{12,8},{8,12},{16,20},{20,16},{28,24},{24,28},{25,29},... | collective-permute-start | bytes 393224 | tf_op jit(solution)/shard_map/ppermute | solution.py:204
  30.7 3.8 %collective-permute-start.3 = (f32[64,512]{1,0:T(8,128)S(1)}, f32[64,512]{1,0:T(8,128)S(1)}, u32[]{:S(2)}, u32[]{:S(2)}) collective-permute-start(f32[64,512]{1,0:T(8,128)S(1)} %residual.1.r_ref), channel_id=1, source_target_pairs={{4,12},{12,4},{8,16},{16,8},{20,28},{28,20},{24,25},{25,24},{29,21... | collective-permute-start | bytes 393224 | tf_op jit(solution)/shard_map/ppermute | solution.py:205

commit v2 on v1

v2 whole, which is shorter than its diff:
```python
import functools
import math

import jax
import jax.numpy as jnp
import numpy as np
from jax import lax
from jax.experimental import pallas as pl
from jax.experimental.pallas import tpu as pltpu
from jax.sharding import PartitionSpec as P

GHOST = 4
CORNER_WEIGHT = 0.05
AXES = ("tm", "space")
F32 = jnp.float32
BF16 = jnp.bfloat16


def there_and_back(count):
    return list(range(0, count, 2)) + list(range(count - 1 - count % 2, 0, -2))


def split(value):
    high = value.astype(BF16)
    return high, (value - high.astype(F32)).astype(BF16)


def np_split(value):
    high = value.astype(np.float32).astype(BF16)
    return high, (value - high.astype(np.float64)).astype(np.float32).astype(BF16)


def tables(total, times):
    half = total // 2
    freq = np.arange(half)
    t = np.asarray(times)[:, None]
    angle = 2.0 * math.pi * ((t * freq[None]) % total) / total
    nyquist = np.where(t % 2 == 0, 1.0, -1.0)
    cos, sin = np.cos(angle), np.sin(angle)
    grow = CORNER_WEIGHT ** (t / total)
    forward = np.concatenate([cos, nyquist, -sin[:, 1:]], axis=1) * grow
    twice = np.where(freq == 0, 1.0, 2.0)[None]
    back = np.concatenate([twice * cos, nyquist, -2.0 * sin[:, 1:]], axis=1) / grow / total
    high, low = np_split(forward)
    forward = np.concatenate([high, high, low, low], axis=0)
    high, low = np_split(back)
    back = np.concatenate([high, high, low, low], axis=1)
    root = CORNER_WEIGHT ** (1.0 / total)
    theta = 2.0 * math.pi * freq / total
    lam_re = np.concatenate([1.0 - root * np.cos(theta), [1.0 + root], 1.0 - root * np.cos(theta[1:])])
    lam_im = np.concatenate([root * np.sin(theta), [0.0], -root * np.sin(theta[1:])])
    return forward, back, np.stack([lam_re, lam_im]).astype(np.float32)


def deal_kernel(x_ref, f_ref, out_ref):
    peers, _, _, rows = out_ref.shape
    for p in range(peers):
        out_ref[p, 0] = x_ref[:, p * rows : (p + 1) * rows]
        out_ref[p, 1] = f_ref[:, p * rows : (p + 1) * rows]


def blocks_kernel(where_ref, cols_ref, blocks_ref, own_ref, near_ref, *rest):
    *edge_ref, buffer, sems = rest
    count, size, width = buffer.shape
    chunk = count - 2 * GHOST
    slots = width // size
    block_rows = blocks_ref.shape[0]
    spot = where_ref[0]
    rows = list(range(GHOST, GHOST + chunk)) + list(range(GHOST)) + list(range(GHOST + chunk, count))
    copies = {}
    for b in rows:
        row = jnp.clip(spot * chunk + b - GHOST, 0, block_rows - 1)
        copies[b] = pltpu.make_async_copy(blocks_ref.at[row], buffer.at[b], sems.at[b])
        copies[b].start()
    for b in rows:
        copies[b].wait()
        high, low = split(buffer[b])
        if GHOST <= b < GHOST + chunk:
            ref, at = own_ref, b - GHOST
        else:
            ref, at = near_ref, b if b < GHOST else b - chunk
        ref[at, :size] = high
        ref[at, size:] = low
    if edge_ref:
        ref = edge_ref[0]
        lane = lax.broadcasted_iota(jnp.int32, (8, width), 1)
        found = jnp.zeros((8, width), jnp.int32)
        for b in range(GHOST):
            inner = jnp.where(spot == 0, buffer[GHOST + b], buffer[chunk + b])
            ref[b * size : (b + 1) * size, :] = inner
            row = jnp.where(spot == 0, b, block_rows - GHOST + b)
            for n in range(slots):
                found = jnp.where(lane == n * GHOST + b, cols_ref[n, row], found)
        ref[GHOST * size :, :] = found.astype(F32)


def patch_kernel(where_ref, old_ref, halo_ref, out_ref):
    size = out_ref.shape[1] // 2
    spot, first, last = where_ref[0], where_ref[3], where_ref[4]

    def put(at, row):
        high, low = split(halo_ref[row * size : (row + 1) * size, :])
        out_ref[at, :size] = high
        out_ref[at, size:] = low

    @pl.when(spot == first)
    def _():
        for b in range(GHOST):
            put(b, b)

    @pl.when(spot == last)
    def _():
        for b in range(GHOST):
            put(GHOST + b, b)


def near_blocks_kernel(sel_ref, own_ref, halo_ref, out_ref):
    take = sel_ref[1, pl.program_id(0)]
    value = jnp.where(take == 1, halo_ref[...], own_ref[...])
    high, low = split(value)
    size = value.shape[1]
    out_ref[:, :size] = high
    out_ref[:, size:] = low


def product(a, at, v_ref, size):
    picked = jnp.concatenate([v_ref[pl.ds(pl.multiple_of(row, size), size), :] for row in at], axis=0)
    out = jnp.dot(a, picked, preferred_element_type=F32)
    out = out[:size] + out[size:]
    channels = out.shape[1] // 2
    return out[:, :channels] + out[:, channels:]


def store_split(ref, at, value):
    high, low = split(value)
    rows, channels = value.shape
    ref[at : at + rows, :channels] = high
    ref[at : at + rows, channels:] = low


def halo(ref, extent, spot, after, dims):
    size, slots, chunk, total, steps = dims
    count = total // steps
    width = min(extent, chunk * size)
    pieces = extent // width
    parts = []
    for p in range(pieces):
        crossed = spot >= count - 1 - p if after else spot < pieces - p
        lanes = slice(p * width, (p + 1) * width)
        rows = []
        for j in range(count):
            at = pl.multiple_of(jnp.where(crossed, count - 1 - j, j) * steps, steps)
            rows.append(ref[pl.ds(at, steps), lanes])
        parts.append(jnp.concatenate(rows, axis=0))
    return parts[0] if pieces == 1 else jnp.concatenate(parts, axis=1)


def row_of(ref, spot, rows):
    tall = rows // 128
    part = ref[pl.ds(spot * tall, tall), :]
    return jnp.concatenate([part[i : i + 1] for i in range(tall)], axis=1)


def residual_kernel(
    dims, lasts, where_ref, cols_ref, a_ref, x_ref, f_ref, left_ref, right_ref, start_ref, kd_ref, out_ref, v_ref, c_ref
):
    size, slots, chunk, total, steps = dims
    rows = chunk * size
    edge = GHOST * size
    spot, flip, base = where_ref[0], where_ref[1], where_ref[2]
    store_split(v_ref, 0, halo(left_ref, edge, spot, False, dims).T)
    store_split(v_ref, edge, x_ref[...].T)
    store_split(v_ref, edge + rows, halo(right_ref, edge, spot, True, dims).T)
    for b in range(chunk):
        at = [(cols_ref[n, spot * chunk + b] - base + GHOST) * size for n in range(slots)]
        c_ref[b * size : (b + 1) * size, :] = product(a_ref[b], at, v_ref, size)
    coupled = c_ref[...].T
    kd = row_of(kd_ref, spot, rows)
    start = row_of(start_ref, spot, rows)
    for j, at in enumerate(range(0, total, steps)):
        last = jnp.where(flip == 1, lasts[1][j], lasts[0][j])
        previous = jnp.where(last < 0, start, x_ref[pl.ds(jnp.maximum(last, 0), 1), :])
        span = slice(at, at + steps)
        now = x_ref[span, :]
        previous = jnp.concatenate([previous, now[: steps - 1]], axis=0)
        out_ref[span, :] = f_ref[span, :] + previous - (1.0 + kd) * now - coupled[span]
    out_ref[total:, :] = jnp.broadcast_to(kd, (8, rows))


def sweeps_kernel(
    dims, where_ref, cols_ref, near_ref, a_ref, an_ref, x_ref, r_ref, left_ref, right_ref, fwd_ref, back_ref, lam_ref, out_ref,
    s_ref, cr_ref, ci_ref, v0_ref, v1_ref, y_ref,
):
    size, slots, chunk, total, _ = dims
    rows = chunk * size
    wide = 2 * GHOST * size
    half = total // 2
    spot, flip, base = where_ref[0], where_ref[1], where_ref[2]
    block_rows = cols_ref.shape[1]

    def forward(value):
        high, low = split(value)
        stacked = jnp.concatenate([high, low, high, low], axis=0)
        return lax.dot_general(stacked, fwd_ref[flip], (((0,), (0,)), ((), ())), preferred_element_type=F32)

    s_ref[0:wide, :] = forward(halo(left_ref, wide, spot, False, dims))
    s_ref[wide : wide + rows, :] = forward(r_ref[:total])
    s_ref[wide + rows :, :] = forward(halo(right_ref, wide, spot, True, dims))
    kd = jnp.concatenate([ref[total : total + 1] for ref in (left_ref, r_ref, right_ref)], axis=1)
    kd = jnp.broadcast_to(kd, (total, kd.shape[1])).T
    diag = kd + lam_ref[0:1, :]
    imag = lam_ref[1:2, :]
    inverse = 1.0 / (diag * diag + imag * imag)
    cr_ref[...] = diag * inverse
    ci_ref[...] = imag * inverse

    def divide(value, at):
        swapped = jnp.concatenate([value[:, half:], value[:, :half]], axis=1)
        span = slice(at, at + value.shape[0])
        return value * cr_ref[span, :] + swapped * ci_ref[span, :]

    def column(n, b):
        row = spot * chunk + b
        found = cols_ref[n, jnp.clip(row, 0, block_rows - 1)]
        if b < 0:
            found = jnp.where(row < 0, near_ref[n, jnp.maximum(row + GHOST, 0)], found)
        if b >= chunk:
            found = jnp.where(row >= block_rows, near_ref[n, GHOST + jnp.maximum(row - block_rows, 0)], found)
        return jnp.clip(found - base, -2 * GHOST, chunk + 2 * GHOST - 1)

    store_split(v0_ref, 0, divide(s_ref[...], 0))
    for b in range(-GHOST, chunk + GHOST):
        at = (b + 2 * GHOST) * size
        a = a_ref[b] if 0 <= b < chunk else an_ref[b + GHOST if b < 0 else b - chunk + GHOST]
        coupled = product(a, [(column(n, b) + 2 * GHOST) * size for n in range(slots)], v0_ref, size)
        store_split(v1_ref, at - GHOST * size, divide(s_ref[at : at + size, :] - coupled, at))
    for b in range(chunk):
        at = (b + 2 * GHOST) * size
        coupled = product(a_ref[b], [(column(n, b) + GHOST) * size for n in range(slots)], v1_ref, size)
        high, low = split(divide(s_ref[at : at + size, :] - coupled, at))
        y_ref[b * size : (b + 1) * size, :] = jnp.concatenate([high, low, high, low], axis=1)
    change = lax.dot_general(back_ref[flip], y_ref[...], (((1,), (1,)), ((), ())), preferred_element_type=F32)
    out_ref[...] = x_ref[...] + change


def vmem(count):
    return [pl.BlockSpec(memory_space=pltpu.VMEM)] * count


def smem(count):
    return [pl.BlockSpec(memory_space=pltpu.SMEM)] * count


PARAMS = pltpu.CompilerParams(vmem_limit_bytes=48 * 1024 * 1024)


def local(start_state, forcing, iterate, blocks, columns, kdiag):
    steps, rows_dev = iterate.shape
    block_rows, size, width = blocks.shape
    slots = width // size
    n_tm, n_space = lax.axis_size("tm"), lax.axis_size("space")
    total = steps * n_tm
    chunk = block_rows // n_tm
    rows = chunk * size
    edge = GHOST * size
    wide = 2 * edge
    dims = (size, slots, chunk, total, steps)
    order = there_and_back(n_tm)

    tm_index, space_index = lax.axis_index("tm"), lax.axis_index("space")
    flipped = space_index % 2 == 1
    spot = jnp.where(tm_index % 2 == 0, tm_index // 2, n_tm - 1 - tm_index // 2)
    spot = jnp.where(flipped, n_tm - 1 - spot, spot)
    even = (space_index * n_tm + spot) % 2 == 0

    groups, ring = [], []
    for s in range(n_space):
        members = [t * n_space + s for t in (order if s % 2 == 0 else order[::-1])]
        groups.append(tuple(members))
        ring += members
    groups = tuple(groups)
    count = len(ring)

    def deal(value):
        return lax.all_to_all(value, AXES, 0, 0, axis_index_groups=groups, tiled=True)

    def ring_pairs(first):
        pairs = []
        for i in range(first, count - 1, 2):
            pairs += [(ring[i], ring[i + 1]), (ring[i + 1], ring[i])]
        return pairs

    def neighbours(value, extent):
        if extent <= rows:
            low, high = value[:, :extent], value[:, rows - extent :]
            from_a = lax.ppermute(jnp.where(even, high, low), AXES, ring_pairs(0))
            from_b = lax.ppermute(jnp.where(even, low, high), AXES, ring_pairs(1))
            return jnp.where(even, from_b, from_a), jnp.where(even, from_a, from_b)
        left, right = [], []
        for hop in range(1, extent // rows + 1):
            up = [(ring[i], ring[i + hop]) for i in range(count - hop)]
            left.insert(0, lax.ppermute(value, AXES, up))
            right.append(lax.ppermute(value, AXES, [(j, i) for i, j in up]))
        return jnp.concatenate(left, axis=1), jnp.concatenate(right, axis=1)

    both = pl.pallas_call(
        deal_kernel,
        in_specs=vmem(2),
        out_specs=vmem(1)[0],
        out_shape=jax.ShapeDtypeStruct((n_tm, 2, steps, rows), F32),
        name="deal",
    )(iterate, forcing)
    dealt = deal(both)
    x = dealt[:, 0].reshape(total, rows)
    f = dealt[:, 1].reshape(total, rows)
    times = [[t * steps + j for t in members for j in range(steps)] for members in (order, order[::-1])]
    made = [tables(total, at) for at in times]
    fwd = np.stack([made[0][0], made[1][0]])
    back = np.stack([made[0][1], made[1][1]])
    lasts = [[at.index(at[j] - 1) if at[j] else -1 for j in range(0, total, steps)] for at in times]
    base = space_index * block_rows + spot * chunk
    scalars = [spot, flipped.astype(jnp.int32), base, jnp.int32(0), jnp.int32(n_tm - 1)]
    where = jnp.stack(scalars).astype(jnp.int32)
    columns = columns.T

    alone = chunk >= 2 * GHOST and n_tm > 1
    out_shape = [jax.ShapeDtypeStruct((n, 2 * size, width), BF16) for n in (chunk, 2 * GHOST)]
    if alone:
        out_shape.append(jax.ShapeDtypeStruct((edge + 8, width), F32))
    a_own, a_near, *outer = pl.pallas_call(
        blocks_kernel,
        in_specs=smem(2) + [pl.BlockSpec(memory_space=pl.ANY)],
        out_specs=vmem(len(out_shape)),
        out_shape=out_shape,
        scratch_shapes=[
            pltpu.VMEM((chunk + 2 * GHOST, size, width), F32),
            pltpu.SemaphoreType.DMA((chunk + 2 * GHOST,)),
        ],
        compiler_params=PARAMS,
        name="blocks",
    )(where, columns, blocks)
    if alone:
        pairs = []
        for s in range(n_space - 1):
            i, j = ring[(s + 1) * n_tm - 1], ring[(s + 1) * n_tm]
            pairs += [(i, j), (j, i)]
        outer = lax.ppermute(outer[0], AXES, pairs)
        columns_halo = outer[edge, : GHOST * slots].reshape(slots, GHOST).astype(jnp.int32)
        columns_halo = jnp.concatenate([columns_halo, columns_halo], axis=1)
        a_near = pl.pallas_call(
            patch_kernel,
            in_specs=smem(1) + vmem(2),
            out_specs=vmem(1)[0],
            out_shape=jax.ShapeDtypeStruct(a_near.shape, BF16),
            input_output_aliases={1: 0},
            compiler_params=PARAMS,
            name="patch",
        )(where, a_near, outer)
    else:
        up = [(s, s + 1) for s in range(n_space - 1)]
        down = [(j, i) for i, j in up]
        blocks_halo = [lax.ppermute(blocks[-GHOST:], "space", up), lax.ppermute(blocks[:GHOST], "space", down)]
        blocks_halo = jnp.concatenate(blocks_halo, axis=0)
        columns_halo = [lax.ppermute(columns[:, -GHOST:], "space", up), lax.ppermute(columns[:, :GHOST], "space", down)]
        columns_halo = jnp.concatenate(columns_halo, axis=1)
        unit = math.gcd(chunk, GHOST)
        units = np.arange(0, GHOST, unit)
        at = jnp.concatenate([spot * chunk - GHOST + units, (spot + 1) * chunk + units]) // unit
        own_units, halo_units = block_rows // unit, GHOST // unit
        halo_at = jnp.where(at < 0, at + halo_units, at - own_units + halo_units)
        outside = (at < 0) | (at >= own_units)
        sel = [jnp.clip(at, 0, own_units - 1), outside, jnp.clip(halo_at, 0, 2 * halo_units - 1)]
        a_near = pl.pallas_call(
            near_blocks_kernel,
            grid_spec=pltpu.PrefetchScalarGridSpec(
                num_scalar_prefetch=1,
                grid=(2 * halo_units,),
                in_specs=[
                    pl.BlockSpec((unit, size, width), lambda i, sel: (sel[0, i], 0, 0)),
                    pl.BlockSpec((unit, size, width), lambda i, sel: (sel[2, i], 0, 0)),
                ],
                out_specs=pl.BlockSpec((unit, 2 * size, width), lambda i, sel: (i, 0, 0)),
            ),
            out_shape=jax.ShapeDtypeStruct((2 * GHOST, 2 * size, width), BF16),
            compiler_params=PARAMS,
            name="near_blocks",
        )(jnp.stack(sel).astype(jnp.int32), blocks, blocks_halo)

    x_left, x_right = neighbours(x, edge)
    residual = pl.pallas_call(
        functools.partial(residual_kernel, dims, lasts),
        in_specs=smem(2) + vmem(7),
        out_specs=vmem(1)[0],
        out_shape=jax.ShapeDtypeStruct((total + 8, rows), F32),
        scratch_shapes=[pltpu.VMEM((rows + 2 * edge, 2 * total), BF16), pltpu.VMEM((rows, total), F32)],
        compiler_params=PARAMS,
        name="residual",
    )(where, columns, a_own, x, f, x_left, x_right, start_state.reshape(-1, 128), kdiag.reshape(-1, 128))

    left, right = neighbours(residual, wide)
    span = rows + 2 * wide
    result = pl.pallas_call(
        functools.partial(sweeps_kernel, dims),
        in_specs=smem(3) + vmem(9),
        out_specs=vmem(1)[0],
        out_shape=jax.ShapeDtypeStruct((total, rows), F32),
        scratch_shapes=[pltpu.VMEM((span, total), F32)] * 3
        + [
            pltpu.VMEM((span, 2 * total), BF16),
            pltpu.VMEM((span - wide, 2 * total), BF16),
            pltpu.VMEM((rows, 4 * total), BF16),
        ],
        compiler_params=PARAMS,
        name="sweeps",
    )(where, columns, columns_halo, a_own, a_near, x, residual, left, right, fwd, back, made[0][2])

    returned = deal(result.reshape(n_tm, steps, rows))
    return returned.transpose(1, 0, 2).reshape(steps, rows_dev)


def solution(mesh):
    placed = (
        P("space"),
        P("tm", "space"),
        P("tm", "space"),
        P("space", None, None),
        P("space", None),
        P("space"),
    )
    return jax.shard_map(local, mesh=mesh, in_specs=placed, out_specs=P("tm", "space"), check_vma=False)
```

time: 54.5 us -> 50.9 us (0.934)
  waiting for transfers between devices: 3.05 us -> 8.69 us
  local copies, waits for them, and re-layouts: 6.09 us -> 1.55 us
  other arithmetic: 5.18 us -> 1.05 us
  Pallas kernels: 8.26 us -> 11.1 us
  blocking collectives: 15 us -> 12.9 us
  between operations: 1.57 us -> 0.16 us
    all_to_all x1, waiting for transfers between devices: 0.01 us -> 3.7 us  [deal(): lax.all_to_all(value, AXES, 0, 0, axis_index_groups=groups, tiled=True)]
    dynamic_slice x3 -> x0, local copies, waits for them, and re-layouts: 2.84 us -> none  [the longest x1 1.24 us: local(): spot = jnp.asarray(place, jnp.int32)[tm_index]]
    pallas_call x3 -> x5, Pallas kernels: 8.26 us -> 11.1 us  [the longest x1 3.7 us: local(): pl.pallas_call(functools.partial(sweeps_kernel, dims), in_specs=smem(3) +...]
    all_to_all x1, blocking collectives: 15 us -> 12.9 us  [deal(): lax.all_to_all(value, AXES, 0, 0, axis_index_groups=groups, tiled=True)]
    ppermute x2, waiting for transfers between devices: 3.04 us -> 4.98 us  [neighbours(): from_a = lax.ppermute(jnp.where(even, high, low), AXES, ring_pairs(0))]
    another operation x2 -> x0, other arithmetic: 1.69 us -> none  [the longest x1 1.68 us: local(): jnp.stack([v.reshape(steps, n_tm, rows).transpose(1, 0, 2) for v in (iter...]
    select_n x6 -> x2, other arithmetic: 2.45 us -> 0.95 us  [neighbours(): return (jnp.where(even, from_b, from_a), jnp.where(even, from_a, from_b))]
    slice x4 -> x0, local copies, waits for them, and re-layouts: 1.33 us -> none  [the longest x2 1.28 us: local(): high = packed(blocks[-GHOST:], columns[-GHOST:], kdiag[-wide:])]
  transfers between devices with their start and end apart: 6 -> 6, of which waited for: 1 -> 3; matrix products, arithmetic and copies ran while one was open for 16% -> 1% of each run, Pallas kernels for 6% -> 11%
where the time goes in v2:
time: 50.9 us; the launch traced here: 50.5 us
  starting transfers between devices  15 us (29%)
  blocking collectives  12.9 us (25%)
  Pallas kernels  11.1 us (22%)
  waiting for transfers between devices  8.69 us (17%)
  local copies, waits for them, and re-layouts  1.55 us (3%)
  other arithmetic  1.05 us (2%)
    all_to_all x1, blocking collectives, deal(): lax.all_to_all(value, AXES, 0, 0, axis_index_groups=groups, tiled=True)  12.9 us
    all_to_all x1, starting transfers between devices, deal(): lax.all_to_all(value, AXES, 0, 0, axis_index_groups=groups, tiled=True)  7.32 us
    ppermute x2, starting transfers between devices, neighbours(): from_a = lax.ppermute(jnp.where(even, high, low), AXES, ring_pairs(0))  5.05 us
    ppermute x2, waiting for transfers between devices, neighbours(): from_a = lax.ppermute(jnp.where(even, high, low), AXES, ring_pairs(0))  4.98 us
    pallas_call x1, Pallas kernels, local(): pl.pallas_call(functools.partial(sweeps_kernel, dims), in_specs=smem(3) +...  3.7 us
    all_to_all x1, waiting for transfers between devices, deal(): lax.all_to_all(value, AXES, 0, 0, axis_index_groups=groups, tiled=True)  3.7 us
    pallas_call x1, Pallas kernels, local(): pl.pallas_call(blocks_kernel, in_specs=smem(2) + [pl.BlockSpec(memory_spa...  3.4 us
    ppermute x2, starting transfers between devices, neighbours(): from_b = lax.ppermute(jnp.where(even, low, high), AXES, ring_pairs(1))  1.96 us
  transfers between devices with their start and end apart: 6, of which 3 were waited for; matrix products, arithmetic and copies ran while one was open for 1% of the time, Pallas kernels for 11%

profile of v2, /device:TPU:0, one launch (start us, length us, event | category | flops | bytes accessed | tf_op | source)
XLA Modules:
  0.0 50.5 jit_solution(17951848914556312457)
XLA Ops:
  0.0 1.8 %deal.1 = f32[8,2,8,512]{3,2,1,0:T(8,128)} custom-call(f32[8,4096]{1,0:T(8,128)} %x_ref.1, f32[8,4096]{1,0:T(8,128)} %f_ref.1), custom_call_target="tpu_custom_call" | custom-call | tf_op jit(solution)/shard_map/deal/pallas_call | solution.py:306
  1.8 7.3 %all-to-all-start = ((f32[8,2,8,512]{3,2,1,0:T(8,128)}), f32[8,2,8,512]{3,2,1,0:T(8,128)S(1)}, u32[]{:S(2)}, u32[]{:S(2)}) async-start(f32[8,2,8,512]{3,2,1,0:T(8,128)} %deal.1), calls=%async_computation | async-start | bytes 524288 | tf_op jit(solution)/shard_map/all_to_all | solution.py:285
  9.1 0.1 stack.19.where_ref
  9.2 0.7 %copy-done.2 = s32[64,7]{0,1:T(8,128)S(1)} copy-done((s32[64,7]{0,1:T(8,128)S(1)}, s32[64,7]{0,1:T(8,128)}, u32[]{:S(2)}) %copy-start.2) | copy-done | bytes 1816
  9.9 3.4 %blocks.1 = (bf16[8,128,448]{2,1,0:T(8,128)(2,1)S(1)}, bf16[8,128,448]{2,1,0:T(8,128)(2,1)S(1)}, f32[264,448]{1,0:T(8,128)}) custom-call(s32[5]{0:T(128)S(1)} %stack.19.where_ref, s32[7,64]{1,0:T(8,128)S(1)} %bitcast.15, f32[64,64,448]{2,1,0:T(8,128)} %blocks_ref.1), custom_call_target="tpu_custom_call" | custom-call | tf_op jit(solution)/shard_map/blocks/pallas_call | solution.py:330
  13.3 0.7 %collective-permute-start = (f32[264,448]{1,0:T(8,128)}, f32[264,448]{1,0:T(8,128)S(1)}, u32[]{:S(2)}, u32[]{:S(2)}) collective-permute-start(f32[264,448]{1,0:T(8,128)} %get-tuple-element.8), channel_id=1, source_target_pairs={{4,5},{5,4},{1,2},{2,1},{6,7},{7,6}} | collective-permute-start | bytes 1419272 | tf_op jit(solution)/shard_map/ppermute | solution.py:347
  14.0 3.7 %all-to-all-done = f32[8,2,8,512]{3,2,1,0:T(8,128)S(1)} async-done(((f32[8,2,8,512]{3,2,1,0:T(8,128)}), f32[8,2,8,512]{3,2,1,0:T(8,128)S(1)}, u32[]{:S(2)}, u32[]{:S(2)}) %all-to-all-start) | async-done | bytes 262176 | tf_op jit(solution)/shard_map/all_to_all | solution.py:285
  17.8 1.1 %collective-permute-start.2 = (f32[64,256]{1,0:T(8,128)S(1)}, f32[64,256]{1,0:T(8,128)S(1)}, u32[]{:S(2)}, u32[]{:S(2)}) collective-permute-start(f32[64,256]{1,0:T(8,128)S(1)} %get-tuple-element.17), channel_id=1, source_target_pairs={{0,8},{8,0},{16,24},{24,16},{28,20},{20,28},{12,4},{4,12},{5,13},{... | collective-permute-start | bytes 196616 | tf_op jit(solution)/shard_map/ppermute | solution.py:296
  18.8 0.7 %collective-permute-start.1 = (f32[64,256]{1,0:T(8,128)S(1)}, f32[64,256]{1,0:T(8,128)S(1)}, u32[]{:S(2)}, u32[]{:S(2)}) collective-permute-start(f32[64,256]{1,0:T(8,128)S(1)} %get-tuple-element.18), channel_id=1, source_target_pairs={{8,16},{16,8},{24,28},{28,24},{20,12},{12,20},{4,5},{5,4},{13,21},... | collective-permute-start | bytes 196616 | tf_op jit(solution)/shard_map/ppermute | solution.py:297
  19.5 2.6 %collective-permute-done.2 = f32[64,256]{1,0:T(8,128)S(1)} collective-permute-done((f32[64,256]{1,0:T(8,128)S(1)}, f32[64,256]{1,0:T(8,128)S(1)}, u32[]{:S(2)}, u32[]{:S(2)}) %collective-permute-start.2) | collective-permute-done | bytes 65568 | tf_op jit(solution)/shard_map/ppermute | solution.py:296
  22.1 0.0 collective-permute-done.1
  22.1 1.6 %residual.1.r_ref = f32[72,512]{1,0:T(8,128)S(1)} custom-call(s32[5]{0:T(128)S(1)} %stack.19.where_ref, s32[7,64]{1,0:T(8,128)S(1)} %bitcast.16, bf16[8,128,448]{2,1,0:T(8,128)(2,1)S(1)} %get-tuple-element.9.a_ref, f32[64,512]{1,0:T(8,128)S(1)} %get-tuple-element.14.x_ref, f32[64,512]{1,0:T(8,128)S(1)} %get-tuple-element.13.f_ref, ...), custom_call_target="tpu_custom_call" | custom-call | tf_op jit(solution)/shard_map/residual/pallas_call | solution.py:390
  23.7 4.0 %collective-permute-start.4 = (f32[72,512]{1,0:T(8,128)S(1)}, f32[72,512]{1,0:T(8,128)S(1)}, u32[]{:S(2)}, u32[]{:S(2)}) collective-permute-start(f32[72,512]{1,0:T(8,128)S(1)} %residual.1.r_ref), channel_id=1, source_target_pairs={{0,8},{8,0},{16,24},{24,16},{28,20},{20,28},{12,4},{4,12},{5,13},{... | collective-permute-start | bytes 442376 | tf_op jit(solution)/shard_map/ppermute | solution.py:296
  27.7 1.3 %collective-permute-start.3 = (f32[72,512]{1,0:T(8,128)S(1)}, f32[72,512]{1,0:T(8,128)}, u32[]{:S(2)}, u32[]{:S(2)}) collective-permute-start(f32[72,512]{1,0:T(8,128)S(1)} %residual.1.r_ref), channel_id=1, source_target_pairs={{8,16},{16,8},{24,28},{28,24},{20,12},{12,20},{4,5},{5,4},{13,21},... | collective-permute-start | bytes 442376 | tf_op jit(solution)/shard_map/ppermute | solution.py:297
  29.0 0.0 collective-permute-done.halo_ref
  29.0 0.1 convert_element_type.8
  29.1 0.6 %patch.1.an_ref = bf16[8,128,448]{2,1,0:T(8,128)(2,1)S(1)} custom-call(s32[5]{0:T(128)S(1)} %stack.19.where_ref, bf16[8,128,448]{2,1,0:T(8,128)(2,1)S(1)} %get-tuple-element.10.old_ref, f32[264,448]{1,0:T(8,128)S(1)} %collective-permute-done.halo_ref), custom_call_target="tpu_custom_call", output_to_operand_aliasing={{}: (1, {})} | custom-call | tf_op jit(solution)/shard_map/patch/pallas_call | solution.py:350
  29.7 0.1 pad_add_fusion.near_ref
  29.8 2.4 %collective-permute-done.4 = f32[72,512]{1,0:T(8,128)S(1)} collective-permute-done((f32[72,512]{1,0:T(8,128)S(1)}, f32[72,512]{1,0:T(8,128)S(1)}, u32[]{:S(2)}, u32[]{:S(2)}) %collective-permute-start.4) | collective-permute-done | bytes 147488 | tf_op jit(solution)/shard_map/ppermute | solution.py:296
  32.2 0.0 collective-permute-done.3
  32.2 0.9 %broadcast_select_fusion = (f32[72,512]{1,0:T(8,128)S(1)}, f32[72,512]{1,0:T(8,128)S(1)}) fusion(f32[72,512]{1,0:T(8,128)S(1)} %collective-permute-done.4, f32[72,512]{1,0:T(8,128)} %collective-permute-done.3, pred[]{:T(512)S(6)} %eq.15), kind=kLoop, calls=%fused_computation.2 | loop fusion | flops 73728 | bytes 589825 | tf_op jit(solution)/shard_map/jit(_where)/select_n | solution.py:298
  33.2 3.7 %sweeps.1 = f32[64,512]{1,0:T(8,128)S(1)} custom-call(s32[5]{0:T(128)S(1)} %stack.19.where_ref, s32[7,64]{1,0:T(8,128)S(1)} %bitcast.17, s32[7,8]{1,0:T(8,128)S(1)} %pad_add_fusion.near_ref, bf16[8,128,448]{2,1,0:T(8,128)(2,1)S(1)} %get-tuple-element.9.a_ref, bf16[8,128,448]{2,1,0:T(8,128)(2,1)S(1)} %patch.1.an_ref, f32[64,512]{1,0:T(8,128)S(1)} %get-tuple-element.14.x_ref, ...), custom_call_target="tpu_custom_call" | custom-call | tf_op jit(solution)/shard_map/sweeps/pallas_call | solution.py:402
  36.9 12.9 %all_to_all.10 = f32[8,8,512]{2,1,0:T(8,128)S(1)} all-to-all(f32[8,8,512]{2,1,0:T(8,128)S(1)} %bitcast.14), channel_id=1, replica_groups={{0,8,16,24,28,20,12,4},{5,13,21,29,25,17,9,1},{2,10,18,26,30,22,14,6},{..., dimensions={0} | all-to-all | bytes 262144 | tf_op jit(solution)/shard_map/all_to_all | solution.py:285
  49.8 0.7 %copy.13 = f32[8,4096]{1,0:T(8,128)} copy(f32[8,4096]{1,0:T(8,128)S(1)} %bitcast.20) | data formatting | bytes 262144
  (17 shorter events, 0.1 us)
Async XLA Ops:
  0.0 33.2 %copy-start = (bf16[2,256,64]{2,1,0:T(8,128)(2,1)S(1)}, bf16[2,256,64]{2,1,0:T(8,128)(2,1)}, u32[]{:S(2)}) copy-start(bf16[2,256,64]{2,1,0:T(8,128)(2,1)} %constant.61.clone.fwd_ref) | copy-start | bytes 196612
  0.0 33.2 %copy-start.1 = (bf16[2,64,256]{2,1,0:T(8,128)(2,1)S(1)}, bf16[2,64,256]{2,1,0:T(8,128)(2,1)}, u32[]{:S(2)}) copy-start(bf16[2,64,256]{2,1,0:T(8,128)(2,1)} %constant.62.clone.back_ref) | copy-start | bytes 196612
  0.0 33.2 %copy-start.6 = (f32[2,64]{1,0:T(2,128)S(1)}, f32[2,64]{1,0:T(2,128)}, u32[]{:S(2)}) copy-start(f32[2,64]{1,0:T(2,128)} %constant.63.clone.lam_ref) | copy-start | bytes 1540
  0.0 22.1 %copy-start.3 = (s32[64,7]{0,1:T(8,128)S(1)}, s32[64,7]{0,1:T(8,128)}, u32[]{:S(2)}) copy-start(s32[64,7]{0,1:T(8,128)} %param.13) | copy-start | bytes 5380
  0.0 22.1 %copy-start.4 = (f32[4096]{0:T(1024)S(1)}, f32[4096]{0:T(1024)}, u32[]{:S(2)}) copy-start(f32[4096]{0:T(1024)} %param.9) | copy-start | bytes 49156
  0.0 22.1 %copy-start.5 = (f32[4096]{0:T(1024)S(1)}, f32[4096]{0:T(1024)}, u32[]{:S(2)}) copy-start(f32[4096]{0:T(1024)} %param.14) | copy-start | bytes 49156
  1.8 15.9 %all-to-all-start = ((f32[8,2,8,512]{3,2,1,0:T(8,128)}), f32[8,2,8,512]{3,2,1,0:T(8,128)S(1)}, u32[]{:S(2)}, u32[]{:S(2)}) async-start(f32[8,2,8,512]{3,2,1,0:T(8,128)} %deal.1), calls=%async_computation | async-start | bytes 524288 | tf_op jit(solution)/shard_map/all_to_all | solution.py:285
  9.2 0.7 %copy-start.2 = (s32[64,7]{0,1:T(8,128)S(1)}, s32[64,7]{0,1:T(8,128)}, u32[]{:S(2)}) copy-start(s32[64,7]{0,1:T(8,128)} %param.13) | copy-start | bytes 5380
  13.3 15.7 %collective-permute-start = (f32[264,448]{1,0:T(8,128)}, f32[264,448]{1,0:T(8,128)S(1)}, u32[]{:S(2)}, u32[]{:S(2)}) collective-permute-start(f32[264,448]{1,0:T(8,128)} %get-tuple-element.8), channel_id=1, source_target_pairs={{4,5},{5,4},{1,2},{2,1},{6,7},{7,6}} | collective-permute-start | bytes 1419272 | tf_op jit(solution)/shard_map/ppermute | solution.py:347
  17.8 4.3 %collective-permute-start.2 = (f32[64,256]{1,0:T(8,128)S(1)}, f32[64,256]{1,0:T(8,128)S(1)}, u32[]{:S(2)}, u32[]{:S(2)}) collective-permute-start(f32[64,256]{1,0:T(8,128)S(1)} %get-tuple-element.17), channel_id=1, source_target_pairs={{0,8},{8,0},{16,24},{24,16},{28,20},{20,28},{12,4},{4,12},{5,13},{... | collective-permute-start | bytes 196616 | tf_op jit(solution)/shard_map/ppermute | solution.py:296
  18.8 3.3 %collective-permute-start.1 = (f32[64,256]{1,0:T(8,128)S(1)}, f32[64,256]{1,0:T(8,128)S(1)}, u32[]{:S(2)}, u32[]{:S(2)}) collective-permute-start(f32[64,256]{1,0:T(8,128)S(1)} %get-tuple-element.18), channel_id=1, source_target_pairs={{8,16},{16,8},{24,28},{28,24},{20,12},{12,20},{4,5},{5,4},{13,21},... | collective-permute-start | bytes 196616 | tf_op jit(solution)/shard_map/ppermute | solution.py:297
  23.7 8.5 %collective-permute-start.4 = (f32[72,512]{1,0:T(8,128)S(1)}, f32[72,512]{1,0:T(8,128)S(1)}, u32[]{:S(2)}, u32[]{:S(2)}) collective-permute-start(f32[72,512]{1,0:T(8,128)S(1)} %residual.1.r_ref), channel_id=1, source_target_pairs={{0,8},{8,0},{16,24},{24,16},{28,20},{20,28},{12,4},{4,12},{5,13},{... | collective-permute-start | bytes 442376 | tf_op jit(solution)/shard_map/ppermute | solution.py:296
  27.7 4.5 %collective-permute-start.3 = (f32[72,512]{1,0:T(8,128)S(1)}, f32[72,512]{1,0:T(8,128)}, u32[]{:S(2)}, u32[]{:S(2)}) collective-permute-start(f32[72,512]{1,0:T(8,128)S(1)} %residual.1.r_ref), channel_id=1, source_target_pairs={{8,16},{16,8},{24,28},{28,24},{20,12},{12,20},{4,5},{5,4},{13,21},... | collective-permute-start | bytes 442376 | tf_op jit(solution)/shard_map/ppermute | solution.py:297

commit v3 on v2

--- a/solution.py
+++ b/solution.py
@@ -38,18 +38,22 @@
     nyquist = np.where(t % 2 == 0, 1.0, -1.0)
     cos, sin = np.cos(angle), np.sin(angle)
     grow = CORNER_WEIGHT ** (t / total)
+
+    def swapped(value):
+        return np.roll(value, half, axis=1)
+
     forward = np.concatenate([cos, nyquist, -sin[:, 1:]], axis=1) * grow
+    high, low = np_split(np.concatenate([forward, swapped(forward)], axis=1))
+    forward = np.concatenate([high, low], axis=1)
     twice = np.where(freq == 0, 1.0, 2.0)[None]
-    back = np.concatenate([twice * cos, nyquist, -2.0 * sin[:, 1:]], axis=1) / grow / total
-    high, low = np_split(forward)
-    forward = np.concatenate([high, high, low, low], axis=0)
-    high, low = np_split(back)
-    back = np.concatenate([high, high, low, low], axis=1)
+    high, low = np_split(np.concatenate([twice * cos, nyquist, -2.0 * sin[:, 1:]], axis=1) / grow / total)
+    back = np.concatenate([high, swapped(low)] * 2, axis=1)
     root = CORNER_WEIGHT ** (1.0 / total)
     theta = 2.0 * math.pi * freq / total
     lam_re = np.concatenate([1.0 - root * np.cos(theta), [1.0 + root], 1.0 - root * np.cos(theta[1:])])
     lam_im = np.concatenate([root * np.sin(theta), [0.0], -root * np.sin(theta[1:])])
-    return forward, back, np.stack([lam_re, lam_im]).astype(np.float32)
+    lam = np.stack([lam_re, lam_im])
+    return np.concatenate([forward] * 2, axis=0), back, np.concatenate([lam, swapped(lam)], axis=1).astype(np.float32)
 
 
 def deal_kernel(x_ref, f_ref, out_ref):
@@ -94,16 +98,16 @@
         ref[GHOST * size :, :] = found.astype(F32)
 
 
-def patch_kernel(where_ref, old_ref, halo_ref, out_ref):
+def patch_kernel(last, where_ref, old_ref, halo_ref, out_ref):
     size = out_ref.shape[1] // 2
-    spot, first, last = where_ref[0], where_ref[3], where_ref[4]
+    spot = where_ref[0]
 
     def put(at, row):
         high, low = split(halo_ref[row * size : (row + 1) * size, :])
         out_ref[at, :size] = high
         out_ref[at, size:] = low
 
-    @pl.when(spot == first)
+    @pl.when(spot == 0)
     def _():
         for b in range(GHOST):
             put(b, b)
@@ -127,18 +131,19 @@
     picked = jnp.concatenate([v_ref[pl.ds(pl.multiple_of(row, size), size), :] for row in at], axis=0)
     out = jnp.dot(a, picked, preferred_element_type=F32)
     out = out[:size] + out[size:]
-    channels = out.shape[1] // 2
-    return out[:, :channels] + out[:, channels:]
+    half = out.shape[1] // 2
+    return out[:, :half] + out[:, half:]
 
 
 def store_split(ref, at, value):
     high, low = split(value)
     rows, channels = value.shape
+    half = ref.shape[1] // 2
     ref[at : at + rows, :channels] = high
-    ref[at : at + rows, channels:] = low
-
-
-def halo(ref, extent, spot, after, dims):
+    ref[at : at + rows, half : half + channels] = low
+
+
+def halo(first_ref, second_ref, take_second, extent, spot, after, dims):
     size, slots, chunk, total, steps = dims
     count = total // steps
     width = min(extent, chunk * size)
@@ -150,7 +155,8 @@
         rows = []
         for j in range(count):
             at = pl.multiple_of(jnp.where(crossed, count - 1 - j, j) * steps, steps)
-            rows.append(ref[pl.ds(at, steps), lanes])
+            first, second = first_ref[pl.ds(at, steps), lanes], second_ref[pl.ds(at, steps), lanes]
+            rows.append(jnp.where(take_second, second, first))
         parts.append(jnp.concatenate(rows, axis=0))
     return parts[0] if pieces == 1 else jnp.concatenate(parts, axis=1)
 
@@ -162,52 +168,55 @@
 
 
 def residual_kernel(
-    dims, lasts, where_ref, cols_ref, a_ref, x_ref, f_ref, left_ref, right_ref, start_ref, kd_ref, out_ref, v_ref, c_ref
+    dims, lasts, where_ref, cols_ref, a_ref, xf_ref, one_ref, two_ref, start_ref, kd_ref, out_ref, v_ref, c_ref
 ):
     size, slots, chunk, total, steps = dims
     rows = chunk * size
     edge = GHOST * size
-    spot, flip, base = where_ref[0], where_ref[1], where_ref[2]
-    store_split(v_ref, 0, halo(left_ref, edge, spot, False, dims).T)
-    store_split(v_ref, edge, x_ref[...].T)
-    store_split(v_ref, edge + rows, halo(right_ref, edge, spot, True, dims).T)
+    spot, flip, base, even = where_ref[0], where_ref[1], where_ref[2], where_ref[3] == 1
+    store_split(v_ref, 0, halo(one_ref, two_ref, even, edge, spot, False, dims).T)
+    store_split(v_ref, edge, xf_ref[:, 0].reshape(total, rows).T)
+    store_split(v_ref, edge + rows, halo(two_ref, one_ref, even, edge, spot, True, dims).T)
     for b in range(chunk):
         at = [(cols_ref[n, spot * chunk + b] - base + GHOST) * size for n in range(slots)]
-        c_ref[b * size : (b + 1) * size, :] = product(a_ref[b], at, v_ref, size)
+        c_ref[b * size : (b + 1) * size, :] = product(a_ref[b], at, v_ref, size)[:, :total]
     coupled = c_ref[...].T
     kd = row_of(kd_ref, spot, rows)
     start = row_of(start_ref, spot, rows)
-    for j, at in enumerate(range(0, total, steps)):
+    for j in range(total // steps):
         last = jnp.where(flip == 1, lasts[1][j], lasts[0][j])
-        previous = jnp.where(last < 0, start, x_ref[pl.ds(jnp.maximum(last, 0), 1), :])
-        span = slice(at, at + steps)
-        now = x_ref[span, :]
+        previous = jnp.where(last < 0, start, xf_ref[jnp.maximum(last, 0), 0, steps - 1 : steps, :])
+        span = slice(j * steps, (j + 1) * steps)
+        now = xf_ref[j, 0]
         previous = jnp.concatenate([previous, now[: steps - 1]], axis=0)
-        out_ref[span, :] = f_ref[span, :] + previous - (1.0 + kd) * now - coupled[span]
+        out_ref[span, :] = xf_ref[j, 1] + previous - (1.0 + kd) * now - coupled[span]
     out_ref[total:, :] = jnp.broadcast_to(kd, (8, rows))
 
 
 def sweeps_kernel(
-    dims, where_ref, cols_ref, near_ref, a_ref, an_ref, x_ref, r_ref, left_ref, right_ref, fwd_ref, back_ref, lam_ref, out_ref,
+    dims, where_ref, cols_ref, near_ref, a_ref, an_ref, xf_ref, r_ref, one_ref, two_ref, fwd_ref, back_ref, lam_ref, out_ref,
     s_ref, cr_ref, ci_ref, v0_ref, v1_ref, y_ref,
 ):
     size, slots, chunk, total, _ = dims
     rows = chunk * size
     wide = 2 * GHOST * size
-    half = total // 2
-    spot, flip, base = where_ref[0], where_ref[1], where_ref[2]
+    spot, flip, base, even = where_ref[0], where_ref[1], where_ref[2], where_ref[4] == 1
     block_rows = cols_ref.shape[1]
-
-    def forward(value):
+    fwd = fwd_ref[flip]
+
+    def forward(at, value):
         high, low = split(value)
-        stacked = jnp.concatenate([high, low, high, low], axis=0)
-        return lax.dot_general(stacked, fwd_ref[flip], (((0,), (0,)), ((), ())), preferred_element_type=F32)
-
-    s_ref[0:wide, :] = forward(halo(left_ref, wide, spot, False, dims))
-    s_ref[wide : wide + rows, :] = forward(r_ref[:total])
-    s_ref[wide + rows :, :] = forward(halo(right_ref, wide, spot, True, dims))
-    kd = jnp.concatenate([ref[total : total + 1] for ref in (left_ref, r_ref, right_ref)], axis=1)
-    kd = jnp.broadcast_to(kd, (total, kd.shape[1])).T
+        stacked = jnp.concatenate([high, low], axis=0)
+        out = lax.dot_general(stacked, fwd, (((0,), (0,)), ((), ())), preferred_element_type=F32)
+        s_ref[at : at + value.shape[1], :] = out[:, : 2 * total] + out[:, 2 * total :]
+
+    forward(wide, r_ref[:total])
+    forward(0, halo(one_ref, two_ref, even, wide, spot, False, dims))
+    forward(wide + rows, halo(two_ref, one_ref, even, wide, spot, True, dims))
+    first, second = one_ref[total : total + 1], two_ref[total : total + 1]
+    left, right = jnp.where(even, second, first), jnp.where(even, first, second)
+    kd = jnp.concatenate([left, r_ref[total : total + 1], right], axis=1)
+    kd = jnp.broadcast_to(kd, (2 * total, kd.shape[1])).T
     diag = kd + lam_ref[0:1, :]
     imag = lam_ref[1:2, :]
     inverse = 1.0 / (diag * diag + imag * imag)
@@ -215,9 +224,8 @@
     ci_ref[...] = imag * inverse
 
     def divide(value, at):
-        swapped = jnp.concatenate([value[:, half:], value[:, :half]], axis=1)
         span = slice(at, at + value.shape[0])
-        return value * cr_ref[span, :] + swapped * ci_ref[span, :]
+        return value * cr_ref[span, :] + pltpu.roll(value, total, 1) * ci_ref[span, :]
 
     def column(n, b):
         row = spot * chunk + b
@@ -237,10 +245,9 @@
     for b in range(chunk):
         at = (b + 2 * GHOST) * size
         coupled = product(a_ref[b], [(column(n, b) + GHOST) * size for n in range(slots)], v1_ref, size)
-        high, low = split(divide(s_ref[at : at + size, :] - coupled, at))
-        y_ref[b * size : (b + 1) * size, :] = jnp.concatenate([high, low, high, low], axis=1)
+        store_split(y_ref, b * size, divide(s_ref[at : at + size, :] - coupled, at))
     change = lax.dot_general(back_ref[flip], y_ref[...], (((1,), (1,)), ((), ())), preferred_element_type=F32)
-    out_ref[...] = x_ref[...] + change
+    out_ref[...] = xf_ref[:, 0].reshape(total, rows) + change
 
 
 def vmem(count):
@@ -251,7 +258,8 @@
     return [pl.BlockSpec(memory_space=pltpu.SMEM)] * count
 
 
-PARAMS = pltpu.CompilerParams(vmem_limit_bytes=48 * 1024 * 1024)
+PARAMS = pltpu.CompilerParams(vmem_limit_bytes=16 * 1024 * 1024)
+BLOCKS_PARAMS = pltpu.CompilerParams(vmem_limit_bytes=48 * 1024 * 1024)
 
 
 def local(start_state, forcing, iterate, blocks, columns, kdiag):
@@ -295,7 +303,7 @@
             low, high = value[:, :extent], value[:, rows - extent :]
             from_a = lax.ppermute(jnp.where(even, high, low), AXES, ring_pairs(0))
             from_b = lax.ppermute(jnp.where(even, low, high), AXES, ring_pairs(1))
-            return jnp.where(even, from_b, from_a), jnp.where(even, from_a, from_b)
+            return from_a, from_b
         left, right = [], []
         for hop in range(1, extent // rows + 1):
             up = [(ring[i], ring[i + hop]) for i in range(count - hop)]
@@ -312,15 +320,13 @@
     )(iterate, forcing)
     dealt = deal(both)
     x = dealt[:, 0].reshape(total, rows)
-    f = dealt[:, 1].reshape(total, rows)
     times = [[t * steps + j for t in members for j in range(steps)] for members in (order, order[::-1])]
     made = [tables(total, at) for at in times]
     fwd = np.stack([made[0][0], made[1][0]])
     back = np.stack([made[0][1], made[1][1]])
-    lasts = [[at.index(at[j] - 1) if at[j] else -1 for j in range(0, total, steps)] for at in times]
+    lasts = [[at.index(at[j] - 1) // steps if at[j] else -1 for j in range(0, total, steps)] for at in times]
     base = space_index * block_rows + spot * chunk
-    scalars = [spot, flipped.astype(jnp.int32), base, jnp.int32(0), jnp.int32(n_tm - 1)]
-    where = jnp.stack(scalars).astype(jnp.int32)
+    where = jnp.stack([spot, flipped, base] + [even & (extent <= rows) for extent in (edge, wide)]).astype(jnp.int32)
     columns = columns.T
 
     alone = chunk >= 2 * GHOST and n_tm > 1
@@ -329,14 +335,14 @@
         out_shape.append(jax.ShapeDtypeStruct((edge + 8, width), F32))
     a_own, a_near, *outer = pl.pallas_call(
         blocks_kernel,
-        in_specs=smem(2) + [pl.BlockSpec(memory_space=pl.ANY)],
+        in_specs=smem(2) + [pl.BlockSpec(memory_space=pltpu.HBM)],
         out_specs=vmem(len(out_shape)),
         out_shape=out_shape,
         scratch_shapes=[
             pltpu.VMEM((chunk + 2 * GHOST, size, width), F32),
             pltpu.SemaphoreType.DMA((chunk + 2 * GHOST,)),
         ],
-        compiler_params=PARAMS,
+        compiler_params=BLOCKS_PARAMS,
         name="blocks",
     )(where, columns, blocks)
     if alone:
@@ -348,7 +354,7 @@
         columns_halo = outer[edge, : GHOST * slots].reshape(slots, GHOST).astype(jnp.int32)
         columns_halo = jnp.concatenate([columns_halo, columns_halo], axis=1)
         a_near = pl.pallas_call(
-            patch_kernel,
+            functools.partial(patch_kernel, n_tm - 1),
             in_specs=smem(1) + vmem(2),
             out_specs=vmem(1)[0],
             out_shape=jax.ShapeDtypeStruct(a_near.shape, BF16),
@@ -386,33 +392,29 @@
             name="near_blocks",
         )(jnp.stack(sel).astype(jnp.int32), blocks, blocks_halo)
 
-    x_left, x_right = neighbours(x, edge)
+    one, two = neighbours(x, edge)
     residual = pl.pallas_call(
         functools.partial(residual_kernel, dims, lasts),
-        in_specs=smem(2) + vmem(7),
+        in_specs=smem(2) + vmem(6),
         out_specs=vmem(1)[0],
         out_shape=jax.ShapeDtypeStruct((total + 8, rows), F32),
-        scratch_shapes=[pltpu.VMEM((rows + 2 * edge, 2 * total), BF16), pltpu.VMEM((rows, total), F32)],
+        scratch_shapes=[pltpu.VMEM((rows + 2 * edge, 2 * max(total, 128)), BF16), pltpu.VMEM((rows, total), F32)],
         compiler_params=PARAMS,
         name="residual",
-    )(where, columns, a_own, x, f, x_left, x_right, start_state.reshape(-1, 128), kdiag.reshape(-1, 128))
-
-    left, right = neighbours(residual, wide)
+    )(where, columns, a_own, dealt, one, two, start_state.reshape(-1, 128), kdiag.reshape(-1, 128))
+
+    one, two = neighbours(residual, wide)
     span = rows + 2 * wide
     result = pl.pallas_call(
         functools.partial(sweeps_kernel, dims),
         in_specs=smem(3) + vmem(9),
         out_specs=vmem(1)[0],
         out_shape=jax.ShapeDtypeStruct((total, rows), F32),
-        scratch_shapes=[pltpu.VMEM((span, total), F32)] * 3
-        + [
-            pltpu.VMEM((span, 2 * total), BF16),
-            pltpu.VMEM((span - wide, 2 * total), BF16),
-            pltpu.VMEM((rows, 4 * total), BF16),
-        ],
+        scratch_shapes=[pltpu.VMEM((span, 2 * total), F32)] * 3
+        + [pltpu.VMEM((height, 4 * total), BF16) for height in (span, span - wide, rows)],
         compiler_params=PARAMS,
         name="sweeps",
-    )(where, columns, columns_halo, a_own, a_near, x, residual, left, right, fwd, back, made[0][2])
+    )(where, columns, columns_halo, a_own, a_near, dealt, residual, one, two, fwd, back, made[0][2])
 
     returned = deal(result.reshape(n_tm, steps, rows))
     return returned.transpose(1, 0, 2).reshape(steps, rows_dev)

time: 50.9 us -> 48.8 us (0.959)
  Pallas kernels: 11.1 us -> 10.1 us
  local copies, waits for them, and re-layouts: 1.55 us -> 2.19 us
  starting transfers between devices: 15 us -> 14.4 us
    select_n x3 -> x1, other arithmetic: 0.96 us -> 0.01 us  [neighbours(): from_b = lax.ppermute(jnp.where(even, low, high), AXES, ring_pairs(1))]
    pallas_call x1, Pallas kernels: 3.7 us -> 2.94 us  [local(): pl.pallas_call(functools.partial(sweeps_kernel, dims), in_specs=smem(3) +...]
    convert_element_type x1, local copies, waits for them, and re-layouts: 0.08 us -> 0.73 us  [local(): outer[edge, :GHOST * slots].reshape(slots, GHOST).astype(jnp.int32)]
    ppermute x2, starting transfers between devices: 1.96 us -> 1.31 us  [neighbours(): from_b = lax.ppermute(jnp.where(even, low, high), AXES, ring_pairs(1))]
    ppermute x2, waiting for transfers between devices: 4.98 us -> 4.47 us  [neighbours(): from_a = lax.ppermute(jnp.where(even, high, low), AXES, ring_pairs(0))]
    convert_element_type x1, other arithmetic: 0.02 us -> 0.53 us  [local(): outer[edge, :GHOST * slots].reshape(slots, GHOST).astype(jnp.int32)]
  transfers between devices with their start and end apart: 6 -> 6, of which waited for: 3 -> 3; matrix products, arithmetic and copies ran while one was open for 1% -> 3% of each run, Pallas kernels for 11% -> 11%
where the time goes in v3:
time: 48.8 us; the launch traced here: 48.4 us
  starting transfers between devices  14.4 us (30%)
  blocking collectives  12.8 us (26%)
  Pallas kernels  10.1 us (21%)
  waiting for transfers between devices  8.2 us (17%)
  local copies, waits for them, and re-layouts  2.19 us (4%)
  other arithmetic  0.62 us (1%)
    all_to_all x1, blocking collectives, deal(): lax.all_to_all(value, AXES, 0, 0, axis_index_groups=groups, tiled=True)  12.8 us
    all_to_all x1, starting transfers between devices, deal(): lax.all_to_all(value, AXES, 0, 0, axis_index_groups=groups, tiled=True)  7.32 us
    ppermute x2, starting transfers between devices, neighbours(): from_a = lax.ppermute(jnp.where(even, high, low), AXES, ring_pairs(0))  5.04 us
    ppermute x2, waiting for transfers between devices, neighbours(): from_a = lax.ppermute(jnp.where(even, high, low), AXES, ring_pairs(0))  4.47 us
    all_to_all x1, waiting for transfers between devices, deal(): lax.all_to_all(value, AXES, 0, 0, axis_index_groups=groups, tiled=True)  3.73 us
    pallas_call x1, Pallas kernels, local(): pl.pallas_call(blocks_kernel, in_specs=smem(2) + [pl.BlockSpec(memory_spa...  3.41 us
    pallas_call x1, Pallas kernels, local(): pl.pallas_call(functools.partial(sweeps_kernel, dims), in_specs=smem(3) +...  2.94 us
    pallas_call x1, Pallas kernels, local(): pl.pallas_call(deal_kernel, in_specs=vmem(2), out_specs=vmem(1)[0], out_s...  1.77 us
  transfers between devices with their start and end apart: 6, of which 3 were waited for; matrix products, arithmetic and copies ran while one was open for 3% of the time, Pallas kernels for 11%

profile of v3, /device:TPU:0, one launch (start us, length us, event | category | flops | bytes accessed | tf_op | source)
XLA Modules:
  0.0 48.4 jit_solution(8104882076516896947)
XLA Ops:
  0.0 1.8 %deal.1 = f32[8,2,8,512]{3,2,1,0:T(8,128)} custom-call(f32[8,4096]{1,0:T(8,128)} %x_ref.1, f32[8,4096]{1,0:T(8,128)} %f_ref.1), custom_call_target="tpu_custom_call" | custom-call | tf_op jit(solution)/shard_map/deal/pallas_call | solution.py:314
  1.8 7.3 %all-to-all-start = ((f32[8,2,8,512]{3,2,1,0:T(8,128)}), f32[8,2,8,512]{3,2,1,0:T(8,128)S(1)}, u32[]{:S(2)}, u32[]{:S(2)}) async-start(f32[8,2,8,512]{3,2,1,0:T(8,128)} %deal.1), calls=%async_computation | async-start | bytes 524288 | tf_op jit(solution)/shard_map/all_to_all | solution.py:293
  9.1 0.1 stack.28.where_ref
  9.2 0.7 %copy-done.2 = s32[64,7]{0,1:T(8,128)S(1)} copy-done((s32[64,7]{0,1:T(8,128)S(1)}, s32[64,7]{0,1:T(8,128)}, u32[]{:S(2)}) %copy-start.2) | copy-done | bytes 1816
  9.9 3.4 %blocks.1 = (bf16[8,128,448]{2,1,0:T(8,128)(2,1)S(1)}, bf16[8,128,448]{2,1,0:T(8,128)(2,1)S(1)}, f32[264,448]{1,0:T(8,128)}) custom-call(s32[5]{0:T(128)S(1)} %stack.28.where_ref, s32[7,64]{1,0:T(8,128)S(1)} %bitcast.14, f32[64,64,448]{2,1,0:T(8,128)} %blocks_ref.1), custom_call_target="tpu_custom_call" | custom-call | tf_op jit(solution)/shard_map/blocks/pallas_call | solution.py:336
  13.3 0.7 %collective-permute-start = (f32[264,448]{1,0:T(8,128)}, f32[264,448]{1,0:T(8,128)S(1)}, u32[]{:S(2)}, u32[]{:S(2)}) collective-permute-start(f32[264,448]{1,0:T(8,128)} %get-tuple-element.8), channel_id=1, source_target_pairs={{4,5},{5,4},{1,2},{2,1},{6,7},{7,6}} | collective-permute-start | bytes 1419272 | tf_op jit(solution)/shard_map/ppermute | solution.py:353
  14.0 3.7 %all-to-all-done.xf_ref = f32[8,2,8,512]{3,2,1,0:T(8,128)S(1)} async-done(((f32[8,2,8,512]{3,2,1,0:T(8,128)}), f32[8,2,8,512]{3,2,1,0:T(8,128)S(1)}, u32[]{:S(2)}, u32[]{:S(2)}) %all-to-all-start) | async-done | bytes 262176 | tf_op jit(solution)/shard_map/all_to_all | solution.py:293
  17.8 1.1 %collective-permute-start.1 = (f32[64,256]{1,0:T(8,128)S(1)}, f32[64,256]{1,0:T(8,128)S(1)}, u32[]{:S(2)}, u32[]{:S(2)}) collective-permute-start(f32[64,256]{1,0:T(8,128)S(1)} %get-tuple-element.12), channel_id=1, source_target_pairs={{0,8},{8,0},{16,24},{24,16},{28,20},{20,28},{12,4},{4,12},{5,13},{... | collective-permute-start | bytes 196616 | tf_op jit(solution)/shard_map/ppermute | solution.py:304
  18.8 0.7 %collective-permute-start.2 = (f32[64,256]{1,0:T(8,128)S(1)}, f32[64,256]{1,0:T(8,128)S(1)}, u32[]{:S(2)}, u32[]{:S(2)}) collective-permute-start(f32[64,256]{1,0:T(8,128)S(1)} %get-tuple-element.11), channel_id=1, source_target_pairs={{8,16},{16,8},{24,28},{28,24},{20,12},{12,20},{4,5},{5,4},{13,21},... | collective-permute-start | bytes 196616 | tf_op jit(solution)/shard_map/ppermute | solution.py:305
  19.5 2.6 %collective-permute-done.1.one_ref = f32[64,256]{1,0:T(8,128)S(1)} collective-permute-done((f32[64,256]{1,0:T(8,128)S(1)}, f32[64,256]{1,0:T(8,128)S(1)}, u32[]{:S(2)}, u32[]{:S(2)}) %collective-permute-start.1) | collective-permute-done | bytes 65568 | tf_op jit(solution)/shard_map/ppermute | solution.py:304
  22.1 0.0 collective-permute-done.2.two_ref
  22.1 1.4 %residual.1.r_ref = f32[72,512]{1,0:T(8,128)S(1)} custom-call(s32[5]{0:T(128)S(1)} %stack.28.where_ref, s32[7,64]{1,0:T(8,128)S(1)} %bitcast.15, bf16[8,128,448]{2,1,0:T(8,128)(2,1)S(1)} %get-tuple-element.9.a_ref, f32[8,2,8,512]{3,2,1,0:T(8,128)S(1)} %all-to-all-done.xf_ref, f32[64,256]{1,0:T(8,128)S(1)} %collective-permute-done.1.one_ref, ...), custom_call_target="tpu_custom_call" | custom-call | tf_op jit(solution)/shard_map/residual/pallas_call | solution.py:396
  23.5 4.0 %collective-permute-start.3 = (f32[72,512]{1,0:T(8,128)S(1)}, f32[72,512]{1,0:T(8,128)S(1)}, u32[]{:S(2)}, u32[]{:S(2)}) collective-permute-start(f32[72,512]{1,0:T(8,128)S(1)} %residual.1.r_ref), channel_id=1, source_target_pairs={{0,8},{8,0},{16,24},{24,16},{28,20},{20,28},{12,4},{4,12},{5,13},{... | collective-permute-start | bytes 442376 | tf_op jit(solution)/shard_map/ppermute | solution.py:304
  27.5 0.7 %collective-permute-start.4 = (f32[72,512]{1,0:T(8,128)S(1)}, f32[72,512]{1,0:T(8,128)S(1)}, u32[]{:S(2)}, u32[]{:S(2)}) collective-permute-start(f32[72,512]{1,0:T(8,128)S(1)} %residual.1.r_ref), channel_id=1, source_target_pairs={{8,16},{16,8},{24,28},{28,24},{20,12},{12,20},{4,5},{5,4},{13,21},... | collective-permute-start | bytes 442376 | tf_op jit(solution)/shard_map/ppermute | solution.py:305
  28.1 0.0 collective-permute-done.halo_ref
  28.1 0.5 %fusion = s32[28]{0:T(128)} fusion(f32[264,448]{1,0:T(8,128)S(1)} %collective-permute-done.halo_ref), kind=kLoop, calls=%fused_computation.5 | loop fusion | flops 28 | bytes 224 | tf_op jit(solution)/shard_map/convert_element_type | solution.py:354
  28.7 0.7 %convert_element_type.10 = s32[7,4]{1,0:T(8,128)S(1)} reshape(s32[28]{0:T(128)} %fusion) | data formatting | bytes 224 | tf_op jit(solution)/shard_map/convert_element_type | solution.py:354
  29.4 0.6 %patch.1.an_ref = bf16[8,128,448]{2,1,0:T(8,128)(2,1)S(1)} custom-call(s32[5]{0:T(128)S(1)} %stack.28.where_ref, bf16[8,128,448]{2,1,0:T(8,128)(2,1)S(1)} %get-tuple-element.10.old_ref, f32[264,448]{1,0:T(8,128)S(1)} %collective-permute-done.halo_ref), custom_call_target="tpu_custom_call", output_to_operand_aliasing={{}: (1, {})} | custom-call | tf_op jit(solution)/shard_map/patch/pallas_call | solution.py:356
  30.0 0.1 pad_add_fusion.near_ref
  30.1 1.9 %collective-permute-done.3.one_ref = f32[72,512]{1,0:T(8,128)S(1)} collective-permute-done((f32[72,512]{1,0:T(8,128)S(1)}, f32[72,512]{1,0:T(8,128)S(1)}, u32[]{:S(2)}, u32[]{:S(2)}) %collective-permute-start.3) | collective-permute-done | bytes 147488 | tf_op jit(solution)/shard_map/ppermute | solution.py:304
  32.0 0.0 collective-permute-done.4.two_ref
  32.0 2.9 %sweeps.1 = f32[64,512]{1,0:T(8,128)S(1)} custom-call(s32[5]{0:T(128)S(1)} %stack.28.where_ref, s32[7,64]{1,0:T(8,128)S(1)} %bitcast.16, s32[7,8]{1,0:T(8,128)S(1)} %pad_add_fusion.near_ref, bf16[8,128,448]{2,1,0:T(8,128)(2,1)S(1)} %get-tuple-element.9.a_ref, bf16[8,128,448]{2,1,0:T(8,128)(2,1)S(1)} %patch.1.an_ref, ...), custom_call_target="tpu_custom_call" | custom-call | tf_op jit(solution)/shard_map/sweeps/pallas_call | solution.py:408
  34.9 12.8 %all_to_all.10 = f32[8,8,512]{2,1,0:T(8,128)S(1)} all-to-all(f32[8,8,512]{2,1,0:T(8,128)S(1)} %bitcast.13), channel_id=1, replica_groups={{0,8,16,24,28,20,12,4},{5,13,21,29,25,17,9,1},{2,10,18,26,30,22,14,6},{..., dimensions={0} | all-to-all | bytes 262144 | tf_op jit(solution)/shard_map/all_to_all | solution.py:293
  47.7 0.7 %copy.13 = f32[8,4096]{1,0:T(8,128)} copy(f32[8,4096]{1,0:T(8,128)S(1)} %bitcast.19) | data formatting | bytes 262144
  (15 shorter events, 0.0 us)
Async XLA Ops:
  0.0 32.0 %copy-start = (bf16[2,128,256]{2,1,0:T(8,128)(2,1)S(1)}, bf16[2,128,256]{2,1,0:T(8,128)(2,1)}, u32[]{:S(2)}) copy-start(bf16[2,128,256]{2,1,0:T(8,128)(2,1)} %constant.57.clone.fwd_ref) | copy-start | bytes 393220
  0.0 32.0 %copy-start.1 = (bf16[2,64,256]{2,1,0:T(8,128)(2,1)S(1)}, bf16[2,64,256]{2,1,0:T(8,128)(2,1)}, u32[]{:S(2)}) copy-start(bf16[2,64,256]{2,1,0:T(8,128)(2,1)} %constant.58.clone.back_ref) | copy-start | bytes 196612
  0.0 32.0 %copy-start.6 = (f32[2,128]{1,0:T(2,128)S(1)}, f32[2,128]{1,0:T(2,128)}, u32[]{:S(2)}) copy-start(f32[2,128]{1,0:T(2,128)} %constant.59.clone.lam_ref) | copy-start | bytes 3076
  0.0 22.1 %copy-start.3 = (s32[64,7]{0,1:T(8,128)S(1)}, s32[64,7]{0,1:T(8,128)}, u32[]{:S(2)}) copy-start(s32[64,7]{0,1:T(8,128)} %param.13) | copy-start | bytes 5380
  0.0 22.1 %copy-start.4 = (f32[4096]{0:T(1024)S(1)}, f32[4096]{0:T(1024)}, u32[]{:S(2)}) copy-start(f32[4096]{0:T(1024)} %param.9) | copy-start | bytes 49156
  0.0 22.1 %copy-start.5 = (f32[4096]{0:T(1024)S(1)}, f32[4096]{0:T(1024)}, u32[]{:S(2)}) copy-start(f32[4096]{0:T(1024)} %param.14) | copy-start | bytes 49156
  1.8 15.9 %all-to-all-start = ((f32[8,2,8,512]{3,2,1,0:T(8,128)}), f32[8,2,8,512]{3,2,1,0:T(8,128)S(1)}, u32[]{:S(2)}, u32[]{:S(2)}) async-start(f32[8,2,8,512]{3,2,1,0:T(8,128)} %deal.1), calls=%async_computation | async-start | bytes 524288 | tf_op jit(solution)/shard_map/all_to_all | solution.py:293
  9.2 0.7 %copy-start.2 = (s32[64,7]{0,1:T(8,128)S(1)}, s32[64,7]{0,1:T(8,128)}, u32[]{:S(2)}) copy-start(s32[64,7]{0,1:T(8,128)} %param.13) | copy-start | bytes 5380
  13.3 14.8 %collective-permute-start = (f32[264,448]{1,0:T(8,128)}, f32[264,448]{1,0:T(8,128)S(1)}, u32[]{:S(2)}, u32[]{:S(2)}) collective-permute-start(f32[264,448]{1,0:T(8,128)} %get-tuple-element.8), channel_id=1, source_target_pairs={{4,5},{5,4},{1,2},{2,1},{6,7},{7,6}} | collective-permute-start | bytes 1419272 | tf_op jit(solution)/shard_map/ppermute | solution.py:353
  17.8 4.3 %collective-permute-start.1 = (f32[64,256]{1,0:T(8,128)S(1)}, f32[64,256]{1,0:T(8,128)S(1)}, u32[]{:S(2)}, u32[]{:S(2)}) collective-permute-start(f32[64,256]{1,0:T(8,128)S(1)} %get-tuple-element.12), channel_id=1, source_target_pairs={{0,8},{8,0},{16,24},{24,16},{28,20},{20,28},{12,4},{4,12},{5,13},{... | collective-permute-start | bytes 196616 | tf_op jit(solution)/shard_map/ppermute | solution.py:304
  18.8 3.3 %collective-permute-start.2 = (f32[64,256]{1,0:T(8,128)S(1)}, f32[64,256]{1,0:T(8,128)S(1)}, u32[]{:S(2)}, u32[]{:S(2)}) collective-permute-start(f32[64,256]{1,0:T(8,128)S(1)} %get-tuple-element.11), channel_id=1, source_target_pairs={{8,16},{16,8},{24,28},{28,24},{20,12},{12,20},{4,5},{5,4},{13,21},... | collective-permute-start | bytes 196616 | tf_op jit(solution)/shard_map/ppermute | solution.py:305
  23.5 8.5 %collective-permute-start.3 = (f32[72,512]{1,0:T(8,128)S(1)}, f32[72,512]{1,0:T(8,128)S(1)}, u32[]{:S(2)}, u32[]{:S(2)}) collective-permute-start(f32[72,512]{1,0:T(8,128)S(1)} %residual.1.r_ref), channel_id=1, source_target_pairs={{0,8},{8,0},{16,24},{24,16},{28,20},{20,28},{12,4},{4,12},{5,13},{... | collective-permute-start | bytes 442376 | tf_op jit(solution)/shard_map/ppermute | solution.py:304
  27.5 4.5 %collective-permute-start.4 = (f32[72,512]{1,0:T(8,128)S(1)}, f32[72,512]{1,0:T(8,128)S(1)}, u32[]{:S(2)}, u32[]{:S(2)}) collective-permute-start(f32[72,512]{1,0:T(8,128)S(1)} %residual.1.r_ref), channel_id=1, source_target_pairs={{8,16},{16,8},{24,28},{28,24},{20,12},{12,20},{4,5},{5,4},{13,21},... | collective-permute-start | bytes 442376 | tf_op jit(solution)/shard_map/ppermute | solution.py:305

commit v4 on v3

v4 whole, which is shorter than its diff:
```python
import functools
import math

import jax
import jax.numpy as jnp
import numpy as np
from jax import lax
from jax.experimental import pallas as pl
from jax.experimental.pallas import tpu as pltpu
from jax.sharding import PartitionSpec as P

GHOST = 4
CORNER_WEIGHT = 0.05
AXES = ("tm", "space")
F32 = jnp.float32
BF16 = jnp.bfloat16


def there_and_back(count):
    return list(range(0, count, 2)) + list(range(count - 1 - count % 2, 0, -2))


def split(value):
    high = value.astype(BF16)
    return high, (value - high.astype(F32)).astype(BF16)


def np_split(value):
    high = value.astype(np.float32).astype(BF16)
    return high, (value - high.astype(np.float64)).astype(np.float32).astype(BF16)


def tables(total, times):
    half = total // 2
    freq = np.arange(half)
    t = np.asarray(times)[:, None]
    angle = 2.0 * math.pi * ((t * freq[None]) % total) / total
    nyquist = np.where(t % 2 == 0, 1.0, -1.0)
    cos, sin = np.cos(angle), np.sin(angle)
    grow = CORNER_WEIGHT ** (t / total)

    def swapped(value):
        return np.roll(value, half, axis=1)

    forward = np.concatenate([cos, nyquist, -sin[:, 1:]], axis=1) * grow
    high, low = np_split(np.concatenate([forward, swapped(forward)], axis=1))
    forward = np.concatenate([high, low], axis=1)
    twice = np.where(freq == 0, 1.0, 2.0)[None]
    high, low = np_split(np.concatenate([twice * cos, nyquist, -2.0 * sin[:, 1:]], axis=1) / grow / total)
    back = np.concatenate([high, swapped(low)] * 2, axis=1)
    root = CORNER_WEIGHT ** (1.0 / total)
    theta = 2.0 * math.pi * freq / total
    lam_re = np.concatenate([1.0 - root * np.cos(theta), [1.0 + root], 1.0 - root * np.cos(theta[1:])])
    lam_im = np.concatenate([root * np.sin(theta), [0.0], -root * np.sin(theta[1:])])
    lam = np.stack([lam_re, lam_im])
    return np.concatenate([forward] * 2, axis=0), back, np.concatenate([lam, swapped(lam)], axis=1).astype(np.float32)


def place(lower_ref, upper_ref, at, value):
    half = value.shape[1] // 2
    turned = pltpu.roll(value, half, 1)
    low = lax.broadcasted_iota(jnp.int32, value.shape, 1) < half
    for i, (first, second) in enumerate(((value, turned), (turned, value))):
        for ref, part in ((lower_ref, jnp.where(low, first, 0.0)), (upper_ref, jnp.where(low, 0.0, second))):
            ref[at + i] = jnp.concatenate(split(part), axis=0)


def couple(block, at, lower_ref, upper_ref):
    size, width = block.shape
    tiles = [lower_ref[at[n]] + upper_ref[at[n + 1]] for n in range(0, len(at) - 1, 2)]
    if len(at) % 2:
        tiles.append(lower_ref[at[-1]])
    picked = jnp.concatenate(tiles, axis=1)[:, :width]
    out = lax.dot_general(
        picked, jnp.concatenate(split(block), axis=0), (((1,), (1,)), ((), ())), preferred_element_type=F32
    )
    steps = out.shape[0] // 2
    out = out[:steps] + out[steps:]
    return out + pltpu.roll(out, size, 1)


def couple_rows(blocks_ref, origin, cols_ref, base, rows, lower_ref, upper_ref, put):
    slots = cols_ref.shape[0]
    size = blocks_ref.shape[1]
    for b in rows:
        pair = [
            couple(blocks_ref[i - origin], [cols_ref[n, i] - base for n in range(slots)], lower_ref, upper_ref)
            for i in (b, b + 1)
        ]
        low = lax.broadcasted_iota(jnp.int32, pair[0].shape, 1) < size
        put(b // 2, jnp.where(low, pair[0], pair[1]))


def sides_kernel(where_ref, x_ref, blocks_ref, one_ref, two_ref):
    even = where_ref[6] == 1
    extent = one_ref.shape[1]
    low, high = x_ref[:, :extent], x_ref[:, x_ref.shape[1] - extent :]
    one_ref[...] = jnp.where(even, high, low)
    two_ref[...] = jnp.where(even, low, high)


def inner_kernel(where_ref, cols_ref, x_ref, blocks_ref, out_ref, lower_ref, upper_ref):
    block_rows = blocks_ref.shape[0]

    def put(i, value):
        out_ref[:, i * 128 : (i + 1) * 128] = value

    for b in range(0, block_rows, 2):
        place(lower_ref, upper_ref, b, x_ref[:, b * 64 : b * 64 + 128])
    rows = range(GHOST, block_rows - GHOST, 2)
    couple_rows(blocks_ref, 0, cols_ref, where_ref[5], rows, lower_ref, upper_ref, put)


def outer_kernel(
    where_ref, cols_ref, x_ref, f_ref, blocks_ref, inner_ref, one_ref, two_ref, start_ref, kd_ref, out_ref, rim_ref,
    lower_ref, upper_ref, edge_ref,
):
    block_rows = cols_ref.shape[1]
    steps = x_ref.shape[0]
    peers, height, _ = out_ref.shape
    tall = x_ref.shape[1] // peers // 128
    even, opening = where_ref[6] == 1, where_ref[7] == 1
    for i in range(0, GHOST, 2):
        lanes = slice(i * 64, i * 64 + 128)
        first, second = one_ref[:, lanes], two_ref[:, lanes]
        place(lower_ref, upper_ref, i, jnp.where(even, second, first))
        place(lower_ref, upper_ref, GHOST + block_rows + i, jnp.where(even, first, second))
    ends = list(range(0, 2 * GHOST, 2)) + list(range(block_rows - 2 * GHOST, block_rows, 2))
    for b in ends:
        place(lower_ref, upper_ref, GHOST + b, x_ref[:, b * 64 : b * 64 + 128])

    def put(i, value):
        edge_ref[i] = value

    outer = [b for b in ends if b < GHOST or b >= block_rows - GHOST]
    couple_rows(blocks_ref, 0, cols_ref, where_ref[5] - GHOST, outer, lower_ref, upper_ref, put)
    for i in range(x_ref.shape[1] // 128):
        lanes = slice(i * 128, (i + 1) * 128)
        now = x_ref[:, lanes]
        coupled = edge_ref[i] if 2 * i in outer else inner_ref[:, lanes]
        kd = kd_ref[i : i + 1, :]
        before = jnp.where(opening, start_ref[i : i + 1, :], 0.0)
        previous = jnp.concatenate([before, now[: steps - 1]], axis=0)
        p, j = i // tall, i % tall
        out_ref[p, j * steps : (j + 1) * steps, :] = f_ref[:, lanes] + previous - (1.0 + kd) * now - coupled
        out_ref[p, steps * tall + j : steps * tall + j + 1, :] = now[steps - 1 :]
        out_ref[p, (steps + 1) * tall + j : (steps + 1) * tall + j + 1, :] = kd
    used = (steps + 2) * tall
    if used < height:
        out_ref[:, used:, :] = jnp.zeros((peers, height - used, 128), F32)

    lowest = where_ref[0] == 0
    _, size, width = blocks_ref.shape
    slots = width // size
    lane = lax.broadcasted_iota(jnp.int32, (8, width), 1)
    found = jnp.zeros((8, width), jnp.int32)
    for b in range(GHOST):
        last = block_rows - GHOST + b
        rim_ref[b * size : (b + 1) * size, :] = jnp.where(lowest, blocks_ref[b], blocks_ref[last])
        for n in range(slots):
            found = jnp.where(lane == n * GHOST + b, cols_ref[n, jnp.where(lowest, b, last)], found)
    rim_ref[GHOST * size :, :] = found.astype(F32)


def blocks_kernel(where_ref, blocks_ref, rim_ref, own_ref, near_ref, buffer, sems):
    count, size, _ = buffer.shape
    chunk = count - 2 * GHOST
    block_rows = blocks_ref.shape[0]
    spot = where_ref[0]
    rows = list(range(GHOST, GHOST + chunk)) + list(range(GHOST)) + list(range(GHOST + chunk, count))
    copies = {}
    for b in rows:
        row = jnp.clip(spot * chunk + b - GHOST, 0, block_rows - 1)
        copies[b] = pltpu.make_async_copy(blocks_ref.at[row], buffer.at[b], sems.at[b])
        copies[b].start()
    for b in rows:
        copies[b].wait()
        value = buffer[b]
        if GHOST <= b < GHOST + chunk:
            ref, at = own_ref, b - GHOST
        else:
            ref, at = near_ref, b if b < GHOST else b - chunk
            row = spot * chunk + b - GHOST
            if rim_ref.shape[0] > GHOST * size + 8:
                at_rim = jnp.where(row < 0, row + GHOST, GHOST + row - block_rows)
            else:
                at_rim = jnp.where(row < 0, row + GHOST, row - block_rows)
            outside = (row < 0) | (row >= block_rows)
            at_rim = pl.multiple_of(jnp.where(outside, at_rim, 0) * size, size)
            value = jnp.where(outside, rim_ref[pl.ds(at_rim, size), :], value)
        high, low = split(value)
        ref[at, :size] = high
        ref[at, size:] = low


def product(a, at, v_ref, size):
    picked = jnp.concatenate([v_ref[pl.ds(pl.multiple_of(row, size), size), :] for row in at], axis=0)
    out = jnp.dot(a, picked, preferred_element_type=F32)
    out = out[:size] + out[size:]
    half = out.shape[1] // 2
    return out[:, :half] + out[:, half:]


def store_split(ref, at, value):
    high, low = split(value)
    rows, channels = value.shape
    half = ref.shape[1] // 2
    ref[at : at + rows, :channels] = high
    ref[at : at + rows, half : half + channels] = low


def gather_chunk(pick, crossed, flip, lasts, dims):
    size, slots, chunk, total, steps = dims
    tall = chunk * size // 128
    count = total // steps
    parts = []
    for j in range(count):
        last = jnp.where(flip == 1, lasts[1][j], lasts[0][j])
        at = jnp.maximum(last, 0)
        held = pick(jnp.where(crossed, count - 1 - j, j))
        other = pick(jnp.where(crossed, count - 1 - at, at))
        wide = [held[i * steps : (i + 1) * steps] for i in range(tall)]
        before = [other[steps * tall + i : steps * tall + i + 1] for i in range(tall)]
        wide, before = jnp.concatenate(wide, axis=1), jnp.concatenate(before, axis=1)
        opens = lax.broadcasted_iota(jnp.int32, wide.shape, 0) == 0
        parts.append(wide + jnp.where(opens & (last >= 0), before, 0.0))
    kd = jnp.concatenate([held[(steps + 1) * tall + i : (steps + 1) * tall + i + 1] for i in range(tall)], axis=1)
    return jnp.concatenate(parts, axis=0), kd


def sweeps_kernel(
    dims, lasts, where_ref, cols_ref, near_ref, a_ref, an_ref, r_ref, one_ref, two_ref, fwd_ref, back_ref, lam_ref, out_ref,
    s_ref, cr_ref, ci_ref, v0_ref, v1_ref, y_ref,
):
    size, slots, chunk, total, steps = dims
    rows = chunk * size
    wide = 2 * GHOST * size
    spot, flip, base, even = where_ref[0], where_ref[1], where_ref[2], where_ref[3] == 1
    count = total // steps
    block_rows = cols_ref.shape[1]
    fwd = fwd_ref[flip]

    def forward(at, value):
        high, low = split(value)
        stacked = jnp.concatenate([high, low], axis=0)
        out = lax.dot_general(stacked, fwd, (((0,), (0,)), ((), ())), preferred_element_type=F32)
        s_ref[at : at + value.shape[1], :] = out[:, : 2 * total] + out[:, 2 * total :]

    def near(first_ref, second_ref, hop):
        return lambda at: jnp.where(even, second_ref[hop, at], first_ref[hop, at])

    hops = one_ref.shape[0]
    chunks = [(near(one_ref, two_ref, h), spot < hops - h) for h in range(hops)]
    chunks += [(lambda at: r_ref[at], False)]
    chunks += [(near(two_ref, one_ref, h), spot >= count - 1 - h) for h in range(hops)]
    kds = []
    for i, (pick, crossed) in enumerate(chunks):
        residual, kd = gather_chunk(pick, crossed, flip, lasts, dims)
        forward(i * rows, residual)
        kds.append(kd)
    kd = jnp.concatenate(kds, axis=1)
    kd = jnp.broadcast_to(kd, (2 * total, kd.shape[1])).T
    diag = kd + lam_ref[0:1, :]
    imag = lam_ref[1:2, :]
    inverse = 1.0 / (diag * diag + imag * imag)
    cr_ref[...] = diag * inverse
    ci_ref[...] = imag * inverse

    def divide(value, at):
        span = slice(at, at + value.shape[0])
        return value * cr_ref[span, :] + pltpu.roll(value, total, 1) * ci_ref[span, :]

    def column(n, b):
        row = spot * chunk + b
        found = cols_ref[n, jnp.clip(row, 0, block_rows - 1)]
        if b < 0:
            found = jnp.where(row < 0, near_ref[n, jnp.maximum(row + GHOST, 0)], found)
        if b >= chunk:
            found = jnp.where(row >= block_rows, near_ref[n, GHOST + jnp.maximum(row - block_rows, 0)], found)
        return jnp.clip(found - base, -2 * GHOST, chunk + 2 * GHOST - 1)

    store_split(v0_ref, 0, divide(s_ref[...], 0))
    for b in range(-GHOST, chunk + GHOST):
        at = (b + 2 * GHOST) * size
        a = a_ref[b] if 0 <= b < chunk else an_ref[b + GHOST if b < 0 else b - chunk + GHOST]
        coupled = product(a, [(column(n, b) + 2 * GHOST) * size for n in range(slots)], v0_ref, size)
        store_split(v1_ref, at - GHOST * size, divide(s_ref[at : at + size, :] - coupled, at))
    for b in range(chunk):
        at = (b + 2 * GHOST) * size
        coupled = product(a_ref[b], [(column(n, b) + GHOST) * size for n in range(slots)], v1_ref, size)
        store_split(y_ref, b * size, divide(s_ref[at : at + size, :] - coupled, at))
    change = lax.dot_general(back_ref[flip], y_ref[...], (((1,), (1,)), ((), ())), preferred_element_type=F32)
    out_ref[...] = change


def vmem(count):
    return [pl.BlockSpec(memory_space=pltpu.VMEM)] * count


def smem(count):
    return [pl.BlockSpec(memory_space=pltpu.SMEM)] * count


def cost(microseconds):
    return pl.CostEstimate(flops=0, transcendentals=0, bytes_accessed=3_000_000 * microseconds)


PARAMS = pltpu.CompilerParams(vmem_limit_bytes=16 * 1024 * 1024)
BLOCKS_PARAMS = pltpu.CompilerParams(vmem_limit_bytes=48 * 1024 * 1024)


def local(start_state, forcing, iterate, blocks, columns, kdiag):
    steps, rows_dev = iterate.shape
    block_rows, size, width = blocks.shape
    slots = width // size
    n_tm, n_space = lax.axis_size("tm"), lax.axis_size("space")
    total = steps * n_tm
    chunk = block_rows // n_tm
    rows = chunk * size
    edge = GHOST * size
    wide = 2 * edge
    dims = (size, slots, chunk, total, steps)
    order = there_and_back(n_tm)

    tm_index, space_index = lax.axis_index("tm"), lax.axis_index("space")
    flipped = space_index % 2 == 1
    spot = jnp.where(tm_index % 2 == 0, tm_index // 2, n_tm - 1 - tm_index // 2)
    spot = jnp.where(flipped, n_tm - 1 - spot, spot)
    even = (space_index * n_tm + spot) % 2 == 0

    groups, ring = [], []
    for s in range(n_space):
        members = [t * n_space + s for t in (order if s % 2 == 0 else order[::-1])]
        groups.append(tuple(members))
        ring += members
    groups = tuple(groups)
    count = len(ring)

    def deal(value):
        return lax.all_to_all(value, AXES, 0, 0, axis_index_groups=groups, tiled=True)

    def ring_pairs(first):
        pairs = []
        for i in range(first, count - 1, 2):
            pairs += [(ring[i], ring[i + 1]), (ring[i + 1], ring[i])]
        return pairs

    def neighbours(value, hops):
        if hops == 1:
            return [lax.ppermute(value, AXES, ring_pairs(first))[None] for first in (0, 1)]
        left, right = [], []
        for hop in range(1, hops + 1):
            up = [(ring[i], ring[i + hop]) for i in range(count - hop)]
            left.insert(0, lax.ppermute(value, AXES, up))
            right.append(lax.ppermute(value, AXES, [(j, i) for i, j in up]))
        return jnp.stack(left), jnp.stack(right)

    times = [[t * steps + j for t in members for j in range(steps)] for members in (order, order[::-1])]
    made = [tables(total, at) for at in times]
    fwd = np.stack([made[0][0], made[1][0]])
    back = np.stack([made[0][1], made[1][1]])
    lasts = [[at.index(at[j] - 1) // steps if at[j] else -1 for j in range(0, total, steps)] for at in times]
    base = space_index * block_rows + spot * chunk
    hops = wide // rows
    here = [spot, flipped, base, even & (hops == 1), spot, space_index * block_rows, space_index % 2 == 0, tm_index == 0]
    where = jnp.stack([jnp.asarray(value, jnp.int32) for value in here])
    columns = columns.T

    given = pl.pallas_call(
        sides_kernel,
        in_specs=smem(1) + vmem(1) + [pl.BlockSpec(memory_space=pl.ANY)],
        out_specs=vmem(2),
        out_shape=[jax.ShapeDtypeStruct((steps, edge), F32)] * 2,
        compiler_params=BLOCKS_PARAMS,
        name="sides",
    )(where, iterate, blocks)
    sides = []
    for first in (0, 1):
        pairs = [(s, s + 1) for s in range(first, n_space - 1, 2)]
        sides.append(lax.ppermute(given[first], "space", pairs + [(j, i) for i, j in pairs]))
    inner = pl.pallas_call(
        inner_kernel,
        in_specs=smem(2) + vmem(2),
        out_specs=vmem(1)[0],
        out_shape=jax.ShapeDtypeStruct((steps, rows_dev), F32),
        scratch_shapes=[pltpu.VMEM((block_rows, 2 * steps, 2 * size), BF16)] * 2,
        compiler_params=PARAMS,
        name="inner",
    )(where, columns, iterate, blocks)
    tall = rows // 128
    height = -(-(steps + 2) * tall // 8) * 8
    residual, rim = pl.pallas_call(
        outer_kernel,
        in_specs=smem(2) + vmem(8),
        out_specs=vmem(2),
        out_shape=[
            jax.ShapeDtypeStruct((n_tm, height, 128), F32),
            jax.ShapeDtypeStruct((edge + 8, width), F32),
        ],
        scratch_shapes=[pltpu.VMEM((block_rows + 2 * GHOST, 2 * steps, 2 * size), BF16)] * 2
        + [pltpu.VMEM((block_rows // 2, steps, 128), F32)],
        compiler_params=PARAMS,
        cost_estimate=cost(1),
        name="outer",
    )(where, columns, iterate, forcing, blocks, inner, *sides, start_state.reshape(-1, 128), kdiag.reshape(-1, 128))
    residual = deal(residual)

    def rim_columns(value):
        return value[edge, : GHOST * slots].reshape(slots, GHOST).astype(jnp.int32)

    if chunk >= 2 * GHOST and n_tm > 1:
        pairs = []
        for s in range(n_space - 1):
            i, j = ring[(s + 1) * n_tm - 1], ring[(s + 1) * n_tm]
            pairs += [(i, j), (j, i)]
        rim = lax.ppermute(rim, AXES, pairs)
        columns_halo = jnp.concatenate([rim_columns(rim)] * 2, axis=1)
    else:
        up = [(s, s + 1) for s in range(n_space - 1)]
        down = [(j, i) for i, j in up]
        rim = [
            lax.ppermute(value, "space", pairs)
            for value, pairs in ((blocks[-GHOST:], up), (columns[:, -GHOST:], up), (blocks[:GHOST], down), (columns[:, :GHOST], down))
        ]
        columns_halo = jnp.concatenate(rim[1::2], axis=1)
        rim = jnp.concatenate([value.reshape(edge, width) for value in rim[::2]], axis=0)
    a_own, a_near = pl.pallas_call(
        blocks_kernel,
        in_specs=smem(1) + [pl.BlockSpec(memory_space=pl.ANY)] + vmem(1),
        out_specs=vmem(2),
        out_shape=[jax.ShapeDtypeStruct((n, 2 * size, width), BF16) for n in (chunk, 2 * GHOST)],
        scratch_shapes=[
            pltpu.VMEM((chunk + 2 * GHOST, size, width), F32),
            pltpu.SemaphoreType.DMA((chunk + 2 * GHOST,)),
        ],
        compiler_params=BLOCKS_PARAMS,
        cost_estimate=cost(2),
        name="blocks",
    )(where, blocks, rim)

    one, two = neighbours(residual, hops)
    span = rows + 2 * wide
    result = pl.pallas_call(
        functools.partial(sweeps_kernel, dims, lasts),
        in_specs=smem(3) + vmem(8),
        out_specs=vmem(1)[0],
        out_shape=jax.ShapeDtypeStruct((total, rows), F32),
        scratch_shapes=[pltpu.VMEM((span, 2 * total), F32)] * 3
        + [pltpu.VMEM((height, 4 * total), BF16) for height in (span, span - wide, rows)],
        compiler_params=PARAMS,
        cost_estimate=cost(3),
        name="sweeps",
    )(where, columns, columns_halo, a_own, a_near, residual, one, two, fwd, back, made[0][2])

    returned = deal(result.reshape(n_tm, steps, rows))
    return iterate + returned.transpose(1, 0, 2).reshape(steps, rows_dev)


def solution(mesh):
    placed = (
        P("space"),
        P("tm", "space"),
        P("tm", "space"),
        P("space", None, None),
        P("space", None),
        P("space"),
    )
    return jax.shard_map(local, mesh=mesh, in_specs=placed, out_specs=P("tm", "space"), check_vma=False)
```

time: 48.8 us -> 47.5 us (0.973)
  blocking collectives: 12.8 us -> 28.9 us
  starting transfers between devices: 14.4 us -> 3.52 us
  waiting for transfers between devices: 8.2 us -> 1.18 us
    all_to_all x1 -> x2, blocking collectives: 12.8 us -> 28.9 us  [deal(): lax.all_to_all(value, AXES, 0, 0, axis_index_groups=groups, tiled=True)]
    all_to_all x1 -> x0, starting transfers between devices: 7.32 us -> none  [deal(): lax.all_to_all(value, AXES, 0, 0, axis_index_groups=groups, tiled=True)]
    all_to_all x1 -> x0, waiting for transfers between devices: 3.73 us -> none  [deal(): lax.all_to_all(value, AXES, 0, 0, axis_index_groups=groups, tiled=True)]
    ppermute x5, starting transfers between devices: 7.05 us -> 3.52 us  [the longest x2 1.4 us: neighbours(): lax.ppermute(value, AXES, ring_pairs(first))[None]]
    ppermute x5, waiting for transfers between devices: 4.47 us -> 1.18 us  [the longest x2 1.16 us: neighbours(): lax.ppermute(value, AXES, ring_pairs(first))[None]]
    unnamed x15 -> x20, local copies, waits for them, and re-layouts: 1.36 us -> 2.44 us
    add x0 -> x1, other arithmetic: none -> 0.68 us  [local(): return iterate + returned.transpose(1, 0, 2).reshape(steps, rows_dev)]
    convert_element_type x1, local copies, waits for them, and re-layouts: 0.73 us -> 0.08 us  [rim_columns(): return value[edge, :GHOST * slots].reshape(slots, GHOST).astype(jnp.int32)]
  transfers between devices with their start and end apart: 6 -> 5, of which waited for: 3 -> 1; matrix products, arithmetic and copies ran while one was open for 3% -> 0% of each run, Pallas kernels for 11% -> 11%
where the time goes in v4:
time: 47.5 us; the launch traced here: 47.3 us
  blocking collectives  28.9 us (61%)
  Pallas kernels  10.1 us (21%)
  starting transfers between devices  3.52 us (7%)
  local copies, waits for them, and re-layouts  2.61 us (5%)
  waiting for transfers between devices  1.18 us (2%)
  other arithmetic  0.77 us (2%)
    all_to_all x2, blocking collectives, deal(): lax.all_to_all(value, AXES, 0, 0, axis_index_groups=groups, tiled=True)  28.9 us
    pallas_call x1, Pallas kernels, local(): pl.pallas_call(functools.partial(sweeps_kernel, dims, lasts), in_specs=sm...  3.03 us
    pallas_call x1, Pallas kernels, local(): pl.pallas_call(inner_kernel, in_specs=smem(2) + vmem(2), out_specs=vmem(1...  2.85 us
    pallas_call x1, Pallas kernels, local(): pl.pallas_call(blocks_kernel, in_specs=smem(1) + [pl.BlockSpec(memory_spa...  2.56 us
    unnamed x20, local copies, waits for them, and re-layouts  2.44 us
    ppermute x2, starting transfers between devices, neighbours(): lax.ppermute(value, AXES, ring_pairs(first))[None]  1.4 us
    ppermute x2, starting transfers between devices, local(): lax.ppermute(given[first], 'space', pairs + [(j, i) for i, j in pairs])  1.3 us
    ppermute x2, waiting for transfers between devices, neighbours(): lax.ppermute(value, AXES, ring_pairs(first))[None]  1.16 us
  transfers between devices with their start and end apart: 5, of which 1 were waited for; matrix products, arithmetic and copies ran while one was open for 0% of the time, Pallas kernels for 11%

profile of v4, /device:TPU:0, one launch (start us, length us, event | category | flops | bytes accessed | tf_op | source)
XLA Modules:
  0.0 47.3 jit_solution(16635565249843895650)
XLA Ops:
  0.0 0.1 stack.48.where_ref
  0.1 0.9 %copy-done.1 = f32[8,4096]{1,0:T(8,128)S(1)} copy-done((f32[8,4096]{1,0:T(8,128)S(1)}, f32[8,4096]{1,0:T(8,128)}, u32[]{:S(2)}) %copy-start.1) | copy-done | bytes 131096
  1.0 0.5 %sides.1 = (f32[8,256]{1,0:T(8,128)S(1)}, f32[8,256]{1,0:T(8,128)S(1)}) custom-call(s32[8]{0:T(128)S(1)} %stack.48.where_ref, f32[8,4096]{1,0:T(8,128)S(1)} %copy-done.1, f32[64,64,448]{2,1,0:T(8,128)} %blocks_ref.7), custom_call_target="tpu_custom_call" | custom-call | tf_op jit(solution)/shard_map/sides/pallas_call | solution.py:369
  1.6 0.5 %collective-permute-start = (f32[8,256]{1,0:T(8,128)S(1)}, f32[8,256]{1,0:T(8,128)S(1)}, u32[]{:S(2)}, u32[]{:S(2)}) collective-permute-start(f32[8,256]{1,0:T(8,128)S(1)} %get-tuple-element.11), channel_id=1, source_target_pairs={{0,1},{2,3},{1,0},{3,2},{4,5},{6,7},{5,4},{7,6},{8,9},{10,11},{9,8... | collective-permute-start | bytes 24584 | tf_op jit(solution)/shard_map/ppermute | solution.py:380
  2.1 0.8 %collective-permute-start.1 = (f32[8,256]{1,0:T(8,128)S(1)}, f32[8,256]{1,0:T(8,128)S(1)}, u32[]{:S(2)}, u32[]{:S(2)}) collective-permute-start(f32[8,256]{1,0:T(8,128)S(1)} %get-tuple-element.12), channel_id=1, source_target_pairs={{1,2},{2,1},{5,6},{6,5},{9,10},{10,9},{13,14},{14,13},{17,18},{18,... | collective-permute-start | bytes 24584 | tf_op jit(solution)/shard_map/ppermute | solution.py:380
  2.9 1.5 %copy-done = f32[64,64,448]{2,1,0:T(8,128)S(1)} copy-done((f32[64,64,448]{2,1,0:T(8,128)S(1)}, f32[64,64,448]{2,1,0:T(8,128)}, u32[]{:S(2)}) %copy-start) | copy-done | bytes 7340056
  4.4 2.8 %inner.1.inner_ref = f32[8,4096]{1,0:T(8,128)S(1)} custom-call(s32[8]{0:T(128)S(1)} %stack.48.where_ref, s32[7,64]{1,0:T(8,128)S(1)} %bitcast.19, f32[8,4096]{1,0:T(8,128)S(1)} %copy-done.1, f32[64,64,448]{2,1,0:T(8,128)S(1)} %copy-done), custom_call_target="tpu_custom_call" | custom-call | tf_op jit(solution)/shard_map/inner/pallas_call | solution.py:381
  7.2 0.0 collective-permute-done.1.two_ref
  7.3 0.0 copy-start.4
  7.3 0.0 copy-start.5
  7.3 0.0 copy-start.9
  7.3 1.2 %outer.1 = (f32[8,40,128]{2,1,0:T(8,128)S(1)}, f32[264,448]{1,0:T(8,128)S(1)}) custom-call(s32[8]{0:T(128)S(1)} %stack.48.where_ref, s32[7,64]{1,0:T(8,128)S(1)} %bitcast.20, f32[8,4096]{1,0:T(8,128)S(1)} %copy-done.1, f32[8,4096]{1,0:T(8,128)S(1)} %copy-done.3, f32[64,64,448]{2,1,0:T(8,128)S(1)} %copy-done, f32[8,4096]{1,0:T(8,128)S(1)} %inner.1.inner_ref, ...), custom_call_target="tpu_custom_call" | custom-call | bytes 3000000 | tf_op jit(solution)/shard_map/outer/pallas_call | solution.py:392
  8.5 0.8 %collective-permute-start.2 = (f32[264,448]{1,0:T(8,128)S(1)}, f32[264,448]{1,0:T(8,128)S(1)}, u32[]{:S(2)}, u32[]{:S(2)}) collective-permute-start(f32[264,448]{1,0:T(8,128)S(1)} %get-tuple-element.13), channel_id=1, source_target_pairs={{4,5},{5,4},{1,2},{2,1},{6,7},{7,6}} | collective-permute-start | bytes 1419272 | tf_op jit(solution)/shard_map/ppermute | solution.py:416
  9.3 15.1 %all_to_all.10.r_ref = f32[8,40,128]{2,1,0:T(8,128)S(1)} all-to-all(f32[8,40,128]{2,1,0:T(8,128)S(1)} %get-tuple-element.16), channel_id=1, replica_groups={{0,8,16,24,28,20,12,4},{5,13,21,29,25,17,9,1},{2,10,18,26,30,22,14,6},{..., dimensions={0} | all-to-all | bytes 327680 | tf_op jit(solution)/shard_map/all_to_all | solution.py:340
  24.4 0.7 %collective-permute-start.3 = (f32[8,40,128]{2,1,0:T(8,128)S(1)}, f32[8,40,128]{2,1,0:T(8,128)S(1)}, u32[]{:S(2)}, u32[]{:S(2)}) collective-permute-start(f32[8,40,128]{2,1,0:T(8,128)S(1)} %all_to_all.10.r_ref), channel_id=1, source_target_pairs={{0,8},{8,0},{16,24},{24,16},{28,20},{20,28},{12,4},{4,12},{5,13},{... | collective-permute-start | bytes 491528 | tf_op jit(solution)/shard_map/ppermute | solution.py:350
  25.1 0.7 %collective-permute-start.4 = (f32[8,40,128]{2,1,0:T(8,128)S(1)}, f32[8,40,128]{2,1,0:T(8,128)S(1)}, u32[]{:S(2)}, u32[]{:S(2)}) collective-permute-start(f32[8,40,128]{2,1,0:T(8,128)S(1)} %all_to_all.10.r_ref), channel_id=1, source_target_pairs={{8,16},{16,8},{24,28},{28,24},{20,12},{12,20},{4,5},{5,4},{13,21},... | collective-permute-start | bytes 491528 | tf_op jit(solution)/shard_map/ppermute | solution.py:350
  25.8 0.1 convert_element_type.11
  25.9 2.6 %blocks.1 = (bf16[8,128,448]{2,1,0:T(8,128)(2,1)S(1)}, bf16[8,128,448]{2,1,0:T(8,128)(2,1)S(1)}) custom-call(s32[8]{0:T(128)S(1)} %stack.48.where_ref, f32[64,64,448]{2,1,0:T(8,128)} %blocks_ref.7, f32[264,448]{1,0:T(8,128)S(1)} %collective-permute-done.2.rim_ref), custom_call_target="tpu_custom_call" | custom-call | bytes 6000000 | tf_op jit(solution)/shard_map/blocks/pallas_call | solution.py:427
  28.5 0.1 pad_add_fusion.near_ref
  28.6 1.2 %collective-permute-done.3 = f32[8,40,128]{2,1,0:T(8,128)S(1)} collective-permute-done((f32[8,40,128]{2,1,0:T(8,128)S(1)}, f32[8,40,128]{2,1,0:T(8,128)S(1)}, u32[]{:S(2)}, u32[]{:S(2)}) %collective-permute-start.3) | collective-permute-done | bytes 163872 | tf_op jit(solution)/shard_map/ppermute | solution.py:350
  29.7 0.0 collective-permute-done.4
  29.7 3.0 %sweeps.1 = f32[64,512]{1,0:T(8,128)S(1)} custom-call(s32[8]{0:T(128)S(1)} %stack.48.where_ref, s32[7,64]{1,0:T(8,128)S(1)} %bitcast.21, s32[7,8]{1,0:T(8,128)S(1)} %pad_add_fusion.near_ref, bf16[8,128,448]{2,1,0:T(8,128)(2,1)S(1)} %get-tuple-element.14.a_ref, bf16[8,128,448]{2,1,0:T(8,128)(2,1)S(1)} %get-tuple-element.15.an_ref, ...), custom_call_target="tpu_custom_call" | custom-call | bytes 9000000 | tf_op jit(solution)/shard_map/sweeps/pallas_call | solution.py:443
  32.8 13.8 %all_to_all.11 = f32[8,8,512]{2,1,0:T(8,128)S(1)} all-to-all(f32[8,8,512]{2,1,0:T(8,128)S(1)} %bitcast.16), channel_id=1, replica_groups={{0,8,16,24,28,20,12,4},{5,13,21,29,25,17,9,1},{2,10,18,26,30,22,14,6},{..., dimensions={0} | all-to-all | bytes 262144 | tf_op jit(solution)/shard_map/all_to_all | solution.py:340
  46.6 0.7 %add.26 = f32[8,4096]{1,0:T(8,128)} add(f32[8,4096]{1,0:T(8,128)S(1)} %copy-done.2, f32[8,4096]{1,0:T(8,128)S(1)} %bitcast.24) | non-fusion elementwise | flops 32768 | bytes 393216 | tf_op jit(solution)/shard_map/add | solution.py:456
  (18 shorter events, 0.1 us)
Async XLA Ops:
  0.0 2.9 %copy-start.6 = (s32[64,7]{0,1:T(8,128)S(1)}, s32[64,7]{0,1:T(8,128)}, u32[]{:S(2)}) copy-start(s32[64,7]{0,1:T(8,128)} %param.13) | copy-start | bytes 5380
  0.1 0.9 %copy-start.1 = (f32[8,4096]{1,0:T(8,128)S(1)}, f32[8,4096]{1,0:T(8,128)}, u32[]{:S(2)}) copy-start(f32[8,4096]{1,0:T(8,128)} %x_ref.5) | copy-start | bytes 393220
  1.0 3.4 %copy-start = (f32[64,64,448]{2,1,0:T(8,128)S(1)}, f32[64,64,448]{2,1,0:T(8,128)}, u32[]{:S(2)}) copy-start(f32[64,64,448]{2,1,0:T(8,128)} %blocks_ref.7) | copy-start | bytes 22020100
  1.0 6.3 %copy-start.3 = (f32[8,4096]{1,0:T(8,128)S(1)}, f32[8,4096]{1,0:T(8,128)}, u32[]{:S(2)}) copy-start(f32[8,4096]{1,0:T(8,128)} %f_ref.1) | copy-start | bytes 393220
  1.0 6.3 %copy-start.7 = (f32[4096]{0:T(1024)S(1)}, f32[4096]{0:T(1024)}, u32[]{:S(2)}) copy-start(f32[4096]{0:T(1024)} %param.9) | copy-start | bytes 49156
  1.0 6.3 %copy-start.8 = (f32[4096]{0:T(1024)S(1)}, f32[4096]{0:T(1024)}, u32[]{:S(2)}) copy-start(f32[4096]{0:T(1024)} %param.14) | copy-start | bytes 49156
  1.6 5.7 %collective-permute-start = (f32[8,256]{1,0:T(8,128)S(1)}, f32[8,256]{1,0:T(8,128)S(1)}, u32[]{:S(2)}, u32[]{:S(2)}) collective-permute-start(f32[8,256]{1,0:T(8,128)S(1)} %get-tuple-element.11), channel_id=1, source_target_pairs={{0,1},{2,3},{1,0},{3,2},{4,5},{6,7},{5,4},{7,6},{8,9},{10,11},{9,8... | collective-permute-start | bytes 24584 | tf_op jit(solution)/shard_map/ppermute | solution.py:380
  2.1 5.2 %collective-permute-start.1 = (f32[8,256]{1,0:T(8,128)S(1)}, f32[8,256]{1,0:T(8,128)S(1)}, u32[]{:S(2)}, u32[]{:S(2)}) collective-permute-start(f32[8,256]{1,0:T(8,128)S(1)} %get-tuple-element.12), channel_id=1, source_target_pairs={{1,2},{2,1},{5,6},{6,5},{9,10},{10,9},{13,14},{14,13},{17,18},{18,... | collective-permute-start | bytes 24584 | tf_op jit(solution)/shard_map/ppermute | solution.py:380
  7.3 22.4 %copy-start.4 = (bf16[2,128,256]{2,1,0:T(8,128)(2,1)S(1)}, bf16[2,128,256]{2,1,0:T(8,128)(2,1)}, u32[]{:S(2)}) copy-start(bf16[2,128,256]{2,1,0:T(8,128)(2,1)} %constant.59.clone.fwd_ref) | copy-start | bytes 393220
  7.3 22.4 %copy-start.5 = (bf16[2,64,256]{2,1,0:T(8,128)(2,1)S(1)}, bf16[2,64,256]{2,1,0:T(8,128)(2,1)}, u32[]{:S(2)}) copy-start(bf16[2,64,256]{2,1,0:T(8,128)(2,1)} %constant.60.clone.back_ref) | copy-start | bytes 196612
  7.3 22.4 %copy-start.9 = (f32[2,128]{1,0:T(2,128)S(1)}, f32[2,128]{1,0:T(2,128)}, u32[]{:S(2)}) copy-start(f32[2,128]{1,0:T(2,128)} %constant.61.clone.lam_ref) | copy-start | bytes 3076
  8.5 38.1 %copy-start.2 = (f32[8,4096]{1,0:T(8,128)S(1)}, f32[8,4096]{1,0:T(8,128)}, u32[]{:S(2)}) copy-start(f32[8,4096]{1,0:T(8,128)} %x_ref.5) | copy-start | bytes 393220
  8.5 17.3 %collective-permute-start.2 = (f32[264,448]{1,0:T(8,128)S(1)}, f32[264,448]{1,0:T(8,128)S(1)}, u32[]{:S(2)}, u32[]{:S(2)}) collective-permute-start(f32[264,448]{1,0:T(8,128)S(1)} %get-tuple-element.13), channel_id=1, source_target_pairs={{4,5},{5,4},{1,2},{2,1},{6,7},{7,6}} | collective-permute-start | bytes 1419272 | tf_op jit(solution)/shard_map/ppermute | solution.py:416
  24.4 5.3 %collective-permute-start.3 = (f32[8,40,128]{2,1,0:T(8,128)S(1)}, f32[8,40,128]{2,1,0:T(8,128)S(1)}, u32[]{:S(2)}, u32[]{:S(2)}) collective-permute-start(f32[8,40,128]{2,1,0:T(8,128)S(1)} %all_to_all.10.r_ref), channel_id=1, source_target_pairs={{0,8},{8,0},{16,24},{24,16},{28,20},{20,28},{12,4},{4,12},{5,13},{... | collective-permute-start | bytes 491528 | tf_op jit(solution)/shard_map/ppermute | solution.py:350
  25.1 4.6 %collective-permute-start.4 = (f32[8,40,128]{2,1,0:T(8,128)S(1)}, f32[8,40,128]{2,1,0:T(8,128)S(1)}, u32[]{:S(2)}, u32[]{:S(2)}) collective-permute-start(f32[8,40,128]{2,1,0:T(8,128)S(1)} %all_to_all.10.r_ref), channel_id=1, source_target_pairs={{8,16},{16,8},{24,28},{28,24},{20,12},{12,20},{4,5},{5,4},{13,21},... | collective-permute-start | bytes 491528 | tf_op jit(solution)/shard_map/ppermute | solution.py:350

commit v5 on v4

--- a/solution.py
+++ b/solution.py
@@ -112,7 +112,7 @@
 
 
 def outer_kernel(
-    where_ref, cols_ref, x_ref, f_ref, blocks_ref, inner_ref, one_ref, two_ref, start_ref, kd_ref, out_ref, rim_ref,
+    where_ref, cols_ref, x_ref, f_ref, blocks_ref, inner_ref, two_ref, one_ref, start_ref, kd_ref, out_ref, rim_ref,
     lower_ref, upper_ref, edge_ref,
 ):
     block_rows = cols_ref.shape[1]
@@ -375,9 +375,9 @@
         name="sides",
     )(where, iterate, blocks)
     sides = []
-    for first in (0, 1):
+    for first in (1, 0):
         pairs = [(s, s + 1) for s in range(first, n_space - 1, 2)]
-        sides.append(lax.ppermute(given[first], "space", pairs + [(j, i) for i, j in pairs]))
+        sides.insert(0, lax.ppermute(given[first], "space", pairs + [(j, i) for i, j in pairs]))
     inner = pl.pallas_call(
         inner_kernel,
         in_specs=smem(2) + vmem(2),
@@ -402,7 +402,7 @@
         compiler_params=PARAMS,
         cost_estimate=cost(1),
         name="outer",
-    )(where, columns, iterate, forcing, blocks, inner, *sides, start_state.reshape(-1, 128), kdiag.reshape(-1, 128))
+    )(where, columns, iterate, forcing, blocks, inner, *sides[::-1], start_state.reshape(-1, 128), kdiag.reshape(-1, 128))
     residual = deal(residual)
 
     def rim_columns(value):

time: 47.5 us -> 47.2 us (level)
  starting transfers between devices: 3.52 us -> 6.9 us
  blocking collectives: 28.9 us -> 26 us
  local copies, waits for them, and re-layouts: 2.61 us -> 1.11 us
  waiting for transfers between devices: 1.18 us -> 1.8 us
    ppermute x2, starting transfers between devices: 1.3 us -> 5.29 us  [local(): lax.ppermute(given[first], 'space', pairs + [(j, i) for i, j in pairs])]
    all_to_all x2, blocking collectives: 28.9 us -> 26 us  [deal(): lax.all_to_all(value, AXES, 0, 0, axis_index_groups=groups, tiled=True)]
    unnamed x20, local copies, waits for them, and re-layouts: 2.44 us -> 0.95 us
    ppermute x2, starting transfers between devices: 1.4 us -> 0.78 us  [neighbours(): lax.ppermute(value, AXES, ring_pairs(first))[None]]
    ppermute x2, waiting for transfers between devices: 1.16 us -> 1.78 us  [neighbours(): lax.ppermute(value, AXES, ring_pairs(first))[None]]
  transfers between devices with their start and end apart: 5 -> 5, of which waited for: 1 -> 1; matrix products, arithmetic and copies ran while one was open for 0% -> 0% of each run, Pallas kernels for 11% -> 12%
where the time goes in v5:
time: 47.2 us; the launch traced here: 46.9 us
  blocking collectives  26 us (55%)
  Pallas kernels  10.1 us (21%)
  starting transfers between devices  6.9 us (15%)
  waiting for transfers between devices  1.8 us (4%)
  local copies, waits for them, and re-layouts  1.11 us (2%)
  other arithmetic  0.77 us (2%)
    all_to_all x2, blocking collectives, deal(): lax.all_to_all(value, AXES, 0, 0, axis_index_groups=groups, tiled=True)  26 us
    ppermute x2, starting transfers between devices, local(): lax.ppermute(given[first], 'space', pairs + [(j, i) for i, j in pairs])  5.29 us
    pallas_call x1, Pallas kernels, local(): pl.pallas_call(functools.partial(sweeps_kernel, dims, lasts), in_specs=sm...  3.02 us
    pallas_call x1, Pallas kernels, local(): pl.pallas_call(inner_kernel, in_specs=smem(2) + vmem(2), out_specs=vmem(1...  2.85 us
    pallas_call x1, Pallas kernels, local(): pl.pallas_call(blocks_kernel, in_specs=smem(1) + [pl.BlockSpec(memory_spa...  2.56 us
    ppermute x2, waiting for transfers between devices, neighbours(): lax.ppermute(value, AXES, ring_pairs(first))[None]  1.78 us
    pallas_call x1, Pallas kernels, local(): pl.pallas_call(outer_kernel, in_specs=smem(2) + vmem(8), out_specs=vmem(2...  1.16 us
    unnamed x20, local copies, waits for them, and re-layouts  0.95 us
  transfers between devices with their start and end apart: 5, of which 1 were waited for; matrix products, arithmetic and copies ran while one was open for 0% of the time, Pallas kernels for 12%

profile of v5, /device:TPU:0, one launch (start us, length us, event | category | flops | bytes accessed | tf_op | source)
XLA Modules:
  0.0 46.9 jit_solution(14692662015725599289)
XLA Ops:
  0.0 0.1 stack.48.where_ref
  0.1 0.9 %copy-done.1 = f32[8,4096]{1,0:T(8,128)S(1)} copy-done((f32[8,4096]{1,0:T(8,128)S(1)}, f32[8,4096]{1,0:T(8,128)}, u32[]{:S(2)}) %copy-start.1) | copy-done | bytes 131096
  1.0 0.5 %sides.1 = (f32[8,256]{1,0:T(8,128)S(1)}, f32[8,256]{1,0:T(8,128)S(1)}) custom-call(s32[8]{0:T(128)S(1)} %stack.48.where_ref, f32[8,4096]{1,0:T(8,128)S(1)} %copy-done.1, f32[64,64,448]{2,1,0:T(8,128)} %blocks_ref.7), custom_call_target="tpu_custom_call" | custom-call | tf_op jit(solution)/shard_map/sides/pallas_call | solution.py:369
  1.6 0.8 %collective-permute-start = (f32[8,256]{1,0:T(8,128)S(1)}, f32[8,256]{1,0:T(8,128)S(1)}, u32[]{:S(2)}, u32[]{:S(2)}) collective-permute-start(f32[8,256]{1,0:T(8,128)S(1)} %get-tuple-element.11), channel_id=1, source_target_pairs={{1,2},{2,1},{5,6},{6,5},{9,10},{10,9},{13,14},{14,13},{17,18},{18,... | collective-permute-start | bytes 24584 | tf_op jit(solution)/shard_map/ppermute | solution.py:380
  2.4 4.5 %collective-permute-start.1 = (f32[8,256]{1,0:T(8,128)S(1)}, f32[8,256]{1,0:T(8,128)S(1)}, u32[]{:S(2)}, u32[]{:S(2)}) collective-permute-start(f32[8,256]{1,0:T(8,128)S(1)} %get-tuple-element.12), channel_id=1, source_target_pairs={{0,1},{2,3},{1,0},{3,2},{4,5},{6,7},{5,4},{7,6},{8,9},{10,11},{9,8... | collective-permute-start | bytes 24584 | tf_op jit(solution)/shard_map/ppermute | solution.py:380
  6.9 2.9 %inner.1.inner_ref = f32[8,4096]{1,0:T(8,128)S(1)} custom-call(s32[8]{0:T(128)S(1)} %stack.48.where_ref, s32[7,64]{1,0:T(8,128)S(1)} %bitcast.19, f32[8,4096]{1,0:T(8,128)S(1)} %copy-done.1, f32[64,64,448]{2,1,0:T(8,128)S(1)} %copy-done), custom_call_target="tpu_custom_call" | custom-call | tf_op jit(solution)/shard_map/inner/pallas_call | solution.py:381
  9.7 0.0 collective-permute-done.1.one_ref
  9.8 0.0 copy-start.4
  9.8 0.0 copy-start.5
  9.8 0.0 copy-start.9
  9.8 1.2 %outer.1 = (f32[8,40,128]{2,1,0:T(8,128)S(1)}, f32[264,448]{1,0:T(8,128)S(1)}) custom-call(s32[8]{0:T(128)S(1)} %stack.48.where_ref, s32[7,64]{1,0:T(8,128)S(1)} %bitcast.20, f32[8,4096]{1,0:T(8,128)S(1)} %copy-done.1, f32[8,4096]{1,0:T(8,128)S(1)} %copy-done.3, f32[64,64,448]{2,1,0:T(8,128)S(1)} %copy-done, f32[8,4096]{1,0:T(8,128)S(1)} %inner.1.inner_ref, ...), custom_call_target="tpu_custom_call" | custom-call | bytes 3000000 | tf_op jit(solution)/shard_map/outer/pallas_call | solution.py:392
  11.0 0.8 %collective-permute-start.2 = (f32[264,448]{1,0:T(8,128)S(1)}, f32[264,448]{1,0:T(8,128)S(1)}, u32[]{:S(2)}, u32[]{:S(2)}) collective-permute-start(f32[264,448]{1,0:T(8,128)S(1)} %get-tuple-element.13), channel_id=1, source_target_pairs={{4,5},{5,4},{1,2},{2,1},{6,7},{7,6}} | collective-permute-start | bytes 1419272 | tf_op jit(solution)/shard_map/ppermute | solution.py:416
  11.8 13.4 %all_to_all.10.r_ref = f32[8,40,128]{2,1,0:T(8,128)S(1)} all-to-all(f32[8,40,128]{2,1,0:T(8,128)S(1)} %get-tuple-element.16), channel_id=1, replica_groups={{0,8,16,24,28,20,12,4},{5,13,21,29,25,17,9,1},{2,10,18,26,30,22,14,6},{..., dimensions={0} | all-to-all | bytes 327680 | tf_op jit(solution)/shard_map/all_to_all | solution.py:340
  25.2 0.1 collective-permute-start.3
  25.3 0.7 %collective-permute-start.4 = (f32[8,40,128]{2,1,0:T(8,128)S(1)}, f32[8,40,128]{2,1,0:T(8,128)S(1)}, u32[]{:S(2)}, u32[]{:S(2)}) collective-permute-start(f32[8,40,128]{2,1,0:T(8,128)S(1)} %all_to_all.10.r_ref), channel_id=1, source_target_pairs={{8,16},{16,8},{24,28},{28,24},{20,12},{12,20},{4,5},{5,4},{13,21},... | collective-permute-start | bytes 491528 | tf_op jit(solution)/shard_map/ppermute | solution.py:350
  26.0 0.0 collective-permute-done.2.rim_ref
  26.0 0.1 convert_element_type.11
  26.1 2.6 %blocks.1 = (bf16[8,128,448]{2,1,0:T(8,128)(2,1)S(1)}, bf16[8,128,448]{2,1,0:T(8,128)(2,1)S(1)}) custom-call(s32[8]{0:T(128)S(1)} %stack.48.where_ref, f32[64,64,448]{2,1,0:T(8,128)} %blocks_ref.7, f32[264,448]{1,0:T(8,128)S(1)} %collective-permute-done.2.rim_ref), custom_call_target="tpu_custom_call" | custom-call | bytes 6000000 | tf_op jit(solution)/shard_map/blocks/pallas_call | solution.py:427
  28.7 0.1 pad_add_fusion.near_ref
  28.8 1.8 %collective-permute-done.3 = f32[8,40,128]{2,1,0:T(8,128)S(1)} collective-permute-done((f32[8,40,128]{2,1,0:T(8,128)S(1)}, f32[8,40,128]{2,1,0:T(8,128)S(1)}, u32[]{:S(2)}, u32[]{:S(2)}) %collective-permute-start.3) | collective-permute-done | bytes 163872 | tf_op jit(solution)/shard_map/ppermute | solution.py:350
  30.5 0.0 collective-permute-done.4
  30.6 3.0 %sweeps.1 = f32[64,512]{1,0:T(8,128)S(1)} custom-call(s32[8]{0:T(128)S(1)} %stack.48.where_ref, s32[7,64]{1,0:T(8,128)S(1)} %bitcast.21, s32[7,8]{1,0:T(8,128)S(1)} %pad_add_fusion.near_ref, bf16[8,128,448]{2,1,0:T(8,128)(2,1)S(1)} %get-tuple-element.14.a_ref, bf16[8,128,448]{2,1,0:T(8,128)(2,1)S(1)} %get-tuple-element.15.an_ref, ...), custom_call_target="tpu_custom_call" | custom-call | bytes 9000000 | tf_op jit(solution)/shard_map/sweeps/pallas_call | solution.py:443
  33.6 12.6 %all_to_all.11 = f32[8,8,512]{2,1,0:T(8,128)S(1)} all-to-all(f32[8,8,512]{2,1,0:T(8,128)S(1)} %bitcast.16), channel_id=1, replica_groups={{0,8,16,24,28,20,12,4},{5,13,21,29,25,17,9,1},{2,10,18,26,30,22,14,6},{..., dimensions={0} | all-to-all | bytes 262144 | tf_op jit(solution)/shard_map/all_to_all | solution.py:340
  46.2 0.7 %add.26 = f32[8,4096]{1,0:T(8,128)} add(f32[8,4096]{1,0:T(8,128)S(1)} %copy-done.2, f32[8,4096]{1,0:T(8,128)S(1)} %bitcast.24) | non-fusion elementwise | flops 32768 | bytes 393216 | tf_op jit(solution)/shard_map/add | solution.py:456
  (18 shorter events, 0.1 us)
Async XLA Ops:
  0.0 6.9 %copy-start.6 = (s32[64,7]{0,1:T(8,128)S(1)}, s32[64,7]{0,1:T(8,128)}, u32[]{:S(2)}) copy-start(s32[64,7]{0,1:T(8,128)} %param.13) | copy-start | bytes 5380
  0.1 0.9 %copy-start.1 = (f32[8,4096]{1,0:T(8,128)S(1)}, f32[8,4096]{1,0:T(8,128)}, u32[]{:S(2)}) copy-start(f32[8,4096]{1,0:T(8,128)} %x_ref.5) | copy-start | bytes 393220
  1.0 5.9 %copy-start = (f32[64,64,448]{2,1,0:T(8,128)S(1)}, f32[64,64,448]{2,1,0:T(8,128)}, u32[]{:S(2)}) copy-start(f32[64,64,448]{2,1,0:T(8,128)} %blocks_ref.7) | copy-start | bytes 22020100
  1.0 8.7 %copy-start.3 = (f32[8,4096]{1,0:T(8,128)S(1)}, f32[8,4096]{1,0:T(8,128)}, u32[]{:S(2)}) copy-start(f32[8,4096]{1,0:T(8,128)} %f_ref.1) | copy-start | bytes 393220
  1.0 8.8 %copy-start.7 = (f32[4096]{0:T(1024)S(1)}, f32[4096]{0:T(1024)}, u32[]{:S(2)}) copy-start(f32[4096]{0:T(1024)} %param.9) | copy-start | bytes 49156
  1.0 8.8 %copy-start.8 = (f32[4096]{0:T(1024)S(1)}, f32[4096]{0:T(1024)}, u32[]{:S(2)}) copy-start(f32[4096]{0:T(1024)} %param.14) | copy-start | bytes 49156
  1.6 8.2 %collective-permute-start = (f32[8,256]{1,0:T(8,128)S(1)}, f32[8,256]{1,0:T(8,128)S(1)}, u32[]{:S(2)}, u32[]{:S(2)}) collective-permute-start(f32[8,256]{1,0:T(8,128)S(1)} %get-tuple-element.11), channel_id=1, source_target_pairs={{1,2},{2,1},{5,6},{6,5},{9,10},{10,9},{13,14},{14,13},{17,18},{18,... | collective-permute-start | bytes 24584 | tf_op jit(solution)/shard_map/ppermute | solution.py:380
  2.4 7.4 %collective-permute-start.1 = (f32[8,256]{1,0:T(8,128)S(1)}, f32[8,256]{1,0:T(8,128)S(1)}, u32[]{:S(2)}, u32[]{:S(2)}) collective-permute-start(f32[8,256]{1,0:T(8,128)S(1)} %get-tuple-element.12), channel_id=1, source_target_pairs={{0,1},{2,3},{1,0},{3,2},{4,5},{6,7},{5,4},{7,6},{8,9},{10,11},{9,8... | collective-permute-start | bytes 24584 | tf_op jit(solution)/shard_map/ppermute | solution.py:380
  9.8 20.8 %copy-start.4 = (bf16[2,128,256]{2,1,0:T(8,128)(2,1)S(1)}, bf16[2,128,256]{2,1,0:T(8,128)(2,1)}, u32[]{:S(2)}) copy-start(bf16[2,128,256]{2,1,0:T(8,128)(2,1)} %constant.59.clone.fwd_ref) | copy-start | bytes 393220
  9.8 20.8 %copy-start.5 = (bf16[2,64,256]{2,1,0:T(8,128)(2,1)S(1)}, bf16[2,64,256]{2,1,0:T(8,128)(2,1)}, u32[]{:S(2)}) copy-start(bf16[2,64,256]{2,1,0:T(8,128)(2,1)} %constant.60.clone.back_ref) | copy-start | bytes 196612
  9.8 20.7 %copy-start.9 = (f32[2,128]{1,0:T(2,128)S(1)}, f32[2,128]{1,0:T(2,128)}, u32[]{:S(2)}) copy-start(f32[2,128]{1,0:T(2,128)} %constant.61.clone.lam_ref) | copy-start | bytes 3076
  11.0 35.3 %copy-start.2 = (f32[8,4096]{1,0:T(8,128)S(1)}, f32[8,4096]{1,0:T(8,128)}, u32[]{:S(2)}) copy-start(f32[8,4096]{1,0:T(8,128)} %x_ref.5) | copy-start | bytes 393220
  11.0 15.0 %collective-permute-start.2 = (f32[264,448]{1,0:T(8,128)S(1)}, f32[264,448]{1,0:T(8,128)S(1)}, u32[]{:S(2)}, u32[]{:S(2)}) collective-permute-start(f32[264,448]{1,0:T(8,128)S(1)} %get-tuple-element.13), channel_id=1, source_target_pairs={{4,5},{5,4},{1,2},{2,1},{6,7},{7,6}} | collective-permute-start | bytes 1419272 | tf_op jit(solution)/shard_map/ppermute | solution.py:416
  25.2 5.3 %collective-permute-start.3 = (f32[8,40,128]{2,1,0:T(8,128)S(1)}, f32[8,40,128]{2,1,0:T(8,128)S(1)}, u32[]{:S(2)}, u32[]{:S(2)}) collective-permute-start(f32[8,40,128]{2,1,0:T(8,128)S(1)} %all_to_all.10.r_ref), channel_id=1, source_target_pairs={{0,8},{8,0},{16,24},{24,16},{28,20},{20,28},{12,4},{4,12},{5,13},{... | collective-permute-start | bytes 491528 | tf_op jit(solution)/shard_map/ppermute | solution.py:350
  25.3 5.2 %collective-permute-start.4 = (f32[8,40,128]{2,1,0:T(8,128)S(1)}, f32[8,40,128]{2,1,0:T(8,128)S(1)}, u32[]{:S(2)}, u32[]{:S(2)}) collective-permute-start(f32[8,40,128]{2,1,0:T(8,128)S(1)} %all_to_all.10.r_ref), channel_id=1, source_target_pairs={{8,16},{16,8},{24,28},{28,24},{20,12},{12,20},{4,5},{5,4},{13,21},... | collective-permute-start | bytes 491528 | tf_op jit(solution)/shard_map/ppermute | solution.py:350

commit v6 on v5

--- a/solution.py
+++ b/solution.py
@@ -274,9 +274,9 @@
         row = spot * chunk + b
         found = cols_ref[n, jnp.clip(row, 0, block_rows - 1)]
         if b < 0:
-            found = jnp.where(row < 0, near_ref[n, jnp.maximum(row + GHOST, 0)], found)
+            found = jnp.where(row < 0, near_ref[n, jnp.clip(row + GHOST, 0, GHOST - 1)], found)
         if b >= chunk:
-            found = jnp.where(row >= block_rows, near_ref[n, GHOST + jnp.maximum(row - block_rows, 0)], found)
+            found = jnp.where(row >= block_rows, near_ref[n, GHOST + jnp.clip(row - block_rows, 0, GHOST - 1)], found)
         return jnp.clip(found - base, -2 * GHOST, chunk + 2 * GHOST - 1)
 
     store_split(v0_ref, 0, divide(s_ref[...], 0))

time: 47.2 us -> 47.2 us (level)
  no operation moved by 1% of the time
where the time goes in v6:
time: 47.2 us; the launch traced here: 46.9 us
  blocking collectives  26 us (55%)
  Pallas kernels  10.1 us (21%)
  starting transfers between devices  6.9 us (15%)
  waiting for transfers between devices  1.8 us (4%)
  local copies, waits for them, and re-layouts  1.11 us (2%)
  other arithmetic  0.77 us (2%)
    all_to_all x2, blocking collectives, deal(): lax.all_to_all(value, AXES, 0, 0, axis_index_groups=groups, tiled=True)  26 us
    ppermute x2, starting transfers between devices, local(): lax.ppermute(given[first], 'space', pairs + [(j, i) for i, j in pairs])  5.29 us
    pallas_call x1, Pallas kernels, local(): pl.pallas_call(functools.partial(sweeps_kernel, dims, lasts), in_specs=sm...  3.04 us
    pallas_call x1, Pallas kernels, local(): pl.pallas_call(inner_kernel, in_specs=smem(2) + vmem(2), out_specs=vmem(1...  2.85 us
    pallas_call x1, Pallas kernels, local(): pl.pallas_call(blocks_kernel, in_specs=smem(1) + [pl.BlockSpec(memory_spa...  2.56 us
    ppermute x2, waiting for transfers between devices, neighbours(): lax.ppermute(value, AXES, ring_pairs(first))[None]  1.78 us
    pallas_call x1, Pallas kernels, local(): pl.pallas_call(outer_kernel, in_specs=smem(2) + vmem(8), out_specs=vmem(2...  1.16 us
    unnamed x20, local copies, waits for them, and re-layouts  0.95 us
  transfers between devices with their start and end apart: 5, of which 1 were waited for; matrix products, arithmetic and copies ran while one was open for 0% of the time, Pallas kernels for 12%

profile of v6, /device:TPU:0, one launch (start us, length us, event | category | flops | bytes accessed | tf_op | source)
XLA Modules:
  0.0 46.9 jit_solution(9233437803395837331)
XLA Ops:
  0.0 0.1 stack.48.where_ref
  0.1 0.9 %copy-done.1 = f32[8,4096]{1,0:T(8,128)S(1)} copy-done((f32[8,4096]{1,0:T(8,128)S(1)}, f32[8,4096]{1,0:T(8,128)}, u32[]{:S(2)}) %copy-start.1) | copy-done | bytes 131096
  1.0 0.5 %sides.1 = (f32[8,256]{1,0:T(8,128)S(1)}, f32[8,256]{1,0:T(8,128)S(1)}) custom-call(s32[8]{0:T(128)S(1)} %stack.48.where_ref, f32[8,4096]{1,0:T(8,128)S(1)} %copy-done.1, f32[64,64,448]{2,1,0:T(8,128)} %blocks_ref.7), custom_call_target="tpu_custom_call" | custom-call | tf_op jit(solution)/shard_map/sides/pallas_call | solution.py:369
  1.6 0.8 %collective-permute-start = (f32[8,256]{1,0:T(8,128)S(1)}, f32[8,256]{1,0:T(8,128)S(1)}, u32[]{:S(2)}, u32[]{:S(2)}) collective-permute-start(f32[8,256]{1,0:T(8,128)S(1)} %get-tuple-element.11), channel_id=1, source_target_pairs={{1,2},{2,1},{5,6},{6,5},{9,10},{10,9},{13,14},{14,13},{17,18},{18,... | collective-permute-start | bytes 24584 | tf_op jit(solution)/shard_map/ppermute | solution.py:380
  2.4 4.5 %collective-permute-start.1 = (f32[8,256]{1,0:T(8,128)S(1)}, f32[8,256]{1,0:T(8,128)S(1)}, u32[]{:S(2)}, u32[]{:S(2)}) collective-permute-start(f32[8,256]{1,0:T(8,128)S(1)} %get-tuple-element.12), channel_id=1, source_target_pairs={{0,1},{2,3},{1,0},{3,2},{4,5},{6,7},{5,4},{7,6},{8,9},{10,11},{9,8... | collective-permute-start | bytes 24584 | tf_op jit(solution)/shard_map/ppermute | solution.py:380
  6.9 2.8 %inner.1.inner_ref = f32[8,4096]{1,0:T(8,128)S(1)} custom-call(s32[8]{0:T(128)S(1)} %stack.48.where_ref, s32[7,64]{1,0:T(8,128)S(1)} %bitcast.19, f32[8,4096]{1,0:T(8,128)S(1)} %copy-done.1, f32[64,64,448]{2,1,0:T(8,128)S(1)} %copy-done), custom_call_target="tpu_custom_call" | custom-call | tf_op jit(solution)/shard_map/inner/pallas_call | solution.py:381
  9.7 0.0 collective-permute-done.two_ref
  9.7 0.0 collective-permute-done.1.one_ref
  9.8 0.0 copy-start.4
  9.8 0.0 copy-start.5
  9.8 0.0 copy-start.9
  9.8 1.2 %outer.1 = (f32[8,40,128]{2,1,0:T(8,128)S(1)}, f32[264,448]{1,0:T(8,128)S(1)}) custom-call(s32[8]{0:T(128)S(1)} %stack.48.where_ref, s32[7,64]{1,0:T(8,128)S(1)} %bitcast.20, f32[8,4096]{1,0:T(8,128)S(1)} %copy-done.1, f32[8,4096]{1,0:T(8,128)S(1)} %copy-done.3, f32[64,64,448]{2,1,0:T(8,128)S(1)} %copy-done, f32[8,4096]{1,0:T(8,128)S(1)} %inner.1.inner_ref, ...), custom_call_target="tpu_custom_call" | custom-call | bytes 3000000 | tf_op jit(solution)/shard_map/outer/pallas_call | solution.py:392
  11.0 0.8 %collective-permute-start.2 = (f32[264,448]{1,0:T(8,128)S(1)}, f32[264,448]{1,0:T(8,128)S(1)}, u32[]{:S(2)}, u32[]{:S(2)}) collective-permute-start(f32[264,448]{1,0:T(8,128)S(1)} %get-tuple-element.13), channel_id=1, source_target_pairs={{4,5},{5,4},{1,2},{2,1},{6,7},{7,6}} | collective-permute-start | bytes 1419272 | tf_op jit(solution)/shard_map/ppermute | solution.py:416
  11.8 13.4 %all_to_all.10.r_ref = f32[8,40,128]{2,1,0:T(8,128)S(1)} all-to-all(f32[8,40,128]{2,1,0:T(8,128)S(1)} %get-tuple-element.16), channel_id=1, replica_groups={{0,8,16,24,28,20,12,4},{5,13,21,29,25,17,9,1},{2,10,18,26,30,22,14,6},{..., dimensions={0} | all-to-all | bytes 327680 | tf_op jit(solution)/shard_map/all_to_all | solution.py:340
  25.2 0.1 collective-permute-start.3
  25.3 0.7 %collective-permute-start.4 = (f32[8,40,128]{2,1,0:T(8,128)S(1)}, f32[8,40,128]{2,1,0:T(8,128)S(1)}, u32[]{:S(2)}, u32[]{:S(2)}) collective-permute-start(f32[8,40,128]{2,1,0:T(8,128)S(1)} %all_to_all.10.r_ref), channel_id=1, source_target_pairs={{8,16},{16,8},{24,28},{28,24},{20,12},{12,20},{4,5},{5,4},{13,21},... | collective-permute-start | bytes 491528 | tf_op jit(solution)/shard_map/ppermute | solution.py:350
  26.0 0.1 convert_element_type.11
  26.1 2.6 %blocks.1 = (bf16[8,128,448]{2,1,0:T(8,128)(2,1)S(1)}, bf16[8,128,448]{2,1,0:T(8,128)(2,1)S(1)}) custom-call(s32[8]{0:T(128)S(1)} %stack.48.where_ref, f32[64,64,448]{2,1,0:T(8,128)} %blocks_ref.7, f32[264,448]{1,0:T(8,128)S(1)} %collective-permute-done.2.rim_ref), custom_call_target="tpu_custom_call" | custom-call | bytes 6000000 | tf_op jit(solution)/shard_map/blocks/pallas_call | solution.py:427
  28.7 0.1 pad_add_fusion.near_ref
  28.8 1.8 %collective-permute-done.3 = f32[8,40,128]{2,1,0:T(8,128)S(1)} collective-permute-done((f32[8,40,128]{2,1,0:T(8,128)S(1)}, f32[8,40,128]{2,1,0:T(8,128)S(1)}, u32[]{:S(2)}, u32[]{:S(2)}) %collective-permute-start.3) | collective-permute-done | bytes 163872 | tf_op jit(solution)/shard_map/ppermute | solution.py:350
  30.5 0.0 collective-permute-done.4
  30.6 3.0 %sweeps.1 = f32[64,512]{1,0:T(8,128)S(1)} custom-call(s32[8]{0:T(128)S(1)} %stack.48.where_ref, s32[7,64]{1,0:T(8,128)S(1)} %bitcast.21, s32[7,8]{1,0:T(8,128)S(1)} %pad_add_fusion.near_ref, bf16[8,128,448]{2,1,0:T(8,128)(2,1)S(1)} %get-tuple-element.14.a_ref, bf16[8,128,448]{2,1,0:T(8,128)(2,1)S(1)} %get-tuple-element.15.an_ref, ...), custom_call_target="tpu_custom_call" | custom-call | bytes 9000000 | tf_op jit(solution)/shard_map/sweeps/pallas_call | solution.py:443
  33.6 12.6 %all_to_all.11 = f32[8,8,512]{2,1,0:T(8,128)S(1)} all-to-all(f32[8,8,512]{2,1,0:T(8,128)S(1)} %bitcast.16), channel_id=1, replica_groups={{0,8,16,24,28,20,12,4},{5,13,21,29,25,17,9,1},{2,10,18,26,30,22,14,6},{..., dimensions={0} | all-to-all | bytes 262144 | tf_op jit(solution)/shard_map/all_to_all | solution.py:340
  46.2 0.7 %add.26 = f32[8,4096]{1,0:T(8,128)} add(f32[8,4096]{1,0:T(8,128)S(1)} %copy-done.2, f32[8,4096]{1,0:T(8,128)S(1)} %bitcast.24) | non-fusion elementwise | flops 32768 | bytes 393216 | tf_op jit(solution)/shard_map/add | solution.py:456
  (18 shorter events, 0.1 us)
Async XLA Ops:
  0.0 6.9 %copy-start.6 = (s32[64,7]{0,1:T(8,128)S(1)}, s32[64,7]{0,1:T(8,128)}, u32[]{:S(2)}) copy-start(s32[64,7]{0,1:T(8,128)} %param.13) | copy-start | bytes 5380
  0.1 0.9 %copy-start.1 = (f32[8,4096]{1,0:T(8,128)S(1)}, f32[8,4096]{1,0:T(8,128)}, u32[]{:S(2)}) copy-start(f32[8,4096]{1,0:T(8,128)} %x_ref.5) | copy-start | bytes 393220
  1.0 5.9 %copy-start = (f32[64,64,448]{2,1,0:T(8,128)S(1)}, f32[64,64,448]{2,1,0:T(8,128)}, u32[]{:S(2)}) copy-start(f32[64,64,448]{2,1,0:T(8,128)} %blocks_ref.7) | copy-start | bytes 22020100
  1.0 8.7 %copy-start.3 = (f32[8,4096]{1,0:T(8,128)S(1)}, f32[8,4096]{1,0:T(8,128)}, u32[]{:S(2)}) copy-start(f32[8,4096]{1,0:T(8,128)} %f_ref.1) | copy-start | bytes 393220
  1.0 8.8 %copy-start.7 = (f32[4096]{0:T(1024)S(1)}, f32[4096]{0:T(1024)}, u32[]{:S(2)}) copy-start(f32[4096]{0:T(1024)} %param.9) | copy-start | bytes 49156
  1.0 8.8 %copy-start.8 = (f32[4096]{0:T(1024)S(1)}, f32[4096]{0:T(1024)}, u32[]{:S(2)}) copy-start(f32[4096]{0:T(1024)} %param.14) | copy-start | bytes 49156
  1.6 8.2 %collective-permute-start = (f32[8,256]{1,0:T(8,128)S(1)}, f32[8,256]{1,0:T(8,128)S(1)}, u32[]{:S(2)}, u32[]{:S(2)}) collective-permute-start(f32[8,256]{1,0:T(8,128)S(1)} %get-tuple-element.11), channel_id=1, source_target_pairs={{1,2},{2,1},{5,6},{6,5},{9,10},{10,9},{13,14},{14,13},{17,18},{18,... | collective-permute-start | bytes 24584 | tf_op jit(solution)/shard_map/ppermute | solution.py:380
  2.4 7.4 %collective-permute-start.1 = (f32[8,256]{1,0:T(8,128)S(1)}, f32[8,256]{1,0:T(8,128)S(1)}, u32[]{:S(2)}, u32[]{:S(2)}) collective-permute-start(f32[8,256]{1,0:T(8,128)S(1)} %get-tuple-element.12), channel_id=1, source_target_pairs={{0,1},{2,3},{1,0},{3,2},{4,5},{6,7},{5,4},{7,6},{8,9},{10,11},{9,8... | collective-permute-start | bytes 24584 | tf_op jit(solution)/shard_map/ppermute | solution.py:380
  9.8 20.8 %copy-start.4 = (bf16[2,128,256]{2,1,0:T(8,128)(2,1)S(1)}, bf16[2,128,256]{2,1,0:T(8,128)(2,1)}, u32[]{:S(2)}) copy-start(bf16[2,128,256]{2,1,0:T(8,128)(2,1)} %constant.59.clone.fwd_ref) | copy-start | bytes 393220
  9.8 20.8 %copy-start.5 = (bf16[2,64,256]{2,1,0:T(8,128)(2,1)S(1)}, bf16[2,64,256]{2,1,0:T(8,128)(2,1)}, u32[]{:S(2)}) copy-start(bf16[2,64,256]{2,1,0:T(8,128)(2,1)} %constant.60.clone.back_ref) | copy-start | bytes 196612
  9.8 20.7 %copy-start.9 = (f32[2,128]{1,0:T(2,128)S(1)}, f32[2,128]{1,0:T(2,128)}, u32[]{:S(2)}) copy-start(f32[2,128]{1,0:T(2,128)} %constant.61.clone.lam_ref) | copy-start | bytes 3076
  11.0 35.3 %copy-start.2 = (f32[8,4096]{1,0:T(8,128)S(1)}, f32[8,4096]{1,0:T(8,128)}, u32[]{:S(2)}) copy-start(f32[8,4096]{1,0:T(8,128)} %x_ref.5) | copy-start | bytes 393220
  11.0 15.0 %collective-permute-start.2 = (f32[264,448]{1,0:T(8,128)S(1)}, f32[264,448]{1,0:T(8,128)S(1)}, u32[]{:S(2)}, u32[]{:S(2)}) collective-permute-start(f32[264,448]{1,0:T(8,128)S(1)} %get-tuple-element.13), channel_id=1, source_target_pairs={{4,5},{5,4},{1,2},{2,1},{6,7},{7,6}} | collective-permute-start | bytes 1419272 | tf_op jit(solution)/shard_map/ppermute | solution.py:416
  25.2 5.3 %collective-permute-start.3 = (f32[8,40,128]{2,1,0:T(8,128)S(1)}, f32[8,40,128]{2,1,0:T(8,128)S(1)}, u32[]{:S(2)}, u32[]{:S(2)}) collective-permute-start(f32[8,40,128]{2,1,0:T(8,128)S(1)} %all_to_all.10.r_ref), channel_id=1, source_target_pairs={{0,8},{8,0},{16,24},{24,16},{28,20},{20,28},{12,4},{4,12},{5,13},{... | collective-permute-start | bytes 491528 | tf_op jit(solution)/shard_map/ppermute | solution.py:350
  25.3 5.2 %collective-permute-start.4 = (f32[8,40,128]{2,1,0:T(8,128)S(1)}, f32[8,40,128]{2,1,0:T(8,128)S(1)}, u32[]{:S(2)}, u32[]{:S(2)}) collective-permute-start(f32[8,40,128]{2,1,0:T(8,128)S(1)} %all_to_all.10.r_ref), channel_id=1, source_target_pairs={{8,16},{16,8},{24,28},{28,24},{20,12},{12,20},{4,5},{5,4},{13,21},... | collective-permute-start | bytes 491528 | tf_op jit(solution)/shard_map/ppermute | solution.py:350

commit v7 on v6

--- a/solution.py
+++ b/solution.py
@@ -167,14 +167,18 @@
     chunk = count - 2 * GHOST
     block_rows = blocks_ref.shape[0]
     spot = where_ref[0]
-    rows = list(range(GHOST, GHOST + chunk)) + list(range(GHOST)) + list(range(GHOST + chunk, count))
-    copies = {}
-    for b in rows:
+    own = list(range(GHOST, GHOST + chunk))
+    others = list(range(GHOST)) + list(range(GHOST + chunk, count))
+    mine = blocks_ref.at[pl.ds(spot * chunk, chunk)]
+    copies = {GHOST: pltpu.make_async_copy(mine, buffer.at[pl.ds(GHOST, chunk)], sems.at[GHOST])}
+    for b in others:
         row = jnp.clip(spot * chunk + b - GHOST, 0, block_rows - 1)
         copies[b] = pltpu.make_async_copy(blocks_ref.at[row], buffer.at[b], sems.at[b])
-        copies[b].start()
-    for b in rows:
-        copies[b].wait()
+    for copy in copies.values():
+        copy.start()
+    for b in own + others:
+        if b in copies:
+            copies[b].wait()
         value = buffer[b]
         if GHOST <= b < GHOST + chunk:
             ref, at = own_ref, b - GHOST
@@ -272,6 +276,8 @@
 
     def column(n, b):
         row = spot * chunk + b
+        if 0 <= b < chunk:
+            return cols_ref[n, row] - base
         found = cols_ref[n, jnp.clip(row, 0, block_rows - 1)]
         if b < 0:
             found = jnp.where(row < 0, near_ref[n, jnp.clip(row + GHOST, 0, GHOST - 1)], found)

time: 47.2 us -> 47.2 us (level)
  no operation moved by 1% of the time
where the time goes in v7:
time: 47.2 us; the launch traced here: 46.9 us
  blocking collectives  26 us (55%)
  Pallas kernels  10.1 us (21%)
  starting transfers between devices  6.9 us (15%)
  waiting for transfers between devices  1.8 us (4%)
  local copies, waits for them, and re-layouts  1.11 us (2%)
  other arithmetic  0.77 us (2%)
    all_to_all x2, blocking collectives, deal(): lax.all_to_all(value, AXES, 0, 0, axis_index_groups=groups, tiled=True)  26 us
    ppermute x2, starting transfers between devices, local(): lax.ppermute(given[first], 'space', pairs + [(j, i) for i, j in pairs])  5.29 us
    pallas_call x1, Pallas kernels, local(): pl.pallas_call(functools.partial(sweeps_kernel, dims, lasts), in_specs=sm...  3.04 us
    pallas_call x1, Pallas kernels, local(): pl.pallas_call(inner_kernel, in_specs=smem(2) + vmem(2), out_specs=vmem(1...  2.85 us
    pallas_call x1, Pallas kernels, local(): pl.pallas_call(blocks_kernel, in_specs=smem(1) + [pl.BlockSpec(memory_spa...  2.55 us
    ppermute x2, waiting for transfers between devices, neighbours(): lax.ppermute(value, AXES, ring_pairs(first))[None]  1.78 us
    pallas_call x1, Pallas kernels, local(): pl.pallas_call(outer_kernel, in_specs=smem(2) + vmem(8), out_specs=vmem(2...  1.16 us
    unnamed x20, local copies, waits for them, and re-layouts  0.95 us
  transfers between devices with their start and end apart: 5, of which 1 were waited for; matrix products, arithmetic and copies ran while one was open for 0% of the time, Pallas kernels for 12%

profile of v7, /device:TPU:0, one launch (start us, length us, event | category | flops | bytes accessed | tf_op | source)
XLA Modules:
  0.0 46.9 jit_solution(4594682932045302304)
XLA Ops:
  0.0 0.1 stack.48.where_ref
  0.1 0.9 %copy-done.1 = f32[8,4096]{1,0:T(8,128)S(1)} copy-done((f32[8,4096]{1,0:T(8,128)S(1)}, f32[8,4096]{1,0:T(8,128)}, u32[]{:S(2)}) %copy-start.1) | copy-done | bytes 131096
  1.0 0.5 %sides.1 = (f32[8,256]{1,0:T(8,128)S(1)}, f32[8,256]{1,0:T(8,128)S(1)}) custom-call(s32[8]{0:T(128)S(1)} %stack.48.where_ref, f32[8,4096]{1,0:T(8,128)S(1)} %copy-done.1, f32[64,64,448]{2,1,0:T(8,128)} %blocks_ref.7), custom_call_target="tpu_custom_call" | custom-call | tf_op jit(solution)/shard_map/sides/pallas_call | solution.py:375
  1.6 0.8 %collective-permute-start = (f32[8,256]{1,0:T(8,128)S(1)}, f32[8,256]{1,0:T(8,128)S(1)}, u32[]{:S(2)}, u32[]{:S(2)}) collective-permute-start(f32[8,256]{1,0:T(8,128)S(1)} %get-tuple-element.11), channel_id=1, source_target_pairs={{1,2},{2,1},{5,6},{6,5},{9,10},{10,9},{13,14},{14,13},{17,18},{18,... | collective-permute-start | bytes 24584 | tf_op jit(solution)/shard_map/ppermute | solution.py:386
  2.4 4.5 %collective-permute-start.1 = (f32[8,256]{1,0:T(8,128)S(1)}, f32[8,256]{1,0:T(8,128)S(1)}, u32[]{:S(2)}, u32[]{:S(2)}) collective-permute-start(f32[8,256]{1,0:T(8,128)S(1)} %get-tuple-element.12), channel_id=1, source_target_pairs={{0,1},{2,3},{1,0},{3,2},{4,5},{6,7},{5,4},{7,6},{8,9},{10,11},{9,8... | collective-permute-start | bytes 24584 | tf_op jit(solution)/shard_map/ppermute | solution.py:386
  6.9 2.8 %inner.1.inner_ref = f32[8,4096]{1,0:T(8,128)S(1)} custom-call(s32[8]{0:T(128)S(1)} %stack.48.where_ref, s32[7,64]{1,0:T(8,128)S(1)} %bitcast.19, f32[8,4096]{1,0:T(8,128)S(1)} %copy-done.1, f32[64,64,448]{2,1,0:T(8,128)S(1)} %copy-done), custom_call_target="tpu_custom_call" | custom-call | tf_op jit(solution)/shard_map/inner/pallas_call | solution.py:387
  9.7 0.0 collective-permute-done.two_ref
  9.7 0.0 collective-permute-done.1.one_ref
  9.8 0.0 copy-start.4
  9.8 0.0 copy-start.5
  9.8 0.0 copy-start.9
  9.8 1.2 %outer.1 = (f32[8,40,128]{2,1,0:T(8,128)S(1)}, f32[264,448]{1,0:T(8,128)S(1)}) custom-call(s32[8]{0:T(128)S(1)} %stack.48.where_ref, s32[7,64]{1,0:T(8,128)S(1)} %bitcast.20, f32[8,4096]{1,0:T(8,128)S(1)} %copy-done.1, f32[8,4096]{1,0:T(8,128)S(1)} %copy-done.3, f32[64,64,448]{2,1,0:T(8,128)S(1)} %copy-done, f32[8,4096]{1,0:T(8,128)S(1)} %inner.1.inner_ref, ...), custom_call_target="tpu_custom_call" | custom-call | bytes 3000000 | tf_op jit(solution)/shard_map/outer/pallas_call | solution.py:398
  11.0 0.8 %collective-permute-start.2 = (f32[264,448]{1,0:T(8,128)S(1)}, f32[264,448]{1,0:T(8,128)S(1)}, u32[]{:S(2)}, u32[]{:S(2)}) collective-permute-start(f32[264,448]{1,0:T(8,128)S(1)} %get-tuple-element.13), channel_id=1, source_target_pairs={{4,5},{5,4},{1,2},{2,1},{6,7},{7,6}} | collective-permute-start | bytes 1419272 | tf_op jit(solution)/shard_map/ppermute | solution.py:422
  11.8 13.4 %all_to_all.10.r_ref = f32[8,40,128]{2,1,0:T(8,128)S(1)} all-to-all(f32[8,40,128]{2,1,0:T(8,128)S(1)} %get-tuple-element.16), channel_id=1, replica_groups={{0,8,16,24,28,20,12,4},{5,13,21,29,25,17,9,1},{2,10,18,26,30,22,14,6},{..., dimensions={0} | all-to-all | bytes 327680 | tf_op jit(solution)/shard_map/all_to_all | solution.py:346
  25.2 0.1 collective-permute-start.3
  25.3 0.7 %collective-permute-start.4 = (f32[8,40,128]{2,1,0:T(8,128)S(1)}, f32[8,40,128]{2,1,0:T(8,128)S(1)}, u32[]{:S(2)}, u32[]{:S(2)}) collective-permute-start(f32[8,40,128]{2,1,0:T(8,128)S(1)} %all_to_all.10.r_ref), channel_id=1, source_target_pairs={{8,16},{16,8},{24,28},{28,24},{20,12},{12,20},{4,5},{5,4},{13,21},... | collective-permute-start | bytes 491528 | tf_op jit(solution)/shard_map/ppermute | solution.py:356
  26.0 0.0 collective-permute-done.2.rim_ref
  26.0 0.1 convert_element_type.11
  26.1 2.6 %blocks.1 = (bf16[8,128,448]{2,1,0:T(8,128)(2,1)S(1)}, bf16[8,128,448]{2,1,0:T(8,128)(2,1)S(1)}) custom-call(s32[8]{0:T(128)S(1)} %stack.48.where_ref, f32[64,64,448]{2,1,0:T(8,128)} %blocks_ref.7, f32[264,448]{1,0:T(8,128)S(1)} %collective-permute-done.2.rim_ref), custom_call_target="tpu_custom_call" | custom-call | bytes 6000000 | tf_op jit(solution)/shard_map/blocks/pallas_call | solution.py:433
  28.7 0.1 pad_add_fusion.near_ref
  28.8 1.8 %collective-permute-done.3 = f32[8,40,128]{2,1,0:T(8,128)S(1)} collective-permute-done((f32[8,40,128]{2,1,0:T(8,128)S(1)}, f32[8,40,128]{2,1,0:T(8,128)S(1)}, u32[]{:S(2)}, u32[]{:S(2)}) %collective-permute-start.3) | collective-permute-done | bytes 163872 | tf_op jit(solution)/shard_map/ppermute | solution.py:356
  30.6 3.0 %sweeps.1 = f32[64,512]{1,0:T(8,128)S(1)} custom-call(s32[8]{0:T(128)S(1)} %stack.48.where_ref, s32[7,64]{1,0:T(8,128)S(1)} %bitcast.21, s32[7,8]{1,0:T(8,128)S(1)} %pad_add_fusion.near_ref, bf16[8,128,448]{2,1,0:T(8,128)(2,1)S(1)} %get-tuple-element.14.a_ref, bf16[8,128,448]{2,1,0:T(8,128)(2,1)S(1)} %get-tuple-element.15.an_ref, ...), custom_call_target="tpu_custom_call" | custom-call | bytes 9000000 | tf_op jit(solution)/shard_map/sweeps/pallas_call | solution.py:449
  33.6 12.6 %all_to_all.11 = f32[8,8,512]{2,1,0:T(8,128)S(1)} all-to-all(f32[8,8,512]{2,1,0:T(8,128)S(1)} %bitcast.16), channel_id=1, replica_groups={{0,8,16,24,28,20,12,4},{5,13,21,29,25,17,9,1},{2,10,18,26,30,22,14,6},{..., dimensions={0} | all-to-all | bytes 262144 | tf_op jit(solution)/shard_map/all_to_all | solution.py:346
  46.2 0.7 %add.26 = f32[8,4096]{1,0:T(8,128)} add(f32[8,4096]{1,0:T(8,128)S(1)} %copy-done.2, f32[8,4096]{1,0:T(8,128)S(1)} %bitcast.24) | non-fusion elementwise | flops 32768 | bytes 393216 | tf_op jit(solution)/shard_map/add | solution.py:462
  (18 shorter events, 0.1 us)
Async XLA Ops:
  0.0 6.9 %copy-start.6 = (s32[64,7]{0,1:T(8,128)S(1)}, s32[64,7]{0,1:T(8,128)}, u32[]{:S(2)}) copy-start(s32[64,7]{0,1:T(8,128)} %param.13) | copy-start | bytes 5380
  0.1 0.9 %copy-start.1 = (f32[8,4096]{1,0:T(8,128)S(1)}, f32[8,4096]{1,0:T(8,128)}, u32[]{:S(2)}) copy-start(f32[8,4096]{1,0:T(8,128)} %x_ref.5) | copy-start | bytes 393220
  1.0 5.9 %copy-start = (f32[64,64,448]{2,1,0:T(8,128)S(1)}, f32[64,64,448]{2,1,0:T(8,128)}, u32[]{:S(2)}) copy-start(f32[64,64,448]{2,1,0:T(8,128)} %blocks_ref.7) | copy-start | bytes 22020100
  1.0 8.7 %copy-start.3 = (f32[8,4096]{1,0:T(8,128)S(1)}, f32[8,4096]{1,0:T(8,128)}, u32[]{:S(2)}) copy-start(f32[8,4096]{1,0:T(8,128)} %f_ref.1) | copy-start | bytes 393220
  1.0 8.8 %copy-start.7 = (f32[4096]{0:T(1024)S(1)}, f32[4096]{0:T(1024)}, u32[]{:S(2)}) copy-start(f32[4096]{0:T(1024)} %param.9) | copy-start | bytes 49156
  1.0 8.8 %copy-start.8 = (f32[4096]{0:T(1024)S(1)}, f32[4096]{0:T(1024)}, u32[]{:S(2)}) copy-start(f32[4096]{0:T(1024)} %param.14) | copy-start | bytes 49156
  1.6 8.2 %collective-permute-start = (f32[8,256]{1,0:T(8,128)S(1)}, f32[8,256]{1,0:T(8,128)S(1)}, u32[]{:S(2)}, u32[]{:S(2)}) collective-permute-start(f32[8,256]{1,0:T(8,128)S(1)} %get-tuple-element.11), channel_id=1, source_target_pairs={{1,2},{2,1},{5,6},{6,5},{9,10},{10,9},{13,14},{14,13},{17,18},{18,... | collective-permute-start | bytes 24584 | tf_op jit(solution)/shard_map/ppermute | solution.py:386
  2.4 7.4 %collective-permute-start.1 = (f32[8,256]{1,0:T(8,128)S(1)}, f32[8,256]{1,0:T(8,128)S(1)}, u32[]{:S(2)}, u32[]{:S(2)}) collective-permute-start(f32[8,256]{1,0:T(8,128)S(1)} %get-tuple-element.12), channel_id=1, source_target_pairs={{0,1},{2,3},{1,0},{3,2},{4,5},{6,7},{5,4},{7,6},{8,9},{10,11},{9,8... | collective-permute-start | bytes 24584 | tf_op jit(solution)/shard_map/ppermute | solution.py:386
  9.8 20.8 %copy-start.4 = (bf16[2,128,256]{2,1,0:T(8,128)(2,1)S(1)}, bf16[2,128,256]{2,1,0:T(8,128)(2,1)}, u32[]{:S(2)}) copy-start(bf16[2,128,256]{2,1,0:T(8,128)(2,1)} %constant.59.clone.fwd_ref) | copy-start | bytes 393220
  9.8 20.8 %copy-start.5 = (bf16[2,64,256]{2,1,0:T(8,128)(2,1)S(1)}, bf16[2,64,256]{2,1,0:T(8,128)(2,1)}, u32[]{:S(2)}) copy-start(bf16[2,64,256]{2,1,0:T(8,128)(2,1)} %constant.60.clone.back_ref) | copy-start | bytes 196612
  9.8 20.7 %copy-start.9 = (f32[2,128]{1,0:T(2,128)S(1)}, f32[2,128]{1,0:T(2,128)}, u32[]{:S(2)}) copy-start(f32[2,128]{1,0:T(2,128)} %constant.61.clone.lam_ref) | copy-start | bytes 3076
  11.0 35.3 %copy-start.2 = (f32[8,4096]{1,0:T(8,128)S(1)}, f32[8,4096]{1,0:T(8,128)}, u32[]{:S(2)}) copy-start(f32[8,4096]{1,0:T(8,128)} %x_ref.5) | copy-start | bytes 393220
  11.0 15.0 %collective-permute-start.2 = (f32[264,448]{1,0:T(8,128)S(1)}, f32[264,448]{1,0:T(8,128)S(1)}, u32[]{:S(2)}, u32[]{:S(2)}) collective-permute-start(f32[264,448]{1,0:T(8,128)S(1)} %get-tuple-element.13), channel_id=1, source_target_pairs={{4,5},{5,4},{1,2},{2,1},{6,7},{7,6}} | collective-permute-start | bytes 1419272 | tf_op jit(solution)/shard_map/ppermute | solution.py:422
  25.2 5.3 %collective-permute-start.3 = (f32[8,40,128]{2,1,0:T(8,128)S(1)}, f32[8,40,128]{2,1,0:T(8,128)S(1)}, u32[]{:S(2)}, u32[]{:S(2)}) collective-permute-start(f32[8,40,128]{2,1,0:T(8,128)S(1)} %all_to_all.10.r_ref), channel_id=1, source_target_pairs={{0,8},{8,0},{16,24},{24,16},{28,20},{20,28},{12,4},{4,12},{5,13},{... | collective-permute-start | bytes 491528 | tf_op jit(solution)/shard_map/ppermute | solution.py:356
  25.3 5.2 %collective-permute-start.4 = (f32[8,40,128]{2,1,0:T(8,128)S(1)}, f32[8,40,128]{2,1,0:T(8,128)S(1)}, u32[]{:S(2)}, u32[]{:S(2)}) collective-permute-start(f32[8,40,128]{2,1,0:T(8,128)S(1)} %all_to_all.10.r_ref), channel_id=1, source_target_pairs={{8,16},{16,8},{24,28},{28,24},{20,12},{12,20},{4,5},{5,4},{13,21},... | collective-permute-start | bytes 491528 | tf_op jit(solution)/shard_map/ppermute | solution.py:356
